TPU v7x, 32 devices: a whole 2x2x4 slice. The times are simulated.
32 devices in a mesh: wide: 16 (over z, y, core), narrow: 2 (over x).
Axes of the slice: x: 2, y: 2, z: 4, core: 2. Of those that a mesh axis runs over, the one named last changes fastest.
Arguments:
- features: bfloat16 [16, 384, 1024], P('wide', 'narrow'), may hold values from -6 to 6
- embedding: bfloat16 [16, 768], P('wide'), may hold values from -6 to 6
- valid_mask: int32 [16, 1024], P('wide'), may hold values from 0 to 1, as said below
- cotangent: bfloat16 [16, 384, 1024], P('wide', 'narrow'), may hold values from -6 to 6
- conv_first: float32 [3456, 384], P('wide', 'narrow'), may hold values from -0.109375 to 0.109375
- conv_first_moment: float32 [3456, 384], P('wide', 'narrow'), may hold values from -48 to 48
- conv_first_square: float32 [3456, 384], P('wide', 'narrow'), may hold values from 5.0176 to 20.0704
- conv_second: float32 [3456, 384], P('wide', 'narrow'), may hold values from -0.109375 to 0.109375
- conv_second_moment: float32 [3456, 384], P('wide', 'narrow'), may hold values from -48 to 48
- conv_second_square: float32 [3456, 384], P('wide', 'narrow'), may hold values from 5.0176 to 20.0704
- film_weight: float32 [768, 2, 384], P('wide', None, 'narrow'), may hold values from -0.21875 to 0.21875
- film_weight_moment: float32 [768, 2, 384], P('wide', None, 'narrow'), may hold values from -20 to 20
- film_weight_square: float32 [768, 2, 384], P('wide', None, 'narrow'), may hold values from 0.9216 to 3.6864
- attend_in: float32 [384, 3, 384], P('wide', None, 'narrow'), may hold values from -0.3125 to 0.3125
- attend_in_moment: float32 [384, 3, 384], P('wide', None, 'narrow'), may hold values from -64 to 64
- attend_in_square: float32 [384, 3, 384], P('wide', None, 'narrow'), may hold values from 10.24 to 40.96
- attend_out: float32 [384, 384], P('wide', 'narrow'), may hold values from -2.5 to 2.5
- attend_out_moment: float32 [384, 384], P('wide', 'narrow'), may hold values from -5 to 5
- attend_out_square: float32 [384, 384], P('wide', 'narrow'), may hold values from 0.1024 to 0.4096
- vectors: float32 [13, 384], P(None, 'narrow')
- vectors_moment: float32 [13, 384], P(None, 'narrow'), may hold values from -48 to 48
- vectors_square: float32 [13, 384], P(None, 'narrow'), may hold values from 5.0176 to 20.0704
Outputs:
- output: bfloat16 [16, 384, 1024], P('wide', 'narrow')
- input_gradient: bfloat16 [16, 384, 1024], P('wide', 'narrow')
- conv_first_gradient: float32 [3456, 384], P('wide', 'narrow')
- conv_first_new: float32 [3456, 384], P('wide', 'narrow')
- conv_first_moment_new: float32 [3456, 384], P('wide', 'narrow')
- conv_first_square_new: float32 [3456, 384], P('wide', 'narrow')
- conv_second_gradient: float32 [3456, 384], P('wide', 'narrow')
- conv_second_new: float32 [3456, 384], P('wide', 'narrow')
- conv_second_moment_new: float32 [3456, 384], P('wide', 'narrow')
- conv_second_square_new: float32 [3456, 384], P('wide', 'narrow')
- film_weight_gradient: float32 [768, 2, 384], P('wide', None, 'narrow')
- film_weight_new: float32 [768, 2, 384], P('wide', None, 'narrow')
- film_weight_moment_new: float32 [768, 2, 384], P('wide', None, 'narrow')
- film_weight_square_new: float32 [768, 2, 384], P('wide', None, 'narrow')
- attend_in_gradient: float32 [384, 3, 384], P('wide', None, 'narrow')
- attend_in_new: float32 [384, 3, 384], P('wide', None, 'narrow')
- attend_in_moment_new: float32 [384, 3, 384], P('wide', None, 'narrow')
- attend_in_square_new: float32 [384, 3, 384], P('wide', None, 'narrow')
- attend_out_gradient: float32 [384, 384], P('wide', 'narrow')
- attend_out_new: float32 [384, 384], P('wide', 'narrow')
- attend_out_moment_new: float32 [384, 384], P('wide', 'narrow')
- attend_out_square_new: float32 [384, 384], P('wide', 'narrow')
- vectors_gradient: float32 [13, 384], P(None, 'narrow')
- vectors_new: float32 [13, 384], P(None, 'narrow')
- vectors_moment_new: float32 [13, 384], P(None, 'narrow')
- vectors_square_new: float32 [13, 384], P(None, 'narrow')
Inputs may be any that keep to these rules, and one draw needn't show every extreme that they name: `valid_mask`: each sample's mask is either all ones or ones exactly on a 16 x 16 square of pixels.
All inputs are finite; a program needn't handle non-finite values.
Results may differ from a plain program's by a relative error of at most 0.02.
Values may be sent and summed in bfloat16 or wider, within the bound.
No kernel may reach another device: no remote copies, remote signals or barrier semaphores. Data moves between devices by JAX's collectives and lax.ppermute only.
A program may use at most 128 MiB of HBM per device.

v0:
```python
import jax
import jax.numpy as jnp
from jax import lax
from jax.sharding import PartitionSpec as P

C = 384
HEADS = 4
GROUPS = 32
EMB = 768
SIDE = 32
STEP = 10


beta_one = 0.9
beta_two = 0.999
adam_eps = 1e-08
decay_rate = 0.01
norm_eps = 1e-05
masked_score = -1e30


def step_rates():
    return (
        2.0 * (9 * C) ** (-0.5),
        2.0 * (9 * C) ** (-0.5),
        2.0 * EMB ** (-0.5),
        2.0 * C ** (-0.5),
        2.0 * (C // 64) ** (-0.5),
        0.5,
    )


def norm_forward(inputs, validity, gain_row, shift_row):
    samples, pixels, channels = inputs.shape
    per_group = C // GROUPS
    grouped = inputs.reshape(samples, pixels, channels // per_group, per_group)
    weight = validity.reshape(samples, pixels, 1, 1)
    tallies = jnp.sum(weight, axis=(1, 3), keepdims=True) * per_group
    average = jnp.sum(grouped * weight, axis=(1, 3), keepdims=True) / tallies
    centred = grouped - average
    variance = jnp.sum(centred * centred * weight, axis=(1, 3), keepdims=True) / tallies
    inverse = lax.rsqrt(variance + norm_eps)
    normed = (centred * inverse).reshape(samples, pixels, channels)
    return ((normed * gain_row + shift_row) * validity[:, :, None], normed, inverse, tallies)


def norm_backward(upstream, normed, inverse, tallies, validity, gain_row):
    samples, pixels, channels = normed.shape
    per_group = C // GROUPS
    masked = upstream * validity[:, :, None]
    gain_grad = jnp.sum(masked * normed, axis=(0, 1))
    shift_grad = jnp.sum(masked, axis=(0, 1))
    scaled = (masked * gain_row).reshape(samples, pixels, channels // per_group, per_group)
    flat_normed = normed.reshape(scaled.shape)
    first_mean = jnp.sum(scaled, axis=(1, 3), keepdims=True) / tallies
    second_mean = jnp.sum(scaled * flat_normed, axis=(1, 3), keepdims=True) / tallies
    weight = validity.reshape(samples, pixels, 1, 1)
    result = weight * inverse * (scaled - first_mean - flat_normed * second_mean)
    return (result.reshape(samples, pixels, channels), gain_grad, shift_grad)


def silu_slope(inputs):
    logistic = jax.nn.sigmoid(inputs)
    return logistic * (1.0 + inputs * (1.0 - logistic))


def convolve(inputs, kernel):
    samples, pixels, channels = inputs.shape
    picture = inputs.reshape(samples, SIDE, SIDE, channels)
    result = lax.conv_general_dilated(
        picture,
        kernel.reshape(3, 3, channels, kernel.shape[1]),
        (1, 1),
        "SAME",
        dimension_numbers=("NHWC", "HWIO", "NHWC"),
        preferred_element_type=jnp.float32,
    )
    return result.reshape(samples, pixels, kernel.shape[1])


def convolve_back(gradient, kernel):
    samples, pixels, outputs = gradient.shape
    channels = kernel.shape[0] // 9
    flipped = kernel.reshape(3, 3, channels, outputs)[::-1, ::-1].transpose(0, 1, 3, 2)
    picture = gradient.reshape(samples, SIDE, SIDE, outputs)
    result = lax.conv_general_dilated(
        picture,
        flipped,
        (1, 1),
        "SAME",
        dimension_numbers=("NHWC", "HWIO", "NHWC"),
        preferred_element_type=jnp.float32,
    )
    return result.reshape(samples, pixels, channels)


def kernel_grad(inputs, gradient):
    samples, pixels, channels = inputs.shape
    picture = inputs.reshape(samples, SIDE, SIDE, channels)
    padded = jnp.pad(picture, ((0, 0), (1, 1), (1, 1), (0, 0)))
    flat_grad = gradient.reshape(samples * pixels, gradient.shape[2])
    blocks = []
    for tap_row in range(3):
        for tap_col in range(3):
            window = padded[:, tap_row : tap_row + SIDE, tap_col : tap_col + SIDE, :].reshape(
                samples * pixels, channels
            )
            blocks.append(
                jnp.einsum("pi,po->io", window, flat_grad, preferred_element_type=jnp.float32)
            )
    return jnp.concatenate(blocks, axis=0)


def split_heads(rows):
    return rows.reshape(rows.shape[0], rows.shape[1] // (C // HEADS), C // HEADS)


def masked_scores(query_heads, key_heads, validity):
    score_scale = (C // HEADS) ** (-0.5)
    scores = (
        jnp.einsum("qhd,khd->hqk", query_heads, key_heads, preferred_element_type=jnp.float32)
        * score_scale
    )
    return jnp.where(validity[None, None, :] > 0, scores, masked_score)


def attend_forward(pieces):
    queries, key_rows, values, validity = pieces
    scores = masked_scores(split_heads(queries), split_heads(key_rows), validity)
    highest = jnp.max(scores, axis=2, keepdims=True)
    exponent = jnp.exp(scores - highest)
    totals = jnp.sum(exponent, axis=2, keepdims=True)
    weights = (exponent / totals).astype(jnp.bfloat16)
    mixture = jnp.einsum(
        "hqk,khd->qhd", weights, split_heads(values), preferred_element_type=jnp.float32
    )
    return (mixture.reshape(queries.shape).astype(jnp.bfloat16), highest + jnp.log(totals))


def attend_backward(pieces):
    queries, key_rows, values, validity, log_total, upstream = pieces
    score_scale = (C // HEADS) ** (-0.5)
    query_heads = split_heads(queries)
    key_heads = split_heads(key_rows)
    up_heads = split_heads(upstream)
    weights = jnp.exp(masked_scores(query_heads, key_heads, validity) - log_total)
    soft_grad = jnp.einsum(
        "qhd,khd->hqk", up_heads, split_heads(values), preferred_element_type=jnp.float32
    )
    value_grad = jnp.einsum(
        "hqk,qhd->khd", weights.astype(jnp.bfloat16), up_heads, preferred_element_type=jnp.float32
    )
    score_grad = weights * (soft_grad - jnp.sum(weights * soft_grad, axis=2, keepdims=True))
    score_grad = score_grad.astype(jnp.bfloat16)
    query_grad = (
        jnp.einsum("hqk,khd->qhd", score_grad, key_heads, preferred_element_type=jnp.float32)
        * score_scale
    )
    key_grad = (
        jnp.einsum("hqk,qhd->khd", score_grad, query_heads, preferred_element_type=jnp.float32)
        * score_scale
    )
    shape_two = queries.shape
    return (
        query_grad.reshape(shape_two).astype(jnp.bfloat16),
        key_grad.reshape(shape_two).astype(jnp.bfloat16),
        value_grad.reshape(shape_two).astype(jnp.bfloat16),
    )


def adam_update(weight, gradient, moment, square, step_rate):
    moment_new = beta_one * moment + (1.0 - beta_one) * gradient
    square_new = beta_two * square + (1.0 - beta_two) * gradient * gradient
    ratio = (
        moment_new
        / (1.0 - beta_one**STEP)
        / (jnp.sqrt(square_new / (1.0 - beta_two**STEP)) + adam_eps)
    )
    return (weight - step_rate * (ratio + decay_rate * weight), moment_new, square_new)


def per_device(
    features,
    embedding,
    valid_mask,
    cotangent,
    conv_first,
    conv_first_moment,
    conv_first_square,
    conv_second,
    conv_second_moment,
    conv_second_square,
    film_weight,
    film_weight_moment,
    film_weight_square,
    attend_in,
    attend_in_moment,
    attend_in_square,
    attend_out,
    attend_out_moment,
    attend_out_square,
    vectors,
    vectors_moment,
    vectors_square,
):
    samples, part_width, pixels = features.shape
    validity = valid_mask.astype(jnp.float32)
    valid_col = validity[:, :, None]
    inputs = jnp.transpose(features.astype(jnp.float32), (0, 2, 1))

    def widen(partial_rows):
        return lax.all_gather(partial_rows, "narrow", axis=2, tiled=True)

    first_full, second_full, film_full, triple_full, out_full = (
        lax.all_gather(conv_first.astype(jnp.bfloat16), "wide", axis=0, tiled=True),
        lax.all_gather(conv_second.astype(jnp.bfloat16), "wide", axis=0, tiled=True),
        lax.all_gather(film_weight.astype(jnp.bfloat16), "wide", axis=0, tiled=True),
        lax.all_gather(attend_in.astype(jnp.bfloat16), "wide", axis=0, tiled=True),
        lax.all_gather(attend_out.astype(jnp.bfloat16), "wide", axis=0, tiled=True),
    )

    def narrow_sum(terms):
        return lax.psum_scatter(
            terms.astype(jnp.bfloat16), "narrow", scatter_dimension=2, tiled=True
        ).astype(jnp.float32)

    def conv_input_back(gradient, kernel_part):
        return narrow_sum(convolve_back(gradient, kernel_part))

    norm_one, normed_one, inverse_one, tallies = norm_forward(
        inputs, validity, vectors[0], vectors[1]
    )
    hidden_one = widen(jax.nn.silu(norm_one).astype(jnp.bfloat16))
    conv_out_one = convolve(hidden_one, first_full) + vectors[2]
    soft_embed = jax.nn.silu(embedding.astype(jnp.float32)).astype(jnp.bfloat16)
    film_terms = jnp.dot(
        soft_embed, film_full.reshape(EMB, 2 * part_width), preferred_element_type=jnp.float32
    )
    film_terms = film_terms.reshape(samples, 2, part_width) + vectors[11:13]
    scale_term = 1.0 + film_terms[:, None, 0]
    shift_term = film_terms[:, None, 1]
    norm_two, normed_two, inverse_two = norm_forward(
        conv_out_one, validity, vectors[3], vectors[4]
    )[:3]
    modulated = norm_two * scale_term + shift_term
    hidden_two = widen((jax.nn.silu(modulated) * valid_col).astype(jnp.bfloat16))
    conv_out_two = convolve(hidden_two, second_full) + vectors[5]
    residual = (inputs + conv_out_two) * valid_col
    norm_three, normed_three, inverse_three = norm_forward(
        residual, validity, vectors[6], vectors[7]
    )[:3]
    hidden_three = widen(norm_three.astype(jnp.bfloat16))
    triple_flat = triple_full.reshape(C, 3 * part_width)
    triple = jnp.dot(hidden_three.reshape(-1, C), triple_flat, preferred_element_type=jnp.float32)
    queries = (
        (triple[:, :part_width] + vectors[8])
        .astype(jnp.bfloat16)
        .reshape(samples, pixels, part_width)
    )
    key_rows = (
        triple[:, part_width : 2 * part_width]
        .astype(jnp.bfloat16)
        .reshape(samples, pixels, part_width)
    )
    values = (
        (triple[:, 2 * part_width :] + vectors[9])
        .astype(jnp.bfloat16)
        .reshape(samples, pixels, part_width)
    )
    attended, log_totals = lax.map(attend_forward, (queries, key_rows, values, validity))
    attended_full = widen(attended)
    projected = jnp.dot(attended_full.reshape(-1, C), out_full, preferred_element_type=jnp.float32)
    projected = projected.reshape(samples, pixels, part_width) + vectors[10]
    output = jnp.transpose((residual + projected * valid_col).astype(jnp.bfloat16), (0, 2, 1))
    upstream = jnp.transpose(cotangent.astype(jnp.float32), (0, 2, 1))
    masked_cotangent = (upstream * valid_col).astype(jnp.bfloat16)
    flat_cotangent = masked_cotangent.reshape(-1, part_width)
    out_grad = jnp.einsum(
        "ni,no->io",
        attended_full.reshape(-1, C),
        flat_cotangent,
        preferred_element_type=jnp.float32,
    )
    out_bias = jnp.sum(masked_cotangent.astype(jnp.float32), axis=(0, 1))
    terms = jnp.einsum(
        "spo,io->spi", masked_cotangent, out_full, preferred_element_type=jnp.float32
    )
    attended_grad = narrow_sum(terms).astype(jnp.bfloat16)
    query_grad, key_grad, value_grad = lax.map(
        attend_backward, (queries, key_rows, values, validity, log_totals, attended_grad)
    )
    triple_grad_rows = jnp.concatenate((query_grad, key_grad, value_grad), axis=2).reshape(
        -1, 3 * part_width
    )
    triple_grad = jnp.einsum(
        "ni,nj->ij",
        hidden_three.reshape(-1, C),
        triple_grad_rows,
        preferred_element_type=jnp.float32,
    ).reshape(C, 3, part_width)
    query_bias = jnp.sum(query_grad.astype(jnp.float32), axis=(0, 1))
    value_bias = jnp.sum(value_grad.astype(jnp.float32), axis=(0, 1))
    terms = jnp.einsum(
        "nj,ij->ni",
        triple_grad_rows,
        triple_full.reshape(C, 3 * part_width),
        preferred_element_type=jnp.float32,
    )
    norm_three_grad = narrow_sum(terms.reshape(samples, pixels, C))
    residual_extra, gain_three, shift_three = norm_backward(
        norm_three_grad, normed_three, inverse_three, tallies, validity, vectors[6]
    )
    residual_grad = (upstream + residual_extra) * valid_col
    conv_two_grad = residual_grad.astype(jnp.bfloat16)
    bias_two = jnp.sum(conv_two_grad.astype(jnp.float32), axis=(0, 1))
    second_grad = kernel_grad(hidden_two, conv_two_grad)
    hidden_two_grad = conv_input_back(conv_two_grad, second_full)
    modulated_grad = hidden_two_grad * valid_col * silu_slope(modulated)
    film_grad = jnp.stack(
        (jnp.sum(modulated_grad * norm_two, axis=1), jnp.sum(modulated_grad, axis=1)), axis=1
    )
    film_grad = film_grad.astype(jnp.bfloat16)
    film_weight_grad = jnp.einsum(
        "se,sj->ej",
        soft_embed,
        film_grad.reshape(samples, 2 * part_width),
        preferred_element_type=jnp.float32,
    ).reshape(EMB, 2, part_width)
    film_bias = jnp.sum(film_grad.astype(jnp.float32), axis=0)
    conv_one_float, gain_two, shift_two = norm_backward(
        modulated_grad * scale_term, normed_two, inverse_two, tallies, validity, vectors[3]
    )
    conv_one_grad = conv_one_float.astype(jnp.bfloat16)
    bias_one = jnp.sum(conv_one_grad.astype(jnp.float32), axis=(0, 1))
    first_grad = kernel_grad(hidden_one, conv_one_grad)
    hidden_one_grad = conv_input_back(conv_one_grad, first_full)
    input_extra, gain_one, shift_one = norm_backward(
        hidden_one_grad * silu_slope(norm_one),
        normed_one,
        inverse_one,
        tallies,
        validity,
        vectors[0],
    )
    input_gradient = jnp.transpose((residual_grad + input_extra).astype(jnp.bfloat16), (0, 2, 1))
    vector_terms = jnp.stack(
        (
            gain_one,
            shift_one,
            bias_one,
            gain_two,
            shift_two,
            bias_two,
            gain_three,
            shift_three,
            query_bias,
            value_bias,
            out_bias,
            film_bias[0],
            film_bias[1],
        ),
        axis=0,
    )
    vector_grad = lax.psum(vector_terms, "wide")
    reduced_out, reduced_triple, reduced_second, reduced_film, reduced_first = (
        lax.psum_scatter(out_grad, "wide", scatter_dimension=0, tiled=True),
        lax.psum_scatter(triple_grad, "wide", scatter_dimension=0, tiled=True),
        lax.psum_scatter(second_grad, "wide", scatter_dimension=0, tiled=True),
        lax.psum_scatter(film_weight_grad, "wide", scatter_dimension=0, tiled=True),
        lax.psum_scatter(first_grad, "wide", scatter_dimension=0, tiled=True),
    )
    rates = step_rates()
    masters = (conv_first, conv_second, film_weight, attend_in, attend_out, vectors)
    reduced = (
        reduced_first,
        reduced_second,
        reduced_film,
        reduced_triple,
        reduced_out,
        vector_grad,
    )
    moments = (
        conv_first_moment,
        conv_second_moment,
        film_weight_moment,
        attend_in_moment,
        attend_out_moment,
        vectors_moment,
    )
    squares = (
        conv_first_square,
        conv_second_square,
        film_weight_square,
        attend_in_square,
        attend_out_square,
        vectors_square,
    )
    results = [output, input_gradient]
    for index in range(6):
        new_weight, moment_new, square_new = adam_update(
            masters[index], reduced[index], moments[index], squares[index], rates[index]
        )
        results = results + [reduced[index], new_weight, moment_new, square_new]
    return tuple(results)


def solution(mesh):
    in_specs = (
        P("wide", "narrow", None),
        P("wide", None),
        P("wide", None),
        P("wide", "narrow", None),
        P("wide", "narrow"),
        P("wide", "narrow"),
        P("wide", "narrow"),
        P("wide", "narrow"),
        P("wide", "narrow"),
        P("wide", "narrow"),
        P("wide", None, "narrow"),
        P("wide", None, "narrow"),
        P("wide", None, "narrow"),
        P("wide", None, "narrow"),
        P("wide", None, "narrow"),
        P("wide", None, "narrow"),
        P("wide", "narrow"),
        P("wide", "narrow"),
        P("wide", "narrow"),
        P(None, "narrow"),
        P(None, "narrow"),
        P(None, "narrow"),
    )
    out_specs = (
        P("wide", "narrow", None),
        P("wide", "narrow", None),
        P("wide", "narrow"),
        P("wide", "narrow"),
        P("wide", "narrow"),
        P("wide", "narrow"),
        P("wide", "narrow"),
        P("wide", "narrow"),
        P("wide", "narrow"),
        P("wide", "narrow"),
        P("wide", None, "narrow"),
        P("wide", None, "narrow"),
        P("wide", None, "narrow"),
        P("wide", None, "narrow"),
        P("wide", None, "narrow"),
        P("wide", None, "narrow"),
        P("wide", None, "narrow"),
        P("wide", None, "narrow"),
        P("wide", "narrow"),
        P("wide", "narrow"),
        P("wide", "narrow"),
        P("wide", "narrow"),
        P(None, "narrow"),
        P(None, "narrow"),
        P(None, "narrow"),
        P(None, "narrow"),
    )
    return jax.shard_map(
        per_device, mesh=mesh, in_specs=in_specs, out_specs=out_specs, check_vma=False
    )
```

profile of v0, /device:TPU:0, one launch (start us, length us, event | category | flops | bytes accessed | tf_op | source)
XLA Modules:
  0.0 665.9 jit_solution(11263942033629149011)
XLA Ops:
  20.8 12.7 %all_gather.27 = bf16[1,1024,384]{1,2,0:T(8,128)(2,1)S(1)} all-gather(bf16[1,1024,192]{1,2,0:T(8,128)(2,1)S(1)} %multiply_convert_fusion.4), channel_id=1, replica_groups=mesh['wide'=16,'narrow'=2] {'narrow'}, dimensions={2}, use_global_device_ids=true | all-gather | bytes 1179648 | tf_op jit(solution)/shard_map/all_gather | solution.py:212
  35.9 24.6 %all_gather.29 = bf16[768,2,192]{2,1,0:T(2,128)(2,1)S(1)} all-gather(bf16[48,2,192]{2,1,0:T(2,128)(2,1)S(1)} %convert_element_type.269), channel_id=1, replica_groups=mesh['wide'=16,'narrow'=2] {'wide'}, dimensions={0}, use_global_device_ids=true | all-gather | bytes 626688 | tf_op jit(solution)/shard_map/all_gather | solution.py:217
  62.1 19.7 %all_gather.33 = bf16[384,3,192]{2,0,1:T(8,128)(2,1)S(1)} all-gather(bf16[24,3,192]{2,0,1:T(8,128)(2,1)S(1)} %convert_element_type.273), channel_id=1, replica_groups=mesh['wide'=16,'narrow'=2] {'wide'}, dimensions={0}, use_global_device_ids=true | all-gather | bytes 470016 | tf_op jit(solution)/shard_map/all_gather | solution.py:218
  83.4 3.7 copy.145
  87.1 5.4 broadcast_add_fusion
  99.4 12.2 %all_gather.30 = bf16[1,1024,384]{1,2,0:T(8,128)(2,1)S(1)} all-gather(bf16[1,1024,192]{1,2,0:T(8,128)(2,1)S(1)} %multiply_convert_fusion.3), channel_id=1, replica_groups=mesh['wide'=16,'narrow'=2] {'narrow'}, dimensions={2}, use_global_device_ids=true | all-gather | bytes 1179648 | tf_op jit(solution)/shard_map/all_gather | solution.py:212
  114.0 3.7 copy.157
  117.7 4.4 fusion.24
  130.0 11.2 %all_gather.32 = bf16[1,1024,384]{1,2,0:T(8,128)(2,1)S(1)} all-gather(bf16[1,1024,192]{1,2,0:T(8,128)(2,1)S(1)} %multiply_convert_fusion.2), channel_id=1, replica_groups=mesh['wide'=16,'narrow'=2] {'narrow'}, dimensions={2}, use_global_device_ids=true | all-gather | bytes 1179648 | tf_op jit(solution)/shard_map/all_gather | solution.py:212
  150.2 10.3 %all_gather.34 = bf16[1,1024,384]{1,2,0:T(8,128)(2,1)S(1)} all-gather(bf16[1,1024,192]{1,2,0:T(8,128)(2,1)S(1)} %bitcast.395), channel_id=1, replica_groups=mesh['wide'=16,'narrow'=2] {'narrow'}, dimensions={2}, use_global_device_ids=true | all-gather | bytes 1179648 | tf_op jit(solution)/shard_map/all_gather | solution.py:212
  163.1 53.4 %reduce-scatter.23.cloned.1.call-done = f32[24,192]{1,0:T(8,128)} async-done(((f32[384,192]{1,0:T(8,128)}), f32[24,192]{1,0:T(8,128)}) %reduce-scatter.23.cloned.1.call-update) | async-done | bytes 18448 | tf_op jit(solution)/shard_map/reduce_scatter | solution.py:366
  217.9 19.9 %all_gather.35 = bf16[384,192]{1,0:T(8,128)(2,1)S(1)} all-gather(bf16[24,192]{1,0:T(8,128)(2,1)S(1)} %get-tuple-element.141), channel_id=1, replica_groups=mesh['wide'=16,'narrow'=2] {'wide'}, dimensions={0}, use_global_device_ids=true | all-gather | bytes 156672 | tf_op jit(solution)/shard_map/all_gather | solution.py:219
  240.9 4.8 copy.190
  249.1 14.0 %reduce-scatter.25.cloned.1.call-done = bf16[192,1024]{1,0:T(8,128)(2,1)} async-done(((bf16[384,1024]{1,0:T(8,128)(2,1)}), bf16[192,1024]{1,0:T(8,128)(2,1)}) %reduce-scatter.25.cloned.1.call-update) | async-done | bytes 393232
  264.7 5.5 multiply_reduce_fusion
  285.7 12.7 %reduce-scatter.15.cloned.1.call-done = bf16[1,1024,192]{1,2,0:T(8,128)(2,1)} async-done(((bf16[1,1024,384]{1,2,0:T(8,128)(2,1)}), bf16[1,1024,192]{1,2,0:T(8,128)(2,1)}) %reduce-scatter.15.cloned.1.call-update) | async-done | bytes 393232 | tf_op jit(solution)/shard_map/reduce_scatter | solution.py:223
  318.9 6.9 %pad_slice_fusion = (bf16[1,32,32,384]{3,2,1,0:T(8,128)(2,1)}, bf16[1,32,32,384]{3,2,1,0:T(8,128)(2,1)}, bf16[1,32,32,384]{3,2,1,0:T(8,128)(2,1)}, bf16[1,32,32,...) fusion(bf16[1,32,32,384]{3,2,1,0:T(8,128)(2,1)} %bitcast.322), kind=kLoop, calls=%fused_computation.70 | loop fusion | bytes 7077888 | tf_op jit(solution)/shard_map/slice | solution.py:105
  363.5 4.8 copy.194
  381.9 4.8 copy.192
  391.6 3.8 reduce-scatter.21.cloned.1.call-done
  397.2 96.2 %all-reduce.5.cloned.1.call-done = f32[768,2,192]{2,1,0:T(2,128)} async-done(((f32[768,2,192]{2,1,0:T(2,128)}), f32[768,2,192]{2,1,0:T(2,128)}) %all-reduce.5.cloned.1.call-update) | async-done | bytes 1179664
  495.3 16.7 %reduce-scatter.19.cloned.1.call-done = bf16[1,1024,192]{1,2,0:T(8,128)(2,1)} async-done(((bf16[1,1024,384]{1,2,0:T(8,128)(2,1)}), bf16[1,1024,192]{1,2,0:T(8,128)(2,1)}) %reduce-scatter.19.cloned.1.call-update) | async-done | bytes 393232 | tf_op jit(solution)/shard_map/reduce_scatter | solution.py:223
  517.2 61.7 %psum.7 = f32[13,192]{1,0:T(8,128)S(1)} all-reduce(f32[13,192]{1,0:T(8,128)S(1)} %stack.68), channel_id=1, replica_groups=mesh['wide'=16,'narrow'=2] {'wide'}, use_global_device_ids=true, to_apply=%region_50.51 | all-reduce | flops 2496 | bytes 19968 | tf_op jit(solution)/shard_map/psum | solution.py:364
  586.5 69.4 %reduce-scatter.27.cloned.1.call-done = f32[216,192]{1,0:T(8,128)} async-done(((f32[3456,192]{1,0:T(8,128)}), f32[216,192]{1,0:T(8,128)}) %reduce-scatter.27.cloned.1.call-update) | async-done | bytes 165904
  (429 shorter events, 166.2 us)
Async XLA Ops:
  7.2 76.2 %all-gather.5.cloned.1.call-start = ((), (), s32[]{:S(2)}) async-start(), calls=%async_computation.13 | async-start | bytes 1671168 | tf_op jit(solution)/shard_map/all_gather | solution.py:215
  8.9 105.2 %all-gather.7.cloned.1.call-start = ((), (), s32[]{:S(2)}) async-start(), calls=%async_computation.14 | async-start | bytes 1671168 | tf_op jit(solution)/shard_map/all_gather | solution.py:216
  10.5 206.0 %reduce-scatter.23.cloned.1.call-start = ((), (), s32[]{:S(2)}) async-start(), calls=%async_computation.12 | async-start | bytes 417792 | tf_op jit(solution)/shard_map/reduce_scatter | solution.py:366
  14.8 497.2 %copy-start.50 = (f32[192]{0:T(256)}, f32[192]{0:T(256)S(1)}, u32[]{:S(2)}) copy-start(f32[192]{0:T(256)S(1)} %sub.234) | copy-start | bytes 2308
  162.6 100.6 %reduce-scatter.25.cloned.1.call-start = ((), (), s32[]{:S(2)}) async-start(), calls=%async_computation.15 | async-start | bytes 1179648
  248.4 50.0 %reduce-scatter.15.cloned.1.call-start = ((), (), s32[]{:S(2)}) async-start(), calls=%async_computation.8 | async-start | bytes 1179648 | tf_op jit(solution)/shard_map/reduce_scatter | solution.py:223
  280.8 52.3 %reduce-scatter.17.cloned.1.call-start = ((), (), s32[]{:S(2)}) async-start(), calls=%async_computation.9 | async-start | bytes 1179648 | tf_op jit(solution)/shard_map/reduce_scatter | solution.py:223
  315.5 79.9 %reduce-scatter.21.cloned.1.call-start = ((), (), s32[]{:S(2)}) async-start(), calls=%async_computation.11 | async-start | bytes 1253376 | tf_op jit(solution)/shard_map/reduce_scatter | solution.py:367
  327.8 165.5 %all-reduce.5.cloned.1.call-start = ((), (), s32[]{:S(2)}) async-start(), calls=%async_computation.18 | async-start | bytes 3145728
  341.4 170.5 %reduce-scatter.19.cloned.1.call-start = ((), (), s32[]{:S(2)}) async-start(), calls=%async_computation.10 | async-start | bytes 1179648 | tf_op jit(solution)/shard_map/reduce_scatter | solution.py:223
  353.0 231.6 %reduce-scatter.29.cloned.1.call-start = ((), (), s32[]{:S(2)}) async-start(), calls=%async_computation.17 | async-start | bytes 3760128
  368.2 287.7 %reduce-scatter.27.cloned.1.call-start = ((), (), s32[]{:S(2)}) async-start(), calls=%async_computation.16 | async-start | bytes 3760128
  388.6 104.7 %copy-start.37 = (f32[48,2,192]{2,1,0:T(2,128)S(1)}, f32[48,2,192]{2,1,0:T(2,128)}, u32[]{:S(2)}) copy-start(f32[48,2,192]{2,1,0:T(2,128)} %param.32) | copy-start | bytes 221188
  388.8 104.6 %copy-start.44 = (f32[48,2,192]{2,1,0:T(2,128)S(1)}, f32[48,2,192]{2,1,0:T(2,128)}, u32[]{:S(2)}) copy-start(f32[48,2,192]{2,1,0:T(2,128)} %param.33) | copy-start | bytes 221188
  388.8 123.2 %copy-start.56 = (f32[192]{0:T(256)S(1)}, f32[192]{0:T(256)}, u32[]{:S(2)}) copy-start(f32[192]{0:T(256)} %copy-done.55) | copy-start | bytes 2308
  388.8 123.2 %copy-start.58 = (f32[1,192]{1,0:T(1,128)S(1)}, f32[1,192]{1,0:T(1,128)}, u32[]{:S(2)}) copy-start(f32[1,192]{1,0:T(1,128)} %copy-done.57) | copy-start | bytes 2308
  388.9 104.4 %copy-start.45 = (f32[48,2,192]{2,1,0:T(2,128)S(1)}, f32[48,2,192]{2,1,0:T(2,128)}, u32[]{:S(2)}) copy-start(f32[48,2,192]{2,1,0:T(2,128)} %param.34) | copy-start | bytes 221188
  388.9 123.1 %copy-start.76 = (f32[1,192]{1,0:T(1,128)S(1)}, f32[1,192]{1,0:T(1,128)}, u32[]{:S(2)}) copy-start(f32[1,192]{1,0:T(1,128)} %copy-done.75) | copy-start | bytes 2308
  388.9 190.0 %copy-start.48 = (f32[13,192]{1,0:T(8,128)S(1)}, f32[13,192]{1,0:T(8,128)}, u32[]{:S(2)}) copy-start(f32[13,192]{1,0:T(8,128)} %param.41) | copy-start | bytes 29956
  388.9 190.0 %copy-start.59 = (f32[13,192]{1,0:T(8,128)S(1)}, f32[13,192]{1,0:T(8,128)}, u32[]{:S(2)}) copy-start(f32[13,192]{1,0:T(8,128)} %param.42) | copy-start | bytes 29956
  388.9 190.0 %copy-start.60 = (f32[13,192]{1,0:T(8,128)S(1)}, f32[13,192]{1,0:T(8,128)}, u32[]{:S(2)}) copy-start(f32[13,192]{1,0:T(8,128)} %param.43) | copy-start | bytes 29956
  389.0 190.6 %copy-start.18 = (f32[1,1024,192]{1,2,0:T(8,128)S(1)}, f32[1,1024,192]{1,2,0:T(8,128)}, u32[]{:S(2)}) copy-start(f32[1,1024,192]{1,2,0:T(8,128)} %get-tuple-element.100) | copy-start | bytes 2359300
  495.3 90.3 %copy-start.42 = (f32[216,192]{0,1:T(8,128)S(1)}, f32[216,192]{0,1:T(8,128)}, u32[]{:S(2)}) copy-start(f32[216,192]{0,1:T(8,128)} %param.30) | copy-start | bytes 497668
  495.3 90.3 %copy-start.43 = (f32[216,192]{0,1:T(8,128)S(1)}, f32[216,192]{0,1:T(8,128)}, u32[]{:S(2)}) copy-start(f32[216,192]{0,1:T(8,128)} %param.31) | copy-start | bytes 497668
  (89 other events, 1101.2 us)
Sparse Core Ops, SparseCore 0:
  10.9 45.0 all-gather.4
  58.9 39.2 all-gather.6
  162.7 53.6 reduce-scatter.22
  248.5 14.6 reduce-scatter.24
  280.9 17.4 reduce-scatter.14
  315.6 17.4 reduce-scatter.16
  337.3 58.1 reduce-scatter.20
  398.9 94.3 all-reduce.4
  495.6 16.3 reduce-scatter.18
  516.2 68.3 reduce-scatter.28
  588.9 66.9 reduce-scatter.26
where the time goes:
time: 675 us; the launch traced here: 666 us
  waiting for transfers between devices  270 us (40%)
  blocking collectives  173 us (26%)
  local copies, waits for them, and re-layouts  89.3 us (13%)
  matrix products  67.1 us (10%)
  other arithmetic  48.1 us (7%)
  between operations  17.2 us (3%)
    unnamed x15, waiting for transfers between devices  183 us
    psum x1, blocking collectives, per_device(): vector_grad = lax.psum(vector_terms, 'wide')  61.7 us
    reduce_scatter x1, waiting for transfers between devices, per_device(): lax.psum_scatter(out_grad, 'wide', scatter_dimension=0, tiled=True)  53.4 us
    all_gather x4, blocking collectives, widen(): return lax.all_gather(partial_rows, 'narrow', axis=2, tiled=True)  46.5 us
    unnamed x216, local copies, waits for them, and re-layouts  34.3 us
    reduce_scatter x3, waiting for transfers between devices, narrow_sum(): lax.psum_scatter(terms.astype(jnp.bfloat16), 'narrow', scatter_dimension=...  30.1 us
    dot_general x18, matrix products, kernel_grad(): jnp.einsum('pi,po->io', window, flat_grad, preferred_element_type=jnp.flo...  25.2 us
    all_gather x1, blocking collectives, per_device(): lax.all_gather(film_weight.astype(jnp.bfloat16), 'wide', axis=0, tiled=True)  24.6 us
  transfers between devices with their start and end apart: 11, of which 9 were waited for; matrix products, arithmetic and copies ran while one was open for 18% of the time, Pallas kernels for 0%

commit v1 on v0

v1 whole, which is shorter than its diff:
```python
import jax
import jax.numpy as jnp
from jax import lax
from jax.experimental import pallas as pl
from jax.experimental.pallas import tpu as pltpu
from jax.sharding import PartitionSpec as P

C = 384
HEADS = 4
GROUPS = 32
EMB = 768
SIDE = 32
STEP = 10
PIX = SIDE * SIDE
HALF = C // 2
PADDED = PIX + 2 * SIDE
HEAD = C // HEADS
ROWS = 216
CHUNK = 64

beta_one = 0.9
beta_two = 0.999
adam_eps = 1e-08
decay_rate = 0.01
norm_eps = 1e-05
masked_score = -1e30
score_scale = HEAD ** (-0.5)
exponent_scale = score_scale * 1.4426950408889634

f32 = jnp.float32
bf16 = jnp.bfloat16
ON_LAST = (((1,), (1,)), ((), ()))
ON_FIRST = (((0,), (0,)), ((), ()))
VMEM_BYTES = 56 * 1024 * 1024


def step_rates():
    return (
        2.0 * (9 * C) ** (-0.5),
        2.0 * (9 * C) ** (-0.5),
        2.0 * EMB ** (-0.5),
        2.0 * C ** (-0.5),
        2.0 * (C // 64) ** (-0.5),
        0.5,
    )


def spec():
    return pl.BlockSpec(memory_space=pltpu.VMEM)


def call(body, outs, ins, scalars, scratch=(), flops=0):
    moved = sum(a.size * a.dtype.itemsize for a in list(ins) + list(outs))
    return pl.pallas_call(
        body,
        out_shape=tuple(outs),
        in_specs=[pl.BlockSpec(memory_space=pltpu.SMEM)] + [spec() for _ in ins],
        out_specs=tuple(spec() for _ in outs),
        scratch_shapes=list(scratch),
        compiler_params=pltpu.CompilerParams(vmem_limit_bytes=VMEM_BYTES),
        cost_estimate=pl.CostEstimate(flops=flops, bytes_accessed=moved, transcendentals=0),
    )(scalars, *ins)


def shaped(shape, kind):
    return jax.ShapeDtypeStruct(shape, kind)


def aligned(value, by):
    return pl.multiple_of(value, by)


def wide_mask(mask_ref, start, count):
    part = mask_ref[pl.ds(start, count), :]
    return jnp.concatenate((part, part, part), axis=1)


def group_sum(row):
    first = (lax.broadcasted_iota(jnp.int32, (C, C), 0) * 5462) >> 16
    second = (lax.broadcasted_iota(jnp.int32, (C, C), 1) * 5462) >> 16
    member = jnp.where(first == second, 1.0, 0.0).astype(f32)
    spread = jnp.broadcast_to(row, (8, C))
    return jnp.dot(
        spread, member, preferred_element_type=f32, precision=lax.Precision.HIGHEST
    )[0:1]


def fold(block):
    return jnp.sum(block.reshape(block.shape[0] // 8, 8, block.shape[1]), axis=0)


def total(acc):
    return jnp.sum(acc, axis=0, keepdims=True)


def chunks(step, init):
    def body(index, carry):
        return step(aligned(index * CHUNK, CHUNK), carry)

    return lax.fori_loop(0, PIX // CHUNK, body, init, unroll=2)


def norm_stats(source_ref, mask_ref):
    zero = jnp.zeros((8, C), f32)

    def first(start, carry):
        sums, count = carry
        valid = wide_mask(mask_ref, start, CHUNK)
        return (sums + fold(source_ref[pl.ds(start, CHUNK), :] * valid), count + fold(valid))

    sums, count = chunks(first, (zero, zero))
    tally = total(count) * float(C // GROUPS)
    mean = group_sum(total(sums)) / tally

    def second(start, carry):
        valid = wide_mask(mask_ref, start, CHUNK)
        centred = source_ref[pl.ds(start, CHUNK), :] - mean
        return carry + fold(centred * centred * valid)

    variance = group_sum(total(chunks(second, zero))) / tally
    return mean, lax.rsqrt(variance + norm_eps), tally


def keep_stats(stat_ref, mean, inverse, tally):
    stat_ref[0:1, :] = mean
    stat_ref[1:2, :] = inverse
    stat_ref[2:3, :] = tally


def column_index(count):
    return lax.broadcasted_iota(jnp.int32, (count, 1), 0) & (SIDE - 1)


def write_taps(rows_ref, taps_ref):
    blank = jnp.zeros((SIDE, 3 * C), bf16)
    taps_ref[0:SIDE, :] = blank
    taps_ref[SIDE + PIX : PADDED, :] = blank
    column = column_index(CHUNK)
    for index in range(PIX // CHUNK):
        start = index * CHUNK
        here = pl.ds(SIDE + start, CHUNK)
        left = rows_ref[pl.ds(7 + start, CHUNK), :]
        right = rows_ref[pl.ds(9 + start, CHUNK), :]
        taps_ref[here, 0:C] = jnp.where(column == 0, 0.0, left).astype(bf16)
        taps_ref[here, C : 2 * C] = rows_ref[pl.ds(8 + start, CHUNK), :].astype(bf16)
        taps_ref[here, 2 * C : 3 * C] = jnp.where(column == SIDE - 1, 0.0, right).astype(bf16)


def lane(count):
    return lax.broadcasted_iota(jnp.int32, (count, 128), 1)


def own_half(block, narrow):
    one, two, three = block[:, 0:128], block[:, 128:256], block[:, 256:384]
    turned_two, turned_three = pltpu.roll(two, 64, 1), pltpu.roll(three, 64, 1)
    upper = jnp.where(lane(block.shape[0]) < 64, turned_two, turned_three)
    return jnp.concatenate(
        (jnp.where(narrow == 0, one, upper), jnp.where(narrow == 0, two, turned_three)), axis=1
    )


def write_own(rows_ref, own_ref, narrow):
    blank = jnp.zeros((SIDE, 256), bf16)
    own_ref[0:SIDE, :] = blank
    own_ref[SIDE + PIX : PADDED, :] = blank
    for index in range(PIX // CHUNK):
        start = index * CHUNK
        block = rows_ref[pl.ds(8 + start, CHUNK), :]
        own_ref[pl.ds(SIDE + start, CHUNK), :] = own_half(block, narrow).astype(bf16)


def convolve(taps_ref, kernel_ref, done, block=512):
    for index in range(PIX // block):
        start = index * block
        acc = None
        for tap in range(3):
            part = jnp.dot(
                taps_ref[pl.ds(start + SIDE * tap, block), :],
                kernel_ref[tap * 3 * C : (tap + 1) * 3 * C, :],
                preferred_element_type=f32,
            )
            acc = part if acc is None else acc + part
        done(start, block, acc)


def convolve_back(taps_ref, kernel_ref, done, block=512):
    for index in range(PIX // block):
        start = index * block
        acc = None
        for tap in range(9):
            tap_row, tap_col = tap // 3, tap % 3
            flipped = 8 - tap
            part = lax.dot_general(
                taps_ref[pl.ds(start + SIDE * tap_row, block), tap_col * C : (tap_col + 1) * C],
                kernel_ref[flipped * C : (flipped + 1) * C, :],
                ON_LAST,
                preferred_element_type=f32,
            )
            acc = part if acc is None else acc + part
        done(start, block, acc)


def kernel_terms(taps_ref, own_ref, terms_ref):
    for tap_col in range(3):
        for tap_row in range(3):
            tap = 3 * tap_row + tap_col
            first = 2 * SIDE - SIDE * tap_row
            terms_ref[tap * C : (tap + 1) * C, :] = lax.dot_general(
                taps_ref[SIDE : SIDE + PIX, tap_col * C : (tap_col + 1) * C],
                own_ref[first : first + PIX, :],
                ON_FIRST,
                preferred_element_type=f32,
            )


def slope(value):
    logistic = lax.logistic(value)
    return logistic * (1.0 + value * (1.0 - logistic))


def tile_parts(block, narrow):
    rows = block.shape[0]
    one = block[:, 0:128]
    two = jnp.concatenate((block[:, 128:192], jnp.zeros((rows, 64), f32)), axis=1)
    turned = jnp.where(lane(rows) < 64, pltpu.roll(one, 64, 1), pltpu.roll(two, 64, 1))
    return jnp.where(narrow == 0, one, turned), jnp.where(narrow == 0, two, one)


def pair_rows(block, top):
    rows = block.shape[0]
    low = block[top:rows]
    if rows < 2 * top:
        low = jnp.concatenate((low, jnp.zeros((2 * top - rows, 128), f32)), axis=0)
    return jnp.where(lane(top) < 64, block[0:top], pltpu.roll(low, 64, 1))


def pad_rows(block, rows):
    if block.shape[0] == rows:
        return block
    return jnp.concatenate((block, jnp.zeros((rows - block.shape[0], block.shape[1]), f32)), axis=0)


def middle(first, second, top, rows):
    one = jnp.where(lane(top) < 64, first, pltpu.roll(second, 64, 1))
    two = jnp.where(lane(top) < 64, pltpu.roll(first, 64, 1), second)
    return jnp.concatenate((one, two[0 : rows - top]), axis=0)


def pack_first(at, conv_ref, out_ref):
    part, shared = tile_parts(conv_ref[...], at[0])
    out_ref[0:224, :] = pad_rows(part, 224).astype(bf16)
    out_ref[224:336, :] = pair_rows(shared, 112).astype(bf16)


FILM_AT, SHARED_AT = 224, 320
FILM_SHARED, IN_AT, IN_SHARED, OUT_AT, OUT_SHARED, SECOND_ROWS = 112, 160, 240, 288, 320, 336


def pack_second(at, conv_ref, film_ref, in_ref, out_weight_ref, out_ref):
    narrow = at[0]

    def put(start, block):
        rows = -(-block.shape[0] // 16) * 16
        out_ref[start : start + rows, :] = pad_rows(block, rows).astype(bf16)

    part, shared = tile_parts(conv_ref[...], narrow)
    put(0, part)
    put(SHARED_AT, pair_rows(shared, 112))
    part, shared = tile_parts(jnp.concatenate((film_ref[0], film_ref[1]), axis=0), narrow)
    put(FILM_AT, part)
    put(SHARED_AT + FILM_SHARED, pair_rows(shared, 48))
    part, shared = tile_parts(jnp.concatenate((in_ref[0], in_ref[1], in_ref[2]), axis=0), narrow)
    put(SHARED_AT + IN_AT, part)
    put(SHARED_AT + IN_SHARED, pair_rows(shared, 40))
    part, shared = tile_parts(out_weight_ref[...], narrow)
    put(SHARED_AT + OUT_AT, part)
    put(SHARED_AT + OUT_SHARED, pair_rows(shared, 16))


class Gathered:
    def __init__(self, at, refs):
        self.narrow, self.core, self.side, self.depth = at[0], at[1], at[2], at[3]
        keys = ((0, 0), (1, 0), (0, 1), (1, 1))
        self.own = dict(zip(keys, refs[:4]))
        self.other = dict(zip(keys, refs[4:]))

    def chips(self):
        for differs in (0, 1):
            for step in range(4):
                yield differs, step, (self.depth ^ step) * 2 + (self.side ^ differs)

    def cores(self, differs, step, start, rows):
        upto = -(-rows // 16) * 16
        found = []
        for across in (0, 1):
            own = self.own[differs, across][step, start : start + upto, :].astype(f32)[0:rows]
            other = self.other[differs, across][step, start : start + upto, :].astype(f32)[0:rows]
            found.append(
                (jnp.where(self.core == 0, own, other), jnp.where(self.core == 0, other, own))
            )
        here, there = found
        return tuple(
            tuple(
                jnp.where((self.narrow == 0) == (tile == 0), here[core], there[core])
                for core in (0, 1)
            )
            for tile in (0, 1)
        )


def place_conv(whole, shared, shared_at, kernel_ref):
    for differs, step, chip in whole.chips():
        rows = pl.ds(aligned(chip * (2 * ROWS), 16), 2 * ROWS)
        low, high = whole.cores(differs, step, 0, ROWS)
        kernel_ref[rows, 0:128] = jnp.concatenate(low, axis=0).astype(bf16)
        kernel_ref[rows, 256:384] = jnp.concatenate(high, axis=0).astype(bf16)
        low, high = shared.cores(differs, step, shared_at, 112)
        kernel_ref[rows, 128:256] = jnp.concatenate(
            [middle(low[core], high[core], 112, ROWS) for core in (0, 1)], axis=0
        ).astype(bf16)


def place_film(whole, shared, film_ref):
    for differs, step, chip in whole.chips():
        rows = pl.ds(aligned(chip * 96, 16), 96)
        low, high = whole.cores(differs, step, FILM_AT, 96)
        for index in (0, 1):
            part = slice(48 * index, 48 * index + 48)
            film_ref[rows, index * C : index * C + 128] = jnp.concatenate(
                [low[core][part] for core in (0, 1)], axis=0
            ).astype(bf16)
            film_ref[rows, index * C + 256 : index * C + 384] = jnp.concatenate(
                [high[core][part] for core in (0, 1)], axis=0
            ).astype(bf16)
        low, high = shared.cores(differs, step, FILM_SHARED, 48)
        both = [middle(low[core], high[core], 48, 96) for core in (0, 1)]
        for index in (0, 1):
            part = slice(48 * index, 48 * index + 48)
            film_ref[rows, index * C + 128 : index * C + 256] = jnp.concatenate(
                [both[core][part] for core in (0, 1)], axis=0
            ).astype(bf16)


def place_attention(shared, in_ref, out_ref):
    for differs, step, chip in shared.chips():
        rows = pl.ds(aligned(chip * 48, 16), 48)
        low, high = shared.cores(differs, step, IN_AT, 72)
        near, far = shared.cores(differs, step, IN_SHARED, 40)
        both = [middle(near[core], far[core], 40, 72) for core in (0, 1)]
        for index in range(3):
            part = slice(24 * index, 24 * index + 24)
            for tile, source in ((0, low), (1, both), (2, high)):
                in_ref[rows, index * C + 128 * tile : index * C + 128 * tile + 128] = (
                    jnp.concatenate([source[core][part] for core in (0, 1)], axis=0)
                )
        low, high = shared.cores(differs, step, OUT_AT, 24)
        near, far = shared.cores(differs, step, OUT_SHARED, 16)
        both = [middle(near[core], far[core], 16, 24) for core in (0, 1)]
        for tile, source in ((0, low), (1, both), (2, high)):
            out_ref[rows, 128 * tile : 128 * tile + 128] = jnp.concatenate(source, axis=0)


def spread_heads(block):
    one, two, three = block[:, 0:128], block[:, 128:256], block[:, 256:384]
    place = lane(block.shape[0])

    def cut(value):
        return jnp.where(place < HEAD, value, 0.0)

    return jnp.concatenate(
        (
            cut(one),
            cut(jnp.where(place < 32, pltpu.roll(one, 32, 1), pltpu.roll(two, 32, 1))),
            cut(jnp.where(place < 64, pltpu.roll(two, 64, 1), pltpu.roll(three, 64, 1))),
            cut(pltpu.roll(three, 96, 1)),
        ),
        axis=1,
    )


def join_heads(block):
    one, two = block[:, 0:128], pltpu.roll(block[:, 128:256], HEAD, 1)
    return jnp.concatenate((jnp.where(lane(block.shape[0]) < HEAD, one, two), two), axis=1)


def first_norm(at, own_ref, other_ref, mask_ref, vec_ref, turned_ref, taps_ref, stat_ref, rows_ref, raw_ref):
    narrow = at[0]
    own = own_ref[...].astype(f32)
    other = other_ref[...].astype(f32)
    low = jnp.where(narrow == 0, own, other)
    high = jnp.where(narrow == 0, other, own)
    for index in range(PIX // 128):
        here = slice(128 * index, 128 * index + 128)
        block = jnp.concatenate((low[:, here], high[:, here]), axis=0).T
        raw_ref[here, :] = block
        turned_ref[here, :] = block.astype(bf16)
    mean, inverse, tally = norm_stats(raw_ref, mask_ref)
    keep_stats(stat_ref, mean, inverse, tally)
    gain, shift = vec_ref[0:1, :], vec_ref[1:2, :]

    def apply(start, carry):
        valid = wide_mask(mask_ref, start, CHUNK)
        normed = (raw_ref[pl.ds(start, CHUNK), :] - mean) * inverse
        value = (normed * gain + shift) * valid
        rows_ref[pl.ds(start + 8, CHUNK), :] = value * lax.logistic(value)
        return carry

    chunks(apply, 0)
    write_taps(rows_ref, taps_ref)


def conv_then_stats(taps_ref, kernel_ref, mask_ref, vec_ref, out_ref, stat_ref):
    bias = vec_ref[2:3, :]

    def done(start, count, acc):
        out_ref[pl.ds(start, count), :] = acc + bias

    convolve(taps_ref, kernel_ref, done)
    keep_stats(stat_ref, *norm_stats(out_ref, mask_ref))


def first_conv(at, taps_ref, mask_ref, vec_ref, *refs):
    whole = Gathered(at, refs[0:8])
    shared = Gathered(at, refs[8:16])
    out_ref, kernel_ref, stat_ref = refs[16:]
    place_conv(whole, shared, 0, kernel_ref)
    conv_then_stats(taps_ref, kernel_ref, mask_ref, vec_ref, out_ref, stat_ref)


def first_conv_plain(at, taps_ref, mask_ref, vec_ref, kernel_ref, out_ref, stat_ref):
    conv_then_stats(taps_ref, kernel_ref, mask_ref, vec_ref, out_ref, stat_ref)


def film_to_third_norm(
    one_ref, stat_two_ref, turned_ref, mask_ref, vec_ref, embed_ref, kernel_ref, film_ref,
    taps_ref, residual_ref, hidden_ref, stat_ref, film_rows_ref, soft_ref, rows_ref,
):
    embed = embed_ref[...].astype(f32)
    soft = (embed * lax.logistic(embed)).astype(bf16)
    soft_ref[...] = jnp.broadcast_to(soft.astype(f32), soft_ref.shape)
    rounded = soft_ref[...].astype(bf16)
    scale = 1.0 + (
        jnp.dot(rounded, film_ref[:, 0:C], preferred_element_type=f32)[0:1] + vec_ref[11:12, :]
    )
    shift = jnp.dot(rounded, film_ref[:, C : 2 * C], preferred_element_type=f32)[0:1] + vec_ref[12:13, :]
    film_rows_ref[0:1, :] = scale
    film_rows_ref[1:2, :] = shift
    mean, inverse = stat_two_ref[0:1, :], stat_two_ref[1:2, :]
    gain_two, shift_two = vec_ref[3:4, :], vec_ref[4:5, :]

    def modulate(start, carry):
        valid = wide_mask(mask_ref, start, CHUNK)
        normed = (one_ref[pl.ds(start, CHUNK), :] - mean) * inverse
        value = (normed * gain_two + shift_two) * valid * scale + shift
        rows_ref[pl.ds(start + 8, CHUNK), :] = value * lax.logistic(value) * valid
        return carry

    chunks(modulate, 0)
    write_taps(rows_ref, taps_ref)
    bias = vec_ref[5:6, :]

    def done(start, count, acc):
        here = pl.ds(start, count)
        valid = wide_mask(mask_ref, start, count)
        residual_ref[here, :] = (turned_ref[here, :].astype(f32) + (acc + bias)) * valid

    convolve(taps_ref, kernel_ref, done)
    mean, inverse, tally = norm_stats(residual_ref, mask_ref)
    keep_stats(stat_ref, mean, inverse, tally)
    gain, shift_three = vec_ref[6:7, :], vec_ref[7:8, :]

    def apply(start, carry):
        valid = wide_mask(mask_ref, start, CHUNK)
        normed = (residual_ref[pl.ds(start, CHUNK), :] - mean) * inverse
        hidden_ref[pl.ds(start, CHUNK), :] = ((normed * gain + shift_three) * valid).astype(bf16)
        return carry

    chunks(apply, 0)


def second_conv(at, one_ref, stat_two_ref, turned_ref, mask_ref, vec_ref, embed_ref, *refs):
    whole = Gathered(at, refs[0:8])
    shared = Gathered(at, refs[8:16])
    taps_ref, residual_ref, hidden_ref, stat_ref, film_rows_ref, kernel_ref = refs[16:22]
    soft_ref, rows_ref, film_ref = refs[22:]
    place_film(whole, shared, film_ref)
    place_conv(whole, shared, 0, kernel_ref)
    film_to_third_norm(
        one_ref, stat_two_ref, turned_ref, mask_ref, vec_ref, embed_ref, kernel_ref, film_ref,
        taps_ref, residual_ref, hidden_ref, stat_ref, film_rows_ref, soft_ref, rows_ref,
    )


def second_conv_plain(
    at, one_ref, stat_two_ref, turned_ref, mask_ref, vec_ref, embed_ref, kernel_ref, film_ref,
    taps_ref, residual_ref, hidden_ref, stat_ref, film_rows_ref, soft_ref, rows_ref,
):
    film_to_third_norm(
        one_ref, stat_two_ref, turned_ref, mask_ref, vec_ref, embed_ref, kernel_ref, film_ref,
        taps_ref, residual_ref, hidden_ref, stat_ref, film_rows_ref, soft_ref, rows_ref,
    )


QUERY = 256


def attention_both(q_ref, k_ref, v_ref, up_ref, out_ref, dq_ref, dk_ref, dv_ref, dk_acc, dv_acc):
    place = lane(QUERY)
    for head in range(HEADS):
        columns = slice(128 * head, 128 * head + 128)
        dk_acc[...] = jnp.zeros_like(dk_acc)
        dv_acc[...] = jnp.zeros_like(dv_acc)

        def block(index, carry):
            rows = pl.ds(aligned(index * QUERY, QUERY), QUERY)
            queries, keys, values = q_ref[rows, columns], k_ref[:, columns], v_ref[:, columns]
            scores = lax.dot_general(queries, keys, ON_LAST, preferred_element_type=f32)
            highest = jnp.max(scores, axis=1, keepdims=True)
            raised = jnp.exp2((scores - highest) * exponent_scale)
            raised_low = raised.astype(bf16)
            mixture = jnp.dot(raised_low, values, preferred_element_type=f32)
            inverse = 1.0 / mixture[:, HEAD : HEAD + 1]
            mixture = mixture * inverse
            out_ref[rows, columns] = mixture.astype(bf16)
            up = (up_ref[rows, columns].astype(f32) * inverse).astype(bf16)
            wide_up = up.astype(f32)
            both = jnp.sum(wide_up * mixture, axis=1, keepdims=True)
            coarse = both.astype(bf16).astype(f32)
            wide_up = jnp.where(place == HEAD, -coarse, wide_up)
            wide_up = jnp.where(place == HEAD + 1, coarse - both, wide_up)
            slopes = lax.dot_general(
                wide_up.astype(bf16), values, ON_LAST, preferred_element_type=f32
            )
            slopes = (raised * slopes).astype(bf16)
            dq_ref[rows, columns] = (
                jnp.dot(slopes, keys, preferred_element_type=f32) * score_scale
            ).astype(bf16)
            dk_acc[...] += lax.dot_general(slopes, queries, ON_FIRST, preferred_element_type=f32)
            dv_acc[...] += lax.dot_general(raised_low, up, ON_FIRST, preferred_element_type=f32)
            return carry

        lax.fori_loop(0, PIX // QUERY, block, 0, unroll=True)
        dk_ref[:, columns] = (dk_acc[...] * score_scale).astype(bf16)
        dv_ref[:, columns] = dv_acc[...].astype(bf16)


def attention_body(
    at, hidden_ref, residual_ref, stat_ref, mask_ref, vec_ref, own_ref, other_ref,
    out_ref, direct_ref, taps_ref, back_ref, vec_grad_ref, in_nat, out_nat,
    in_ref, weight_ref, q_ref, k_ref, v_ref, up_ref, mix_ref, dq_ref, dk_ref, dv_ref,
    dk_acc, dv_acc, cot_ref, rows_ref, turn_ref, own_cot,
):
    narrow = at[0]
    for index in range(3):
        in_ref[:, 512 * index : 512 * index + 512] = spread_heads(
            in_nat[:, C * index : C * index + C]
        ).astype(bf16)
    blank = jnp.zeros((32, C), bf16)
    for head in range(HEADS):
        weight_ref[128 * head : 128 * head + HEAD, :] = out_nat[HEAD * head : HEAD * head + HEAD, :].astype(bf16)
        weight_ref[128 * head + HEAD : 128 * head + 128, :] = blank
    own = own_ref[...].astype(f32)
    other = other_ref[...].astype(f32)
    low = jnp.where(narrow == 0, own, other)
    high = jnp.where(narrow == 0, other, own)
    zero = jnp.zeros((8, C), f32)
    bias_out = zero
    for index in range(PIX // 128):
        here = slice(128 * index, 128 * index + 128)
        block = jnp.concatenate((low[:, here], high[:, here]), axis=0).T
        rows_ref[pl.ds(8 + 128 * index, 128), :] = block
        part = block * wide_mask(mask_ref, 128 * index, 128)
        bias_out = bias_out + fold(part)
        cot_ref[here, :] = part.astype(bf16)
        own_cot[here, :] = own_half(part, narrow).astype(bf16)
    bias_q = spread_heads(jnp.broadcast_to(vec_ref[8:9, :], (8, C)))[0:1]
    bias_v = spread_heads(jnp.broadcast_to(vec_ref[9:10, :], (8, C)))[0:1]
    block_rows = 256
    spare = lax.broadcasted_iota(jnp.int32, (block_rows, 512), 1) & 127
    for index in range(PIX // block_rows):
        here = slice(block_rows * index, block_rows * index + block_rows)
        hidden = hidden_ref[here, :]
        value = jnp.dot(hidden, in_ref[:, 0:512], preferred_element_type=f32) + bias_q
        q_ref[here, :] = jnp.where(spare == HEAD, 1.0, value).astype(bf16)
        value = jnp.dot(hidden, in_ref[:, 512:1024], preferred_element_type=f32)
        valid = mask_ref[here, :]
        barred = jnp.where(valid > 0, 0.0, masked_score)
        barred = jnp.concatenate((barred, barred, barred, barred), axis=1)
        k_ref[here, :] = jnp.where(spare == HEAD, barred, value).astype(bf16)
        value = jnp.dot(hidden, in_ref[:, 1024:1536], preferred_element_type=f32) + bias_v
        v_ref[here, :] = jnp.where((spare == HEAD) | (spare == HEAD + 1), 1.0, value).astype(bf16)
        up_ref[here, :] = lax.dot_general(
            cot_ref[here, :], weight_ref[...], ON_LAST, preferred_element_type=f32
        ).astype(bf16)
    attention_both(q_ref, k_ref, v_ref, up_ref, mix_ref, dq_ref, dk_ref, dv_ref, dk_acc, dv_acc)
    bias = vec_ref[10:11, :]
    for index in range(PIX // 128):
        here = slice(128 * index, 128 * index + 128)
        value = jnp.dot(mix_ref[here, :], weight_ref[...], preferred_element_type=f32) + bias
        valid = wide_mask(mask_ref, 128 * index, 128)
        turn_ref[:, here] = (residual_ref[here, :] + value * valid).T
    out_ref[...] = turn_ref[pl.ds(aligned(narrow * HALF, 16), HALF), :].astype(bf16)
    heads_here = pl.ds(aligned(narrow * 256, 128), 256)
    terms = lax.dot_general(mix_ref[...], own_cot[...], ON_FIRST, preferred_element_type=f32)
    for head in range(HEADS):
        out_nat[HEAD * head : HEAD * head + HEAD, 0:256] = terms[128 * head : 128 * head + HEAD]
    sums = []
    for index, source in enumerate((dq_ref, dk_ref, dv_ref)):
        terms = lax.dot_general(
            hidden_ref[...], source[:, heads_here], ON_FIRST, preferred_element_type=f32
        )
        in_nat[:, 256 * index : 256 * index + 256] = join_heads(terms)
        acc = jnp.zeros((8, 512), f32)
        if index != 1:
            for part in range(PIX // 128):
                acc = acc + fold(source[128 * part : 128 * part + 128, :].astype(f32))
        sums.append(acc)
    mean, inverse, tally = stat_ref[0:1, :], stat_ref[1:2, :], stat_ref[2:3, :]
    gain = vec_ref[6:7, :]
    acc_shift, acc_gain = zero, zero
    for index in range(PIX // 256):
        here = slice(256 * index, 256 * index + 256)
        value = None
        for part, source in enumerate((dq_ref, dk_ref, dv_ref)):
            term = lax.dot_general(
                source[here, :], in_ref[:, 512 * part : 512 * part + 512], ON_LAST,
                preferred_element_type=f32,
            )
            value = term if value is None else value + term
        value = value * wide_mask(mask_ref, 256 * index, 256)
        normed = (residual_ref[here, :] - mean) * inverse
        acc_shift = acc_shift + fold(value)
        acc_gain = acc_gain + fold(value * normed)
        direct_ref[here, :] = value
    shift_grad, gain_grad = total(acc_shift), total(acc_gain)
    first_mean = group_sum(gain * shift_grad) / tally
    second_mean = group_sum(gain * gain_grad) / tally

    def back(start, carry):
        valid = wide_mask(mask_ref, start, CHUNK)
        here = pl.ds(start, CHUNK)
        normed = (residual_ref[here, :] - mean) * inverse
        extra = (direct_ref[here, :] * gain - first_mean - normed * second_mean) * inverse
        value = (rows_ref[pl.ds(start + 8, CHUNK), :] + extra) * valid
        direct_ref[here, :] = value
        low = value.astype(bf16).astype(f32)
        rows_ref[pl.ds(start + 8, CHUNK), :] = low
        return carry + fold(low)

    bias_two = chunks(back, zero)
    write_taps(rows_ref, taps_ref)
    write_own(rows_ref, back_ref, narrow)
    vec_grad_ref[...] = jnp.zeros_like(vec_grad_ref)
    vec_grad_ref[5:6, :] = total(bias_two)
    vec_grad_ref[6:7, :] = gain_grad
    vec_grad_ref[7:8, :] = shift_grad
    for row, acc in ((8, sums[0]), (9, sums[2])):
        pair_one, pair_two = join_heads(acc[:, 0:256]), join_heads(acc[:, 256:512])
        turned = pltpu.roll(pair_two[:, 0:128], 64, 1)
        natural = jnp.concatenate(
            (
                pair_one[:, 0:128],
                jnp.where(lane(8) < 64, pair_one[:, 128:256], turned),
                jnp.where(lane(8) < 64, turned, pltpu.roll(pair_two[:, 128:256], 64, 1)),
            ),
            axis=1,
        )
        vec_grad_ref[row : row + 1, :] = total(natural)
    vec_grad_ref[10:11, :] = total(bias_out)


def unit_rows(grad, chip, core):
    return pl.ds(aligned(chip * 2 * grad + core * grad, 8), grad)


def attention(at, hidden_ref, residual_ref, stat_ref, mask_ref, vec_ref, own_ref, other_ref, *refs):
    shared = Gathered(at, refs[0:8])
    out_ref, direct_ref, taps_ref, back_ref, vec_grad_ref, keep_ref, send_ref = refs[8:15]
    in_nat, out_nat = refs[15:17]
    place_attention(shared, in_nat, out_nat)
    attention_body(
        at, hidden_ref, residual_ref, stat_ref, mask_ref, vec_ref, own_ref, other_ref,
        out_ref, direct_ref, taps_ref, back_ref, vec_grad_ref, *refs[15:],
    )
    for chip in range(8):
        for target, core in ((keep_ref, at[1]), (send_ref, 1 - at[1])):
            rows = unit_rows(24, chip, core)
            block = jnp.concatenate(
                [in_nat[rows, 256 * index : 256 * index + 256] for index in range(3)], axis=0
            )
            target[chip, 0:80, :] = pad_rows(block[:, 0:128], 80).astype(bf16)
            target[chip, 80:128, :] = pad_rows(pair_rows(block[:, 128:256], 40), 48).astype(bf16)
            block = out_nat[rows, 0:256]
            target[chip, 128:160, :] = pad_rows(block[:, 0:128], 32).astype(bf16)
            target[chip, 160:176, :] = pair_rows(block[:, 128:256], 16).astype(bf16)


def attention_plain(
    at, hidden_ref, residual_ref, stat_ref, mask_ref, vec_ref, own_ref, other_ref,
    in_given, out_given, out_ref, direct_ref, taps_ref, back_ref, vec_grad_ref,
    in_term_ref, out_term_ref, *refs,
):
    in_nat, out_nat = refs[0:2]
    in_nat[...] = in_given[...].astype(f32)
    out_nat[...] = out_given[...].astype(f32)
    attention_body(
        at, hidden_ref, residual_ref, stat_ref, mask_ref, vec_ref, own_ref, other_ref,
        out_ref, direct_ref, taps_ref, back_ref, vec_grad_ref, *refs,
    )
    in_term_ref[...] = in_nat[:, 0:768]
    out_term_ref[...] = out_nat[:, 0:256]


def pack_units(terms_ref, at, keep_ref, send_ref):
    for chip in range(8):
        for target, core in ((keep_ref, at[1]), (send_ref, 1 - at[1])):
            rows = unit_rows(ROWS, chip, core)
            target[chip, 0:224, :] = pad_rows(terms_ref[rows, 0:128], 224).astype(bf16)
            target[chip, 224:336, :] = pair_rows(terms_ref[rows, 128:256], 112).astype(bf16)


def conv_terms(at, taps_ref, own_ref, keep_ref, send_ref, terms_ref):
    kernel_terms(taps_ref, own_ref, terms_ref)
    pack_units(terms_ref, at, keep_ref, send_ref)


def conv_terms_plain(at, taps_ref, own_ref, terms_ref):
    kernel_terms(taps_ref, own_ref, terms_ref)


def second_back(
    at, taps_ref, kernel_ref, one_ref, stat_ref, film_rows_ref, mask_ref, vec_ref, vec_in_ref,
    back_taps_ref, back_ref, vec_grad_ref, grad_ref, rows_ref,
):
    def done(start, count, acc):
        grad_ref[pl.ds(start, count), :] = acc

    convolve_back(taps_ref, kernel_ref, done)
    mean, inverse, tally = stat_ref[0:1, :], stat_ref[1:2, :], stat_ref[2:3, :]
    gain, shift = vec_ref[3:4, :], vec_ref[4:5, :]
    scale, offset = film_rows_ref[0:1, :], film_rows_ref[1:2, :]
    zero = jnp.zeros((8, C), f32)

    def gather(start, carry):
        plain, with_normed = carry
        valid = wide_mask(mask_ref, start, CHUNK)
        here = pl.ds(start, CHUNK)
        normed = (one_ref[here, :] - mean) * inverse
        value = grad_ref[here, :] * valid * slope((normed * gain + shift) * valid * scale + offset)
        grad_ref[here, :] = value
        return (plain + fold(value), with_normed + fold(value * normed))

    plain, with_normed = chunks(gather, (zero, zero))
    plain, with_normed = total(plain), total(with_normed)
    gain_grad, shift_grad = scale * with_normed, scale * plain
    first_mean = group_sum(gain * shift_grad) / tally
    second_mean = group_sum(gain * gain_grad) / tally
    joint = scale * gain

    def back(start, carry):
        valid = wide_mask(mask_ref, start, CHUNK)
        here = pl.ds(start, CHUNK)
        normed = (one_ref[here, :] - mean) * inverse
        value = (grad_ref[here, :] * joint - first_mean - normed * second_mean) * inverse * valid
        low = value.astype(bf16).astype(f32)
        rows_ref[pl.ds(start + 8, CHUNK), :] = low
        return carry + fold(low)

    bias = chunks(back, zero)
    write_taps(rows_ref, back_taps_ref)
    write_own(rows_ref, back_ref, at[0])
    vec_grad_ref[...] = vec_in_ref[...]
    vec_grad_ref[2:3, :] = total(bias)
    vec_grad_ref[3:4, :] = gain_grad
    vec_grad_ref[4:5, :] = shift_grad
    vec_grad_ref[11:12, :] = (gain * with_normed + shift * plain).astype(bf16).astype(f32)
    vec_grad_ref[12:13, :] = plain.astype(bf16).astype(f32)


def first_back(
    at, taps_ref, kernel_ref, turned_ref, stat_ref, direct_ref, mask_ref, vec_ref, vec_in_ref,
    out_ref, vec_grad_ref, grad_ref, turn_ref,
):
    def done(start, count, acc):
        grad_ref[pl.ds(start, count), :] = acc

    convolve_back(taps_ref, kernel_ref, done)
    mean, inverse, tally = stat_ref[0:1, :], stat_ref[1:2, :], stat_ref[2:3, :]
    gain, shift = vec_ref[0:1, :], vec_ref[1:2, :]
    zero = jnp.zeros((8, C), f32)

    def gather(start, carry):
        plain, with_normed = carry
        valid = wide_mask(mask_ref, start, CHUNK)
        here = pl.ds(start, CHUNK)
        normed = (turned_ref[here, :].astype(f32) - mean) * inverse
        value = grad_ref[here, :] * slope((normed * gain + shift) * valid) * valid
        grad_ref[here, :] = value
        return (plain + fold(value), with_normed + fold(value * normed))

    plain, with_normed = chunks(gather, (zero, zero))
    shift_grad, gain_grad = total(plain), total(with_normed)
    first_mean = group_sum(gain * shift_grad) / tally
    second_mean = group_sum(gain * gain_grad) / tally
    for index in range(PIX // 128):
        here = slice(128 * index, 128 * index + 128)
        valid = wide_mask(mask_ref, 128 * index, 128)
        normed = (turned_ref[here, :].astype(f32) - mean) * inverse
        value = (grad_ref[here, :] * gain - first_mean - normed * second_mean) * inverse * valid
        turn_ref[:, here] = (value + direct_ref[here, :]).T
    out_ref[...] = turn_ref[pl.ds(aligned(at[0] * HALF, 16), HALF), :].astype(bf16)
    vec_grad_ref[...] = vec_in_ref[...]
    vec_grad_ref[0:1, :] = gain_grad
    vec_grad_ref[1:2, :] = shift_grad


def add_cores(at, keep_ref, back_ref, own_ref, across_ref):
    for depth in range(4):
        for target, side in ((own_ref, at[2]), (across_ref, 1 - at[2])):
            chip = depth * 2 + side
            target[depth] = (keep_ref[chip].astype(f32) + back_ref[chip].astype(f32)).astype(bf16)


def add_sides(at, own_ref, back_ref, mine_ref, *across):
    for step, target in enumerate((mine_ref,) + across):
        depth = at[3] ^ step
        target[...] = (own_ref[depth].astype(f32) + back_ref[depth].astype(f32)).astype(bf16)


def adam_update(weight, gradient, moment, square, step_rate):
    moment_new = beta_one * moment + (1.0 - beta_one) * gradient
    square_new = beta_two * square + (1.0 - beta_two) * gradient * gradient
    ratio = (
        moment_new
        / (1.0 - beta_one**STEP)
        / (jnp.sqrt(square_new / (1.0 - beta_two**STEP)) + adam_eps)
    )
    return (weight - step_rate * (ratio + decay_rate * weight), moment_new, square_new)


def unpair_rows(block, rows):
    top = block.shape[0]
    return jnp.concatenate((block, pltpu.roll(block, 64, 1)[0 : rows - top]), axis=0)


def conv_adam(parts, weight_ref, moment_ref, square_ref, outs, rate):
    def summed(start, stop):
        return sum(part[start:stop, :].astype(f32) for part in parts[1:]) + parts[0][
            start:stop, :
        ].astype(f32)

    low = summed(0, 224)[0:ROWS]
    high = unpair_rows(summed(224, 336), ROWS)
    for columns, gradient in ((slice(0, 128), low), (slice(128, 192), high[:, 0:64])):
        results = adam_update(
            weight_ref[:, columns], gradient, moment_ref[:, columns], square_ref[:, columns], rate
        )
        for out, value in zip(outs, (gradient,) + results):
            out[:, columns] = value
    return summed


def finish_first(at, *refs):
    conv_adam(refs[0:4], *refs[4:7], refs[7:11], step_rates()[0])


def finish_second(at, *refs):
    summed = conv_adam(refs[0:4], *refs[4:7], refs[7:11], step_rates()[1])
    in_ref, out_ref = refs[11:]
    low = summed(336, 416)[0:72]
    high = unpair_rows(summed(416, 464)[0:40], 72)
    for index in range(3):
        part = slice(24 * index, 24 * index + 24)
        in_ref[index, :, 0:128] = low[part]
        in_ref[index, :, 128:192] = high[part, 0:64]
    out_ref[:, 0:128] = summed(464, 496)[0:24]
    out_ref[:, 128:192] = unpair_rows(summed(496, 512), 24)[:, 0:64]


def gather_units(unit, cut, wide):
    core_swap = [(i, i ^ 1) for i in range(wide)]
    side_swap = [(i, i ^ 2) for i in range(wide)]
    flip = [(0, 1), (1, 0)]
    column = [unit] + [
        lax.ppermute(unit, "wide", [(i, i ^ (4 * step)) for i in range(wide)])
        for step in (1, 2, 3)
    ]
    one = jnp.stack([part[:cut] for part in column])
    two = jnp.stack([part[cut:] for part in column])
    side_one, side_two = (lax.ppermute(v, "wide", side_swap) for v in (one, two))
    over_one, over_two = (lax.ppermute(v, "narrow", flip) for v in (one, two))
    far_one = lax.ppermute(over_one, "wide", side_swap)
    far_two = lax.ppermute(side_two, "narrow", flip)
    ones = [one, side_one, over_one, far_one]
    twos = [two, side_two, over_two, far_two]
    ones = ones + [lax.ppermute(v, "wide", core_swap) for v in ones]
    twos = twos + [lax.ppermute(v, "wide", core_swap) for v in twos]
    return ones, twos


def reduce_units(keep, send, scalars, wide):
    rows = keep.shape[1]
    back = lax.ppermute(send, "wide", [(i, i ^ 1) for i in range(wide)])
    four = shaped((4, rows, 128), bf16)
    one = shaped((rows, 128), bf16)
    own, across = call(add_cores, (four, four), (keep, back), scalars)
    back = lax.ppermute(across, "wide", [(i, i ^ 2) for i in range(wide)])
    parts = call(add_sides, (one,) * 4, (own, back), scalars)
    return [parts[0]] + [
        lax.ppermute(parts[step], "wide", [(i, i ^ (4 * step)) for i in range(wide)])
        for step in (1, 2, 3)
    ]


def sum_vectors(terms, wide):
    for step in (1, 2, 4, 8):
        terms = terms + lax.ppermute(terms, "wide", [(i, i ^ step) for i in range(wide)])
    return terms


def per_device(
    features,
    embedding,
    valid_mask,
    cotangent,
    conv_first,
    conv_first_moment,
    conv_first_square,
    conv_second,
    conv_second_moment,
    conv_second_square,
    film_weight,
    film_weight_moment,
    film_weight_square,
    attend_in,
    attend_in_moment,
    attend_in_square,
    attend_out,
    attend_out_moment,
    attend_out_square,
    vectors,
    vectors_moment,
    vectors_square,
):
    wide = lax.axis_size("wide")
    unit_path = wide == 16
    narrow_at = lax.axis_index("narrow").astype(jnp.int32)
    wide_at = lax.axis_index("wide").astype(jnp.int32)
    scalars = jnp.stack((narrow_at, wide_at & 1, (wide_at >> 1) & 1, wide_at >> 2))
    flip = [(0, 1), (1, 0)]
    plane = shaped((PIX, C), f32)
    low_plane = shaped((PIX, C), bf16)
    taps = shaped((PADDED, 3 * C), bf16)
    back_half = shaped((PADDED, 256), bf16)
    kernel = shaped((9 * C, C), bf16)
    stats = shaped((8, C), f32)
    vec_rows = shaped((16, C), f32)
    half_plane = shaped((HALF, PIX), bf16)
    rows_scratch = pltpu.VMEM((PIX + 16, C), f32)

    vec_half = jnp.pad(vectors, ((0, 3), (0, 0)))
    vec_other = lax.ppermute(vec_half, "narrow", flip)
    vecs = jnp.where(
        narrow_at == 0,
        jnp.concatenate((vec_half, vec_other), axis=1),
        jnp.concatenate((vec_other, vec_half), axis=1),
    )
    mask = jnp.broadcast_to(valid_mask[0].astype(f32)[:, None], (PIX, 128))
    own_features = features[0]
    own_cotangent = cotangent[0]
    other_features = lax.ppermute(own_features, "narrow", flip)

    if unit_path:
        (unit_first,) = call(
            pack_first, (shaped((336, 128), bf16),), (conv_first,), scalars
        )
        first_ones, first_twos = gather_units(unit_first, 224, wide)
        (unit_second,) = call(
            pack_second,
            (shaped((SHARED_AT + SECOND_ROWS, 128), bf16),),
            (
                conv_second,
                jnp.transpose(film_weight, (1, 0, 2)),
                jnp.transpose(attend_in, (1, 0, 2)),
                attend_out,
            ),
            scalars,
        )
        second_ones, second_twos = gather_units(unit_second, SHARED_AT, wide)
    else:

        def whole(array, axis):
            array = lax.all_gather(array.astype(bf16), "wide", axis=0, tiled=True)
            return lax.all_gather(array, "narrow", axis=axis, tiled=True)

        first_full, second_full = whole(conv_first, 1), whole(conv_second, 1)
        film_full = whole(film_weight, 2).reshape(EMB, 2 * C)
        in_full = whole(attend_in, 2).reshape(C, 3 * C)
        out_full = whole(attend_out, 1)
    other_cotangent = lax.ppermute(own_cotangent, "narrow", flip)

    turned, taps_one, stat_one = call(
        first_norm,
        (low_plane, taps, stats),
        (own_features, other_features, mask, vecs),
        scalars,
        (rows_scratch, pltpu.VMEM((PIX, C), f32)),
    )
    if unit_path:
        out_one, kernel_one, stat_two = call(
            first_conv,
            (plane, kernel, stats),
            (taps_one, mask, vecs, *first_ones, *first_twos),
            scalars,
            flops=2 * 9 * C * C * PIX,
        )
    else:
        kernel_one = first_full
        out_one, stat_two = call(
            first_conv_plain, (plane, stats), (taps_one, mask, vecs, kernel_one), scalars
        )
    common = (out_one, stat_two, turned, mask, vecs, embedding)
    scratch = (pltpu.VMEM((16, EMB), f32), rows_scratch)
    if unit_path:
        taps_two, residual, hidden, stat_three, film_rows, kernel_two = call(
            second_conv,
            (taps, plane, low_plane, stats, stats, kernel),
            common + (*second_ones, *second_twos),
            scalars,
            scratch + (pltpu.VMEM((EMB, 2 * C), bf16),),
            flops=2 * 9 * C * C * PIX,
        )
    else:
        kernel_two = second_full
        taps_two, residual, hidden, stat_three, film_rows = call(
            second_conv_plain,
            (taps, plane, low_plane, stats, stats),
            common + (kernel_two, film_full),
            scalars,
            scratch,
        )
    common = (hidden, residual, stat_three, mask, vecs, own_cotangent, other_cotangent)
    padded = pltpu.VMEM((PIX, 512), bf16)
    scratch = (
        pltpu.VMEM((C, 3 * C), f32),
        pltpu.VMEM((C, C), f32),
        pltpu.VMEM((C, 1536), bf16),
        pltpu.VMEM((512, C), bf16),
        *([padded] * 8),
        pltpu.VMEM((PIX, 128), f32),
        pltpu.VMEM((PIX, 128), f32),
        pltpu.VMEM((PIX, C), bf16),
        rows_scratch,
        pltpu.VMEM((C, PIX), f32),
        pltpu.VMEM((PIX, 256), bf16),
    )
    flops = 2 * HEADS * PIX * PIX * 128 * 6
    if unit_path:
        units = shaped((8, 176, 128), bf16)
        output, direct, taps_back, back_two, vec_grad, keep_att, send_att = call(
            attention,
            (half_plane, plane, taps, back_half, vec_rows, units, units),
            common + tuple(second_twos),
            scalars,
            scratch,
            flops=flops,
        )
        units = shaped((8, 336, 128), bf16)
        keep, send = call(
            conv_terms,
            (units, units),
            (taps_two, back_two),
            scalars,
            (pltpu.VMEM((9 * C, 256), f32),),
            flops=2 * 9 * C * 256 * PIX,
        )
        parts_second = reduce_units(
            jnp.concatenate((keep, keep_att), axis=1),
            jnp.concatenate((send, send_att), axis=1),
            scalars,
            wide,
        )
    else:
        output, direct, taps_back, back_two, vec_grad, in_term, out_term = call(
            attention_plain,
            (
                half_plane, plane, taps, back_half, vec_rows,
                shaped((C, 768), f32), shaped((C, 256), f32),
            ),
            common + (in_full, out_full),
            scalars,
            scratch,
        )
        (second_term,) = call(
            conv_terms_plain, (shaped((9 * C, 256), f32),), (taps_two, back_two), scalars
        )
    taps_back_one, back_one, vec_grad = call(
        second_back,
        (taps, back_half, vec_rows),
        (taps_back, kernel_two, out_one, stat_two, film_rows, mask, vecs, vec_grad),
        scalars,
        (pltpu.VMEM((PIX, C), f32), rows_scratch),
        flops=2 * 9 * C * C * PIX,
    )
    if unit_path:
        units = shaped((8, 336, 128), bf16)
        keep, send = call(
            conv_terms,
            (units, units),
            (taps_one, back_one),
            scalars,
            (pltpu.VMEM((9 * C, 256), f32),),
            flops=2 * 9 * C * 256 * PIX,
        )
        parts_first = reduce_units(keep, send, scalars, wide)
    else:
        (first_term,) = call(
            conv_terms_plain, (shaped((9 * C, 256), f32),), (taps_one, back_one), scalars
        )
    soft = jax.nn.silu(embedding.astype(f32)).astype(bf16)
    soft_all = lax.all_gather(soft, "wide", axis=0, tiled=True)
    rows_here = film_weight.shape[0]
    soft_here = lax.dynamic_slice_in_dim(soft_all, wide_at * rows_here, rows_here, axis=1)
    film_term = lax.dynamic_slice_in_dim(vec_grad[11:13], narrow_at * HALF, HALF, axis=1)
    film_all = lax.all_gather(film_term.astype(bf16)[None], "wide", axis=0, tiled=True)
    film_gradient = jnp.einsum("se,stj->etj", soft_here, film_all, preferred_element_type=f32)

    input_gradient, vec_grad = call(
        first_back,
        (half_plane, vec_rows),
        (taps_back_one, kernel_one, turned, stat_one, direct, mask, vecs, vec_grad),
        scalars,
        (pltpu.VMEM((PIX, C), f32), pltpu.VMEM((C, PIX), f32)),
        flops=2 * 9 * C * C * PIX,
    )
    vec_half = lax.dynamic_slice_in_dim(vec_grad, narrow_at * HALF, HALF, axis=1)
    if unit_path:
        vec_sum = sum_vectors(vec_half, wide)[:13]
    else:
        vec_sum = lax.psum(vec_half, "wide")[:13]

    rates = step_rates()
    shard = shaped(conv_first.shape, f32)
    if unit_path:
        second_results = call(
            finish_second,
            (shard,) * 4 + (shaped((3, 24, HALF), f32), shaped((24, HALF), f32)),
            (*parts_second, conv_second, conv_second_moment, conv_second_square),
            scalars,
        )
        in_gradient = jnp.transpose(second_results[4], (1, 0, 2))
        out_gradient = second_results[5]
        second_results = second_results[:4]
        first_results = call(
            finish_first,
            (shard,) * 4,
            (*parts_first, conv_first, conv_first_moment, conv_first_square),
            scalars,
        )
    else:

        def scatter(term):
            return lax.psum_scatter(term, "wide", scatter_dimension=0, tiled=True)

        first_gradient = scatter(first_term[:, :HALF])
        second_gradient = scatter(second_term[:, :HALF])
        in_gradient = scatter(in_term.reshape(C, 3, 256)[:, :, :HALF])
        out_gradient = scatter(out_term[:, :HALF])
        first_results = (first_gradient,) + adam_update(
            conv_first, first_gradient, conv_first_moment, conv_first_square, rates[0]
        )
        second_results = (second_gradient,) + adam_update(
            conv_second, second_gradient, conv_second_moment, conv_second_square, rates[1]
        )

    def finish(weight, gradient, moment, square, rate):
        return (gradient,) + adam_update(weight, gradient, moment, square, rate)

    return (
        output[None],
        input_gradient[None],
        *first_results,
        *second_results,
        *finish(film_weight, film_gradient, film_weight_moment, film_weight_square, rates[2]),
        *finish(attend_in, in_gradient, attend_in_moment, attend_in_square, rates[3]),
        *finish(attend_out, out_gradient, attend_out_moment, attend_out_square, rates[4]),
        *finish(vectors, vec_sum, vectors_moment, vectors_square, rates[5]),
    )


def solution(mesh):
    in_specs = (
        P("wide", "narrow", None),
        P("wide", None),
        P("wide", None),
        P("wide", "narrow", None),
        P("wide", "narrow"),
        P("wide", "narrow"),
        P("wide", "narrow"),
        P("wide", "narrow"),
        P("wide", "narrow"),
        P("wide", "narrow"),
        P("wide", None, "narrow"),
        P("wide", None, "narrow"),
        P("wide", None, "narrow"),
        P("wide", None, "narrow"),
        P("wide", None, "narrow"),
        P("wide", None, "narrow"),
        P("wide", "narrow"),
        P("wide", "narrow"),
        P("wide", "narrow"),
        P(None, "narrow"),
        P(None, "narrow"),
        P(None, "narrow"),
    )
    out_specs = (
        P("wide", "narrow", None),
        P("wide", "narrow", None),
        P("wide", "narrow"),
        P("wide", "narrow"),
        P("wide", "narrow"),
        P("wide", "narrow"),
        P("wide", "narrow"),
        P("wide", "narrow"),
        P("wide", "narrow"),
        P("wide", "narrow"),
        P("wide", None, "narrow"),
        P("wide", None, "narrow"),
        P("wide", None, "narrow"),
        P("wide", None, "narrow"),
        P("wide", None, "narrow"),
        P("wide", None, "narrow"),
        P("wide", None, "narrow"),
        P("wide", None, "narrow"),
        P("wide", "narrow"),
        P("wide", "narrow"),
        P("wide", "narrow"),
        P("wide", "narrow"),
        P(None, "narrow"),
        P(None, "narrow"),
        P(None, "narrow"),
        P(None, "narrow"),
    )
    return jax.shard_map(
        per_device, mesh=mesh, in_specs=in_specs, out_specs=out_specs, check_vma=False
    )
```

time: 675 us -> 306 us (0.45)
  the two profiles are of different devices: /device:TPU:0 before, /device:TPU:21 now
where the time goes in v1:
time: 306 us; the launch traced here: 301 us
  Pallas kernels  119 us (39%)
  waiting for transfers between devices  51.1 us (17%)
  starting transfers between devices  48.9 us (16%)
  local copies, waits for them, and re-layouts  40.3 us (13%)
  blocking collectives  34 us (11%)
  other arithmetic  6.63 us (2%)
    pallas_call x16, Pallas kernels, call(): pl.pallas_call(body, out_shape=tuple(outs), in_specs=[pl.BlockSpec(memory...  119 us
    unnamed x144, local copies, waits for them, and re-layouts  34.3 us
    all_gather x1, blocking collectives, per_device(): lax.all_gather(film_term.astype(bf16)[None], 'wide', axis=0, tiled=True)  18.1 us
    all_gather x1, blocking collectives, per_device(): soft_all = lax.all_gather(soft, 'wide', axis=0, tiled=True)  15.9 us
    ppermute x8, starting transfers between devices, gather_units(): twos = twos + [lax.ppermute(v, 'wide', core_swap) for v in twos]  12.7 us
    ppermute x4, waiting for transfers between devices, sum_vectors(): lax.ppermute(terms, 'wide', [(i, i ^ step) for i in range(wide)])  10.5 us
    ppermute x2, waiting for transfers between devices, gather_units(): far_two = lax.ppermute(side_two, 'narrow', flip)  9.67 us
    ppermute x4, starting transfers between devices, sum_vectors(): lax.ppermute(terms, 'wide', [(i, i ^ step) for i in range(wide)])  9.04 us
  transfers between devices with their start and end apart: 51, of which 13 were waited for; matrix products, arithmetic and copies ran while one was open for 8% of the time, Pallas kernels for 25%

profile of v1, /device:TPU:21, one launch (start us, length us, event | category | flops | bytes accessed | tf_op | source)
XLA Modules:
  0.0 301.4 jit_solution(11809649954551565228)
XLA Ops:
  21.2 4.2 %collective-permute-done.21 = bf16[656,128]{1,0:T(8,128)(2,1)S(1)} collective-permute-done((bf16[656,128]{1,0:T(8,128)(2,1)}, bf16[656,128]{1,0:T(8,128)(2,1)S(1)}, u32[]{:S(2)}, u32[]{:S(2)}) %collective-permute-start.21) | collective-permute-done | bytes 167968 | tf_op jit(solution)/shard_map/ppermute | solution.py:885
  27.8 2.5 collective-permute-start.15
  33.1 3.5 %collective-permute-start.16 = (bf16[4,112,128]{2,1,0:T(8,128)(2,1)S(1)}, bf16[4,112,128]{2,1,0:T(8,128)(2,1)S(1)}, u32[]{:S(2)}, u32[]{:S(2)}) collective-permute-start(bf16[4,112,128]{2,1,0:T(8,128)(2,1)S(1)} %collective-permute-done.12.refs_9_), channel_id=1, source_target_pairs={{0,2},{2,0},{4,6},{6,4},{8,10},{10,8},{12,14},{14,12},{16,18},{18,... | collective-permute-start | bytes 344072 | tf_op jit(solution)/shard_map/ppermute | solution.py:897
  38.8 9.7 %collective-permute-done.14.refs_11_ = bf16[4,112,128]{2,1,0:T(8,128)(2,1)S(1)} collective-permute-done((bf16[4,112,128]{2,1,0:T(8,128)(2,1)S(1)}, bf16[4,112,128]{2,1,0:T(8,128)(2,1)S(1)}, u32[]{:S(2)}, u32[]{:S(2)}) %collective-permute-start.14) | collective-permute-done | bytes 114720 | tf_op jit(solution)/shard_map/ppermute | solution.py:893
  54.2 2.8 collective-permute-done.23.refs_2_
  57.0 3.0 collective-permute-start.32
  62.0 5.6 %collective-permute-done.29.refs_9_.refs_1_ = bf16[4,336,128]{2,1,0:T(8,128)(2,1)S(1)} collective-permute-done((bf16[4,336,128]{2,1,0:T(8,128)(2,1)S(1)}, bf16[4,336,128]{2,1,0:T(8,128)(2,1)S(1)}, u32[]{:S(2)}, u32[]{:S(2)}) %collective-permute-start.29) | collective-permute-done | bytes 344096 | tf_op jit(solution)/shard_map/ppermute | solution.py:890
  69.4 3.2 %collective-permute-done.7.refs_3_ = bf16[4,224,128]{2,1,0:T(8,128)(2,1)} collective-permute-done((bf16[4,224,128]{2,1,0:T(8,128)(2,1)S(1)}, bf16[4,224,128]{2,1,0:T(8,128)(2,1)}, u32[]{:S(2)}, u32[]{:S(2)}) %collective-permute-start.7) | collective-permute-done | bytes 229408 | tf_op jit(solution)/shard_map/ppermute | solution.py:892
  76.1 3.5 %collective-permute-done.24.refs_3_ = bf16[4,320,128]{2,1,0:T(8,128)(2,1)} collective-permute-done((bf16[4,320,128]{2,1,0:T(8,128)(2,1)}, bf16[4,320,128]{2,1,0:T(8,128)(2,1)}, u32[]{:S(2)}, u32[]{:S(2)}) %collective-permute-start.24) | collective-permute-done | bytes 327712 | tf_op jit(solution)/shard_map/ppermute | solution.py:892
  82.6 5.6 %shard_map.413 = (bf16[1024,384]{1,0:T(8,128)(2,1)}, bf16[1088,1152]{1,0:T(8,128)(2,1)}, f32[8,384]{1,0:T(8,128)}) custom-call(s32[4]{0:T(128)} %pad_add_fusion.at, bf16[192,1024]{1,0:T(8,128)(2,1)} %bitcast.57, bf16[192,1024]{1,0:T(8,128)(2,1)} %copy-done.5, f32[1024,128]{1,0:T(8,128)} %broadcast_in_dim.15.mask_ref, f32[16,384]{1,0:T(8,128)} %maximum_select_fusion.vec_ref), custom_call_target="tpu_custom_call" | custom-call | bytes 4640768 | tf_op jit(solution)/shard_map/pallas_call | solution.py:54
  88.7 11.0 %shard_map.415 = (f32[1024,384]{1,0:T(8,128)}, bf16[3456,384]{1,0:T(8,128)(2,1)}, f32[8,384]{1,0:T(8,128)}) custom-call(s32[4]{0:T(128)} %pad_add_fusion.at, bf16[1088,1152]{1,0:T(8,128)(2,1)} %get-tuple-element.76.taps_ref, f32[1024,128]{1,0:T(8,128)} %broadcast_in_dim.15.mask_ref, f32[16,384]{1,0:T(8,128)} %maximum_select_fusion.vec_ref, ...), custom_call_target="tpu_custom_call" | custom-call | flops 2717908992 | bytes 10047488 | tf_op jit(solution)/shard_map/pallas_call | solution.py:54
  100.8 14.8 %shard_map.417 = (bf16[1088,1152]{1,0:T(8,128)(2,1)}, f32[1024,384]{1,0:T(8,128)}, bf16[1024,384]{1,0:T(8,128)(2,1)}, f32[8,384]{1,0:T(8,128)}, f32[8,384]{1,0:T(8,128)}, /*index=5*/bf16[3456,384]{1,0:T(8,128)(2,1)}) custom-call(s32[4]{0:T(128)} %pad_add_fusion.at, f32[1024,384]{1,0:T(8,128)} %get-tuple-element.77.one_ref, ...), custom_call_target="tpu_custom_call" | custom-call | flops 2717908992 | bytes 15840768 | tf_op jit(solution)/shard_map/pallas_call | solution.py:54
  116.4 35.0 %shard_map.418 = (bf16[192,1024]{1,0:T(8,128)(2,1)}, f32[1024,384]{1,0:T(8,128)}, bf16[1088,1152]{1,0:T(8,128)(2,1)}, bf16[1088,256]{1,0:T(8,128)(2,1)}, f32[16,...) custom-call(s32[4]{0:T(128)} %pad_add_fusion.at, ...), custom_call_target="tpu_custom_call" | custom-call | flops 6442450944 | bytes 12234752 | tf_op jit(solution)/shard_map/pallas_call | solution.py:54
  151.4 5.3 %shard_map.425 = (bf16[8,336,128]{2,1,0:T(8,128)(2,1)}, bf16[8,336,128]{2,1,0:T(8,128)(2,1)}) custom-call(s32[4]{0:T(128)} %pad_add_fusion.at, bf16[1088,1152]{1,0:T(8,128)(2,1)} %get-tuple-element.107.taps_ref, bf16[1088,256]{1,0:T(8,128)(2,1)} %get-tuple-element.108.own_ref), custom_call_target="tpu_custom_call" | custom-call | flops 1811939328 | bytes 4440064 | tf_op jit(solution)/shard_map/pallas_call | solution.py:54
  158.3 12.6 %shard_map.419 = (bf16[1088,1152]{1,0:T(8,128)(2,1)}, bf16[1088,256]{1,0:T(8,128)(2,1)}, f32[16,384]{1,0:T(8,128)}) custom-call(s32[4]{0:T(128)} %pad_add_fusion.at, bf16[1088,1152]{1,0:T(8,128)(2,1)} %get-tuple-element.84.taps_ref, bf16[3456,384]{1,0:T(8,128)(2,1)} %get-tuple-element.85.kernel_ref, f32[1024,384]{1,0:T(8,128)} %get-tuple-element.77.one_ref, ...), custom_call_target="tpu_custom_call" | custom-call | flops 2717908992 | bytes 10420224 | tf_op jit(solution)/shard_map/pallas_call | solution.py:54
  170.9 5.2 %shard_map.421 = (bf16[8,336,128]{2,1,0:T(8,128)(2,1)}, bf16[8,336,128]{2,1,0:T(8,128)(2,1)}) custom-call(s32[4]{0:T(128)} %pad_add_fusion.at, bf16[1088,1152]{1,0:T(8,128)(2,1)} %get-tuple-element.76.taps_ref, bf16[1088,256]{1,0:T(8,128)(2,1)} %get-tuple-element.94.own_ref), custom_call_target="tpu_custom_call" | custom-call | flops 1811939328 | bytes 4440064 | tf_op jit(solution)/shard_map/pallas_call | solution.py:54
  176.3 15.9 %all-gather.1 = bf16[16,1,768]{2,1,0:T(2,128)(2,1)S(1)} all-gather(bf16[1,1,768]{2,1,0:T(2,128)(2,1)S(1)} %convert_bitcast_fusion), channel_id=1, replica_groups=mesh['wide'=16,'narrow'=2] {'wide'}, dimensions={0}, use_global_device_ids=true | all-gather | bytes 26112 | tf_op jit(solution)/shard_map/all_gather | solution.py:1121
  192.2 11.4 %shard_map.420 = (bf16[192,1024]{1,0:T(8,128)(2,1)}, f32[16,384]{1,0:T(8,128)}) custom-call(s32[4]{0:T(128)} %pad_add_fusion.at, bf16[1088,1152]{1,0:T(8,128)(2,1)} %get-tuple-element.88.taps_ref, bf16[3456,384]{1,0:T(8,128)(2,1)} %get-tuple-element.89.kernel_ref, bf16[1024,384]{1,0:T(8,128)(2,1)} %get-tuple-element.79.turned_ref, ...), custom_call_target="tpu_custom_call" | custom-call | flops 2717908992 | bytes 8523776 | tf_op jit(solution)/shard_map/pallas_call | solution.py:54
  211.7 2.7 shard_map.426
  220.1 10.5 %collective-permute-done.48 = f32[16,192]{1,0:T(8,128)S(1)} collective-permute-done((f32[16,192]{1,0:T(8,128)S(1)}, f32[16,192]{1,0:T(8,128)S(1)}, u32[]{:S(2)}, u32[]{:S(2)}) %collective-permute-start.48) | collective-permute-done | bytes 12320 | tf_op jit(solution)/shard_map/ppermute | solution.py:917
  230.6 3.0 collective-permute-start.49
  233.6 18.1 %all-gather.2 = bf16[16,2,192]{2,1,0:T(2,128)(2,1)S(1)} all-gather(bf16[1,2,192]{2,1,0:T(2,128)(2,1)S(1)} %fusion.7), channel_id=2, replica_groups=mesh['wide'=16,'narrow'=2] {'wide'}, dimensions={0}, use_global_device_ids=true | all-gather | bytes 13056 | tf_op jit(solution)/shard_map/all_gather | solution.py:1125
  251.7 4.3 %collective-permute-start.50 = (f32[16,192]{1,0:T(8,128)S(1)}, f32[16,192]{1,0:T(8,128)S(1)}, u32[]{:S(2)}, u32[]{:S(2)}) collective-permute-start(f32[16,192]{1,0:T(8,128)S(1)} %add.105), channel_id=1, source_target_pairs={{0,16},{2,18},{4,20},{6,22},{8,24},{10,26},{12,28},{14,30},{16,0},... | collective-permute-start | bytes 36872 | tf_op jit(solution)/shard_map/ppermute | solution.py:917
  270.5 7.9 %collective-permute-done.41.refs_3_ = bf16[336,128]{1,0:T(8,128)(2,1)S(1)} collective-permute-done((bf16[336,128]{1,0:T(8,128)(2,1)}, bf16[336,128]{1,0:T(8,128)(2,1)S(1)}, u32[]{:S(2)}, u32[]{:S(2)}) %collective-permute-start.41) | collective-permute-done | bytes 86048 | tf_op jit(solution)/shard_map/ppermute | solution.py:910
  (278 shorter events, 98.5 us)
Async XLA Ops:
  4.7 16.0 %collective-permute-start.2 = (bf16[336,128]{1,0:T(8,128)(2,1)}, bf16[336,128]{1,0:T(8,128)(2,1)S(1)}, u32[]{:S(2)}, u32[]{:S(2)}) collective-permute-start(bf16[336,128]{1,0:T(8,128)(2,1)} %shard_map.414), channel_id=1, source_target_pairs={{0,8},{2,10},{4,12},{6,14},{8,0},{10,2},{12,4},{14,6},{16,24},{18,... | collective-permute-start | bytes 258056 | tf_op jit(solution)/shard_map/ppermute | solution.py:885
  30.7 22.4 %collective-permute-start = (bf16[192,1024]{1,0:T(8,128)(2,1)S(1)}, bf16[192,1024]{1,0:T(8,128)(2,1)S(1)}, u32[]{:S(2)}, u32[]{:S(2)}) collective-permute-start(bf16[192,1024]{1,0:T(8,128)(2,1)S(1)} %bitcast.58), channel_id=1, source_target_pairs={{0,1},{1,0},{2,3},{3,2},{4,5},{5,4},{6,7},{7,6},{8,9},{9,8},{10,11... | collective-permute-start | bytes 1179656 | tf_op jit(solution)/shard_map/ppermute | solution.py:971
  32.0 18.9 %collective-permute-start.5 = (bf16[4,224,128]{2,1,0:T(8,128)(2,1)S(1)}, bf16[4,224,128]{2,1,0:T(8,128)(2,1)S(1)}, u32[]{:S(2)}, u32[]{:S(2)}) collective-permute-start(bf16[4,224,128]{2,1,0:T(8,128)(2,1)S(1)} %pad_maximum_fusion.4.refs_0_), channel_id=1, source_target_pairs={{0,4},{2,6},{4,0},{6,2},{8,12},{10,14},{12,8},{14,10},{16,20},{18,... | collective-permute-start | bytes 688136 | tf_op jit(solution)/shard_map/ppermute | solution.py:890
  32.2 16.3 %collective-permute-start.14 = (bf16[4,112,128]{2,1,0:T(8,128)(2,1)S(1)}, bf16[4,112,128]{2,1,0:T(8,128)(2,1)S(1)}, u32[]{:S(2)}, u32[]{:S(2)}) collective-permute-start(bf16[4,112,128]{2,1,0:T(8,128)(2,1)S(1)} %collective-permute-done.12.refs_9_), channel_id=1, source_target_pairs={{0,1},{1,0},{2,3},{3,2},{4,5},{5,4},{6,7},{7,6},{8,9},{9,8},{10,11... | collective-permute-start | bytes 344072 | tf_op jit(solution)/shard_map/ppermute | solution.py:893
  33.1 16.1 %collective-permute-start.16 = (bf16[4,112,128]{2,1,0:T(8,128)(2,1)S(1)}, bf16[4,112,128]{2,1,0:T(8,128)(2,1)S(1)}, u32[]{:S(2)}, u32[]{:S(2)}) collective-permute-start(bf16[4,112,128]{2,1,0:T(8,128)(2,1)S(1)} %collective-permute-done.12.refs_9_), channel_id=1, source_target_pairs={{0,2},{2,0},{4,6},{6,4},{8,10},{10,8},{12,14},{14,12},{16,18},{18,... | collective-permute-start | bytes 344072 | tf_op jit(solution)/shard_map/ppermute | solution.py:897
  37.6 14.8 %collective-permute-start.8 = (bf16[4,224,128]{2,1,0:T(8,128)(2,1)S(1)}, bf16[4,224,128]{2,1,0:T(8,128)(2,1)S(1)}, u32[]{:S(2)}, u32[]{:S(2)}) collective-permute-start(bf16[4,224,128]{2,1,0:T(8,128)(2,1)S(1)} %pad_maximum_fusion.4.refs_0_), channel_id=1, source_target_pairs={{0,2},{2,0},{4,6},{6,4},{8,10},{10,8},{12,14},{14,12},{16,18},{18,... | collective-permute-start | bytes 688136 | tf_op jit(solution)/shard_map/ppermute | solution.py:896
  52.4 15.2 %collective-permute-start.29 = (bf16[4,336,128]{2,1,0:T(8,128)(2,1)S(1)}, bf16[4,336,128]{2,1,0:T(8,128)(2,1)S(1)}, u32[]{:S(2)}, u32[]{:S(2)}) collective-permute-start(bf16[4,336,128]{2,1,0:T(8,128)(2,1)S(1)} %pad_maximum_fusion.2.refs_8_.refs_0_), channel_id=1, source_target_pairs={{0,4},{2,6},{4,0},{6,2},{8,12},{10,14},{12,8},{14,10},{16,20},{18,... | collective-permute-start | bytes 1032200 | tf_op jit(solution)/shard_map/ppermute | solution.py:890
  53.6 15.2 %collective-permute-start.30 = (bf16[4,336,128]{2,1,0:T(8,128)(2,1)S(1)}, bf16[4,336,128]{2,1,0:T(8,128)(2,1)S(1)}, u32[]{:S(2)}, u32[]{:S(2)}) collective-permute-start(bf16[4,336,128]{2,1,0:T(8,128)(2,1)S(1)} %pad_maximum_fusion.2.refs_8_.refs_0_), channel_id=1, source_target_pairs={{0,1},{1,0},{2,3},{3,2},{4,5},{5,4},{6,7},{7,6},{8,9},{9,8},{10,11... | collective-permute-start | bytes 1032200 | tf_op jit(solution)/shard_map/ppermute | solution.py:891
  75.7 24.0 %collective-permute-start.33 = (bf16[4,336,128]{2,1,0:T(8,128)(2,1)S(1)}, bf16[4,336,128]{2,1,0:T(8,128)(2,1)S(1)}, u32[]{:S(2)}, u32[]{:S(2)}) collective-permute-start(bf16[4,336,128]{2,1,0:T(8,128)(2,1)S(1)} %collective-permute-done.29.refs_9_.refs_1_), channel_id=1, source_target_pairs={{0,2},{2,0},{4,6},{6,4},{8,10},{10,8},{12,14},{14,12},{16,18},{18,... | collective-permute-start | bytes 1032200 | tf_op jit(solution)/shard_map/ppermute | solution.py:897
  79.6 20.1 %collective-permute-start.34 = (bf16[4,336,128]{2,1,0:T(8,128)(2,1)S(1)}, bf16[4,336,128]{2,1,0:T(8,128)(2,1)S(1)}, u32[]{:S(2)}, u32[]{:S(2)}) collective-permute-start(bf16[4,336,128]{2,1,0:T(8,128)(2,1)S(1)} %collective-permute-done.30.refs_10_.refs_2_), channel_id=1, source_target_pairs={{0,2},{2,0},{4,6},{6,4},{8,10},{10,8},{12,14},{14,12},{16,18},{18,... | collective-permute-start | bytes 1032200 | tf_op jit(solution)/shard_map/ppermute | solution.py:897
  80.4 19.4 %collective-permute-start.28 = (bf16[4,320,128]{2,1,0:T(8,128)(2,1)}, bf16[4,320,128]{2,1,0:T(8,128)(2,1)S(1)}, u32[]{:S(2)}, u32[]{:S(2)}) collective-permute-start(bf16[4,320,128]{2,1,0:T(8,128)(2,1)} %collective-permute-done.24.refs_3_), channel_id=1, source_target_pairs={{0,2},{2,0},{4,6},{6,4},{8,10},{10,8},{12,14},{14,12},{16,18},{18,... | collective-permute-start | bytes 983048 | tf_op jit(solution)/shard_map/ppermute | solution.py:896
  80.4 19.4 %collective-permute-start.35 = (bf16[4,336,128]{2,1,0:T(8,128)(2,1)S(1)}, bf16[4,336,128]{2,1,0:T(8,128)(2,1)S(1)}, u32[]{:S(2)}, u32[]{:S(2)}) collective-permute-start(bf16[4,336,128]{2,1,0:T(8,128)(2,1)S(1)} %collective-permute-done.31.refs_11_.refs_3_), channel_id=1, source_target_pairs={{0,2},{2,0},{4,6},{6,4},{8,10},{10,8},{12,14},{14,12},{16,18},{18,... | collective-permute-start | bytes 1032200 | tf_op jit(solution)/shard_map/ppermute | solution.py:897
  88.2 27.4 %collective-permute-start.36 = (bf16[192,1024]{1,0:T(8,128)(2,1)S(1)}, bf16[192,1024]{1,0:T(8,128)(2,1)S(1)}, u32[]{:S(2)}, u32[]{:S(2)}) collective-permute-start(bf16[192,1024]{1,0:T(8,128)(2,1)S(1)} %bitcast.64), channel_id=1, source_target_pairs={{0,1},{1,0},{2,3},{3,2},{4,5},{5,4},{6,7},{7,6},{8,9},{9,8},{10,11... | collective-permute-start | bytes 1179656 | tf_op jit(solution)/shard_map/ppermute | solution.py:1000
  157.9 52.8 %collective-permute-start.42 = (bf16[8,512,128]{2,1,0:T(8,128)(2,1)S(1)}, bf16[8,512,128]{2,1,0:T(8,128)(2,1)S(1)}, u32[]{:S(2)}, u32[]{:S(2)}) collective-permute-start(bf16[8,512,128]{2,1,0:T(8,128)(2,1)S(1)} %pad_maximum_fusion.1), channel_id=1, source_target_pairs={{0,2},{2,0},{4,6},{6,4},{8,10},{10,8},{12,14},{14,12},{16,18},{18,... | collective-permute-start | bytes 3145736 | tf_op jit(solution)/shard_map/ppermute | solution.py:903
  176.1 29.8 %collective-permute-start.37 = (bf16[8,336,128]{2,1,0:T(8,128)(2,1)}, bf16[8,336,128]{2,1,0:T(8,128)(2,1)S(1)}, u32[]{:S(2)}, u32[]{:S(2)}) collective-permute-start(bf16[8,336,128]{2,1,0:T(8,128)(2,1)} %get-tuple-element.96), channel_id=1, source_target_pairs={{0,2},{2,0},{4,6},{6,4},{8,10},{10,8},{12,14},{14,12},{16,18},{18,... | collective-permute-start | bytes 2064392 | tf_op jit(solution)/shard_map/ppermute | solution.py:903
  209.2 46.8 %collective-permute-start.38 = (bf16[4,336,128]{2,1,0:T(8,128)(2,1)}, bf16[4,336,128]{2,1,0:T(8,128)(2,1)S(1)}, u32[]{:S(2)}, u32[]{:S(2)}) collective-permute-start(bf16[4,336,128]{2,1,0:T(8,128)(2,1)} %get-tuple-element.98), channel_id=1, source_target_pairs={{0,4},{2,6},{4,0},{6,2},{8,12},{10,14},{12,8},{14,10},{16,20},{18,... | collective-permute-start | bytes 1032200 | tf_op jit(solution)/shard_map/ppermute | solution.py:907
  214.4 50.0 %collective-permute-start.43 = (bf16[4,512,128]{2,1,0:T(8,128)(2,1)}, bf16[4,512,128]{2,1,0:T(8,128)(2,1)S(1)}, u32[]{:S(2)}, u32[]{:S(2)}) collective-permute-start(bf16[4,512,128]{2,1,0:T(8,128)(2,1)} %get-tuple-element.114), channel_id=1, source_target_pairs={{0,4},{2,6},{4,0},{6,2},{8,12},{10,14},{12,8},{14,10},{16,20},{18,... | collective-permute-start | bytes 1572872 | tf_op jit(solution)/shard_map/ppermute | solution.py:907
  214.5 16.0 %collective-permute-start.48 = (f32[16,192]{1,0:T(8,128)S(1)}, f32[16,192]{1,0:T(8,128)S(1)}, u32[]{:S(2)}, u32[]{:S(2)}) collective-permute-start(f32[16,192]{1,0:T(8,128)S(1)} %fusion.13), channel_id=1, source_target_pairs={{0,4},{2,6},{4,0},{6,2},{8,12},{10,14},{12,8},{14,10},{16,20},{18,... | collective-permute-start | bytes 36872 | tf_op jit(solution)/shard_map/ppermute | solution.py:917
  230.6 21.1 %collective-permute-start.49 = (f32[16,192]{1,0:T(8,128)S(1)}, f32[16,192]{1,0:T(8,128)S(1)}, u32[]{:S(2)}, u32[]{:S(2)}) collective-permute-start(f32[16,192]{1,0:T(8,128)S(1)} %add.104), channel_id=1, source_target_pairs={{0,8},{2,10},{4,12},{6,14},{8,0},{10,2},{12,4},{14,6},{16,24},{18,... | collective-permute-start | bytes 36872 | tf_op jit(solution)/shard_map/ppermute | solution.py:917
  251.7 16.4 %collective-permute-start.50 = (f32[16,192]{1,0:T(8,128)S(1)}, f32[16,192]{1,0:T(8,128)S(1)}, u32[]{:S(2)}, u32[]{:S(2)}) collective-permute-start(f32[16,192]{1,0:T(8,128)S(1)} %add.105), channel_id=1, source_target_pairs={{0,16},{2,18},{4,20},{6,22},{8,24},{10,26},{12,28},{14,30},{16,0},... | collective-permute-start | bytes 36872 | tf_op jit(solution)/shard_map/ppermute | solution.py:917
  262.3 16.2 %collective-permute-start.41 = (bf16[336,128]{1,0:T(8,128)(2,1)}, bf16[336,128]{1,0:T(8,128)(2,1)S(1)}, u32[]{:S(2)}, u32[]{:S(2)}) collective-permute-start(bf16[336,128]{1,0:T(8,128)(2,1)} %get-tuple-element.102), channel_id=1, source_target_pairs={{0,24},{2,26},{4,28},{6,30},{8,16},{10,18},{12,20},{14,22},{16,8},... | collective-permute-start | bytes 258056 | tf_op jit(solution)/shard_map/ppermute | solution.py:910
  267.2 21.4 %collective-permute-start.44 = (bf16[512,128]{1,0:T(8,128)(2,1)}, bf16[512,128]{1,0:T(8,128)(2,1)S(1)}, u32[]{:S(2)}, u32[]{:S(2)}) collective-permute-start(bf16[512,128]{1,0:T(8,128)(2,1)} %get-tuple-element.116), channel_id=1, source_target_pairs={{0,8},{2,10},{4,12},{6,14},{8,0},{10,2},{12,4},{14,6},{16,24},{18,... | collective-permute-start | bytes 393224 | tf_op jit(solution)/shard_map/ppermute | solution.py:910
  268.1 20.5 %collective-permute-start.45 = (bf16[512,128]{1,0:T(8,128)(2,1)}, bf16[512,128]{1,0:T(8,128)(2,1)S(1)}, u32[]{:S(2)}, u32[]{:S(2)}) collective-permute-start(bf16[512,128]{1,0:T(8,128)(2,1)} %get-tuple-element.117), channel_id=1, source_target_pairs={{0,16},{2,18},{4,20},{6,22},{8,24},{10,26},{12,28},{14,30},{16,0},... | collective-permute-start | bytes 393224 | tf_op jit(solution)/shard_map/ppermute | solution.py:910
  268.4 20.2 %collective-permute-start.46 = (bf16[512,128]{1,0:T(8,128)(2,1)}, bf16[512,128]{1,0:T(8,128)(2,1)S(1)}, u32[]{:S(2)}, u32[]{:S(2)}) collective-permute-start(bf16[512,128]{1,0:T(8,128)(2,1)} %get-tuple-element.118), channel_id=1, source_target_pairs={{0,24},{2,26},{4,28},{6,30},{8,16},{10,18},{12,20},{14,22},{16,8},... | collective-permute-start | bytes 393224 | tf_op jit(solution)/shard_map/ppermute | solution.py:910
  (89 other events, 1435.5 us)

commit v2 on v1

--- a/solution.py
+++ b/solution.py
@@ -31,7 +31,7 @@
 bf16 = jnp.bfloat16
 ON_LAST = (((1,), (1,)), ((), ()))
 ON_FIRST = (((0,), (0,)), ((), ()))
-VMEM_BYTES = 56 * 1024 * 1024
+VMEM_BYTES = 45 * 1024 * 1024
 
 
 def step_rates():
@@ -49,16 +49,21 @@
     return pl.BlockSpec(memory_space=pltpu.VMEM)
 
 
-def call(body, outs, ins, scalars, scratch=(), flops=0):
-    moved = sum(a.size * a.dtype.itemsize for a in list(ins) + list(outs))
+def call(body, outs, ins, scalars, scratch=(), far=(), aliases=None, flops=0):
+    far = tuple(pltpu.with_memory_space_constraint(v, pltpu.HBM) for v in far)
+    ins = tuple(ins) + far
+    limit = VMEM_BYTES if body in (middle_of_block, attention_plain) else VMEM_BYTES // 3
     return pl.pallas_call(
         body,
         out_shape=tuple(outs),
-        in_specs=[pl.BlockSpec(memory_space=pltpu.SMEM)] + [spec() for _ in ins],
+        in_specs=[pl.BlockSpec(memory_space=pltpu.SMEM)]
+        + [spec() for _ in ins[: len(ins) - len(far)]]
+        + [pl.BlockSpec(memory_space=pltpu.HBM) for _ in far],
         out_specs=tuple(spec() for _ in outs),
         scratch_shapes=list(scratch),
-        compiler_params=pltpu.CompilerParams(vmem_limit_bytes=VMEM_BYTES),
-        cost_estimate=pl.CostEstimate(flops=flops, bytes_accessed=moved, transcendentals=0),
+        input_output_aliases=aliases or {},
+        compiler_params=pltpu.CompilerParams(vmem_limit_bytes=limit),
+        cost_estimate=pl.CostEstimate(flops=flops, bytes_accessed=1024, transcendentals=0),
     )(scalars, *ins)
 
 
@@ -246,43 +251,80 @@
     return jnp.concatenate((one, two[0 : rows - top]), axis=0)
 
 
+def pack_exchange(at, features_ref, vec_ref, out_ref):
+    out_ref[0:HALF, :] = features_ref[...]
+    vec = jnp.concatenate((vec_ref[...], jnp.zeros((3, HALF), f32)), axis=0)
+    coarse = vec.astype(bf16)
+    out_ref[HALF : HALF + 16, :] = jnp.zeros((16, PIX), bf16)
+    out_ref[HALF : HALF + 16, 0:HALF] = coarse
+    out_ref[HALF : HALF + 16, 256 : 256 + HALF] = (vec - coarse.astype(f32)).astype(bf16)
+
+
 def pack_first(at, conv_ref, out_ref):
-    part, shared = tile_parts(conv_ref[...], at[0])
+    part, shared = tile_parts(conv_ref[...].T, at[0])
     out_ref[0:224, :] = pad_rows(part, 224).astype(bf16)
     out_ref[224:336, :] = pair_rows(shared, 112).astype(bf16)
 
 
-FILM_AT, SHARED_AT = 224, 320
-FILM_SHARED, IN_AT, IN_SHARED, OUT_AT, OUT_SHARED, SECOND_ROWS = 112, 160, 240, 288, 320, 336
-
-
-def pack_second(at, conv_ref, film_ref, in_ref, out_weight_ref, out_ref):
+FIRST_ROWS = 336
+FILM_AT, FILM_SHARED, EMBED_AT, IN_AT, IN_SHARED, OUT_AT, OUT_SHARED, SECOND_ROWS = 336, 432, 480, 496, 576, 624, 656, 672
+
+
+def stack(at, *refs):
+    for step in range(4):
+        refs[-1][step] = refs[step][...]
+
+
+def pass_on(at, *refs):
+    pass
+
+
+def put_rows(out_ref, start, block):
+    rows = -(-block.shape[0] // 16) * 16
+    out_ref[start : start + rows, :] = pad_rows(block, rows).astype(bf16)
+
+
+def pack_second(at, conv_ref, film_ref, embed_ref, in_ref, out_weight_ref, out_ref):
     narrow = at[0]
-
-    def put(start, block):
-        rows = -(-block.shape[0] // 16) * 16
-        out_ref[start : start + rows, :] = pad_rows(block, rows).astype(bf16)
-
-    part, shared = tile_parts(conv_ref[...], narrow)
-    put(0, part)
-    put(SHARED_AT, pair_rows(shared, 112))
-    part, shared = tile_parts(jnp.concatenate((film_ref[0], film_ref[1]), axis=0), narrow)
-    put(FILM_AT, part)
-    put(SHARED_AT + FILM_SHARED, pair_rows(shared, 48))
+    embed = embed_ref[...].astype(f32)
+    put_rows(
+        out_ref,
+        EMBED_AT,
+        jnp.concatenate([embed[:, 128 * i : 128 * i + 128] for i in range(EMB // 128)], axis=0),
+    )
+    part, shared = tile_parts(conv_ref[...].T, narrow)
+    put_rows(out_ref, 0, part)
+    put_rows(out_ref, 224, pair_rows(shared, 112))
+    part, shared = tile_parts(
+        jnp.concatenate((film_ref[:, 0, :], film_ref[:, 1, :]), axis=0), narrow
+    )
+    put_rows(out_ref, FILM_AT, part)
+    put_rows(out_ref, FILM_SHARED, pair_rows(shared, 48))
     part, shared = tile_parts(jnp.concatenate((in_ref[0], in_ref[1], in_ref[2]), axis=0), narrow)
-    put(SHARED_AT + IN_AT, part)
-    put(SHARED_AT + IN_SHARED, pair_rows(shared, 40))
+    put_rows(out_ref, IN_AT, part)
+    put_rows(out_ref, IN_SHARED, pair_rows(shared, 40))
     part, shared = tile_parts(out_weight_ref[...], narrow)
-    put(SHARED_AT + OUT_AT, part)
-    put(SHARED_AT + OUT_SHARED, pair_rows(shared, 16))
+    put_rows(out_ref, OUT_AT, part)
+    put_rows(out_ref, OUT_SHARED, pair_rows(shared, 16))
 
 
 class Gathered:
-    def __init__(self, at, refs):
+    def __init__(self, at, refs, held_ref, sems):
         self.narrow, self.core, self.side, self.depth = at[0], at[1], at[2], at[3]
-        keys = ((0, 0), (1, 0), (0, 1), (1, 1))
-        self.own = dict(zip(keys, refs[:4]))
-        self.other = dict(zip(keys, refs[4:]))
+        self.held = held_ref
+        self.copies = {}
+        for differs in (0, 1):
+            for index in range(differs, 8, 2):
+                copy = pltpu.make_async_copy(refs[index], held_ref.at[index], sems.at[index])
+                copy.start()
+                self.copies[index] = copy
+
+    def part(self, other, differs, across, step):
+        return self.held.at[4 * other + 2 * across + differs, step]
+
+    def wait(self, differs):
+        for index in range(differs, 8, 2):
+            self.copies[index].wait()
 
     def chips(self):
         for differs in (0, 1):
@@ -293,8 +335,8 @@
         upto = -(-rows // 16) * 16
         found = []
         for across in (0, 1):
-            own = self.own[differs, across][step, start : start + upto, :].astype(f32)[0:rows]
-            other = self.other[differs, across][step, start : start + upto, :].astype(f32)[0:rows]
+            own = self.part(0, differs, across, step)[start : start + upto, :].astype(f32)[0:rows]
+            other = self.part(1, differs, across, step)[start : start + upto, :].astype(f32)[0:rows]
             found.append(
                 (jnp.where(self.core == 0, own, other), jnp.where(self.core == 0, other, own))
             )
@@ -308,22 +350,24 @@
         )
 
 
-def place_conv(whole, shared, shared_at, kernel_ref):
-    for differs, step, chip in whole.chips():
+def place_conv(units, kernel_ref):
+    for differs, step, chip in units.chips():
+        if step == 0:
+            units.wait(differs)
         rows = pl.ds(aligned(chip * (2 * ROWS), 16), 2 * ROWS)
-        low, high = whole.cores(differs, step, 0, ROWS)
+        low, high = units.cores(differs, step, 0, ROWS)
         kernel_ref[rows, 0:128] = jnp.concatenate(low, axis=0).astype(bf16)
         kernel_ref[rows, 256:384] = jnp.concatenate(high, axis=0).astype(bf16)
-        low, high = shared.cores(differs, step, shared_at, 112)
+        low, high = units.cores(differs, step, 224, 112)
         kernel_ref[rows, 128:256] = jnp.concatenate(
             [middle(low[core], high[core], 112, ROWS) for core in (0, 1)], axis=0
         ).astype(bf16)
 
 
-def place_film(whole, shared, film_ref):
-    for differs, step, chip in whole.chips():
+def place_film(units, film_ref):
+    for differs, step, chip in units.chips():
         rows = pl.ds(aligned(chip * 96, 16), 96)
-        low, high = whole.cores(differs, step, FILM_AT, 96)
+        low, high = units.cores(differs, step, FILM_AT, 96)
         for index in (0, 1):
             part = slice(48 * index, 48 * index + 48)
             film_ref[rows, index * C : index * C + 128] = jnp.concatenate(
@@ -332,7 +376,7 @@
             film_ref[rows, index * C + 256 : index * C + 384] = jnp.concatenate(
                 [high[core][part] for core in (0, 1)], axis=0
             ).astype(bf16)
-        low, high = shared.cores(differs, step, FILM_SHARED, 48)
+        low, high = units.cores(differs, step, FILM_SHARED, 48)
         both = [middle(low[core], high[core], 48, 96) for core in (0, 1)]
         for index in (0, 1):
             part = slice(48 * index, 48 * index + 48)
@@ -341,11 +385,21 @@
             ).astype(bf16)
 
 
-def place_attention(shared, in_ref, out_ref):
+def place_embeddings(shared, soft_ref):
     for differs, step, chip in shared.chips():
+        for other in (0, 1):
+            row = 4 * step + 2 * differs + other
+            part = shared.part(other, differs, 0, step)[EMBED_AT : EMBED_AT + 16, :].astype(f32)
+            part = (part * lax.logistic(part)).astype(bf16).astype(f32)
+            for index in range(EMB // 128):
+                soft_ref[row : row + 1, 128 * index : 128 * index + 128] = part[index : index + 1]
+
+
+def place_attention(units, in_ref, out_ref):
+    for differs, step, chip in units.chips():
         rows = pl.ds(aligned(chip * 48, 16), 48)
-        low, high = shared.cores(differs, step, IN_AT, 72)
-        near, far = shared.cores(differs, step, IN_SHARED, 40)
+        low, high = units.cores(differs, step, IN_AT, 72)
+        near, far = units.cores(differs, step, IN_SHARED, 40)
         both = [middle(near[core], far[core], 40, 72) for core in (0, 1)]
         for index in range(3):
             part = slice(24 * index, 24 * index + 24)
@@ -353,8 +407,8 @@
                 in_ref[rows, index * C + 128 * tile : index * C + 128 * tile + 128] = (
                     jnp.concatenate([source[core][part] for core in (0, 1)], axis=0)
                 )
-        low, high = shared.cores(differs, step, OUT_AT, 24)
-        near, far = shared.cores(differs, step, OUT_SHARED, 16)
+        low, high = units.cores(differs, step, OUT_AT, 24)
+        near, far = units.cores(differs, step, OUT_SHARED, 16)
         both = [middle(near[core], far[core], 16, 24) for core in (0, 1)]
         for tile, source in ((0, low), (1, both), (2, high)):
             out_ref[rows, 128 * tile : 128 * tile + 128] = jnp.concatenate(source, axis=0)
@@ -383,10 +437,20 @@
     return jnp.concatenate((jnp.where(lane(block.shape[0]) < HEAD, one, two), two), axis=1)
 
 
-def first_norm(at, own_ref, other_ref, mask_ref, vec_ref, turned_ref, taps_ref, stat_ref, rows_ref, raw_ref):
+def first_norm(at, own_ref, other_ref, mask_ref, vec_own_ref, cot_ref, *refs):
+    turned_ref, taps_ref, stat_ref, vec_ref, cot_out_ref, rows_ref, raw_ref = refs[-7:]
     narrow = at[0]
+    cot_out_ref[...] = cot_ref[...]
+    own = vec_own_ref[...]
+    other = (
+        other_ref[HALF : HALF + 16, 0:HALF].astype(f32)
+        + other_ref[HALF : HALF + 16, 256 : 256 + HALF].astype(f32)
+    )[0:13]
+    vec_ref[0:13, 0:HALF] = jnp.where(narrow == 0, own, other)
+    vec_ref[0:13, HALF:C] = jnp.where(narrow == 0, other, own)
+    vec_ref[13:16, :] = jnp.zeros((3, C), f32)
     own = own_ref[...].astype(f32)
-    other = other_ref[...].astype(f32)
+    other = other_ref[0:HALF, :].astype(f32)
     low = jnp.where(narrow == 0, own, other)
     high = jnp.where(narrow == 0, other, own)
     for index in range(PIX // 128):
@@ -420,10 +484,9 @@
 
 
 def first_conv(at, taps_ref, mask_ref, vec_ref, *refs):
-    whole = Gathered(at, refs[0:8])
-    shared = Gathered(at, refs[8:16])
-    out_ref, kernel_ref, stat_ref = refs[16:]
-    place_conv(whole, shared, 0, kernel_ref)
+    out_ref, kernel_ref, stat_ref, held_ref, sems = refs[-5:]
+    units = Gathered(at, refs[0:8], held_ref, sems)
+    place_conv(units, kernel_ref)
     conv_then_stats(taps_ref, kernel_ref, mask_ref, vec_ref, out_ref, stat_ref)
 
 
@@ -478,19 +541,6 @@
     chunks(apply, 0)
 
 
-def second_conv(at, one_ref, stat_two_ref, turned_ref, mask_ref, vec_ref, embed_ref, *refs):
-    whole = Gathered(at, refs[0:8])
-    shared = Gathered(at, refs[8:16])
-    taps_ref, residual_ref, hidden_ref, stat_ref, film_rows_ref, kernel_ref = refs[16:22]
-    soft_ref, rows_ref, film_ref = refs[22:]
-    place_film(whole, shared, film_ref)
-    place_conv(whole, shared, 0, kernel_ref)
-    film_to_third_norm(
-        one_ref, stat_two_ref, turned_ref, mask_ref, vec_ref, embed_ref, kernel_ref, film_ref,
-        taps_ref, residual_ref, hidden_ref, stat_ref, film_rows_ref, soft_ref, rows_ref,
-    )
-
-
 def second_conv_plain(
     at, one_ref, stat_two_ref, turned_ref, mask_ref, vec_ref, embed_ref, kernel_ref, film_ref,
     taps_ref, residual_ref, hidden_ref, stat_ref, film_rows_ref, soft_ref, rows_ref,
@@ -504,51 +554,72 @@
 QUERY = 256
 
 
-def attention_both(q_ref, k_ref, v_ref, up_ref, out_ref, dq_ref, dk_ref, dv_ref, dk_acc, dv_acc):
-    place = lane(QUERY)
-    for head in range(HEADS):
-        columns = slice(128 * head, 128 * head + 128)
-        dk_acc[...] = jnp.zeros_like(dk_acc)
-        dv_acc[...] = jnp.zeros_like(dv_acc)
-
-        def block(index, carry):
-            rows = pl.ds(aligned(index * QUERY, QUERY), QUERY)
-            queries, keys, values = q_ref[rows, columns], k_ref[:, columns], v_ref[:, columns]
-            scores = lax.dot_general(queries, keys, ON_LAST, preferred_element_type=f32)
-            highest = jnp.max(scores, axis=1, keepdims=True)
-            raised = jnp.exp2((scores - highest) * exponent_scale)
-            raised_low = raised.astype(bf16)
-            mixture = jnp.dot(raised_low, values, preferred_element_type=f32)
-            inverse = 1.0 / mixture[:, HEAD : HEAD + 1]
-            mixture = mixture * inverse
-            out_ref[rows, columns] = mixture.astype(bf16)
-            up = (up_ref[rows, columns].astype(f32) * inverse).astype(bf16)
-            wide_up = up.astype(f32)
-            both = jnp.sum(wide_up * mixture, axis=1, keepdims=True)
-            coarse = both.astype(bf16).astype(f32)
-            wide_up = jnp.where(place == HEAD, -coarse, wide_up)
-            wide_up = jnp.where(place == HEAD + 1, coarse - both, wide_up)
-            slopes = lax.dot_general(
-                wide_up.astype(bf16), values, ON_LAST, preferred_element_type=f32
-            )
-            slopes = (raised * slopes).astype(bf16)
-            dq_ref[rows, columns] = (
-                jnp.dot(slopes, keys, preferred_element_type=f32) * score_scale
-            ).astype(bf16)
-            dk_acc[...] += lax.dot_general(slopes, queries, ON_FIRST, preferred_element_type=f32)
-            dv_acc[...] += lax.dot_general(raised_low, up, ON_FIRST, preferred_element_type=f32)
-            return carry
-
-        lax.fori_loop(0, PIX // QUERY, block, 0, unroll=True)
-        dk_ref[:, columns] = (dk_acc[...] * score_scale).astype(bf16)
-        dv_ref[:, columns] = dv_acc[...].astype(bf16)
+def attention_both(q_ref, k_ref, v_ref, kt_ref, vt_ref, upt_ref, outt_ref, dqt_ref, dk_acc, dv_acc):
+    place = lax.broadcasted_iota(jnp.int32, (128, QUERY), 0)
+    steps = PIX // QUERY
+
+    def where(item):
+        head, step = divmod(item, steps)
+        return slice(128 * head, 128 * head + 128), slice(step * QUERY, step * QUERY + QUERY), step
+
+    def raise_scores(item):
+        columns, rows, _ = where(item)
+        scores = lax.dot_general(
+            k_ref[:, columns], q_ref[rows, columns], ON_LAST, preferred_element_type=f32
+        )
+        highest = jnp.max(scores, axis=0, keepdims=True)
+        return jnp.exp2((scores - highest) * exponent_scale)
+
+    def score_slopes(item, raised):
+        columns, rows, _ = where(item)
+        low = raised.astype(bf16)
+        mixture = jnp.dot(vt_ref[columns, :], low, preferred_element_type=f32)
+        inverse = 1.0 / mixture[HEAD : HEAD + 1, :]
+        mixture = mixture * inverse
+        outt_ref[columns, rows] = mixture.astype(bf16)
+        up = (upt_ref[columns, rows].astype(f32) * inverse).astype(bf16)
+        wide_up = up.astype(f32)
+        both = jnp.sum(wide_up * mixture, axis=0, keepdims=True)
+        coarse = both.astype(bf16).astype(f32)
+        wide_up = jnp.where(place == HEAD, -coarse, wide_up)
+        wide_up = jnp.where(place == HEAD + 1, coarse - both, wide_up)
+        slopes = jnp.dot(v_ref[:, columns], wide_up.astype(bf16), preferred_element_type=f32)
+        return low, up, (raised * slopes).astype(bf16)
+
+    def gradients(item, low, up, slopes):
+        columns, rows, step = where(item)
+        dqt_ref[columns, rows] = (
+            jnp.dot(kt_ref[columns, :], slopes, preferred_element_type=f32) * score_scale
+        ).astype(bf16)
+        dk = jnp.dot(slopes, q_ref[rows, columns], preferred_element_type=f32)
+        dv = lax.dot_general(low, up, ON_LAST, preferred_element_type=f32)
+        if step == 0:
+            dk_acc[...] = dk
+            dv_acc[...] = dv
+        elif step < steps - 1:
+            dk_acc[...] += dk
+            dv_acc[...] += dv
+        else:
+            k_ref[:, columns] = ((dk_acc[...] + dk) * score_scale).astype(bf16)
+            v_ref[:, columns] = (dv_acc[...] + dv).astype(bf16)
+
+    count = HEADS * steps
+    raised, waiting = raise_scores(0), None
+    for item in range(count):
+        following = raise_scores(item + 1) if item + 1 < count else None
+        found = score_slopes(item, raised)
+        if waiting is not None:
+            gradients(*waiting)
+        waiting = (item, *found)
+        raised = following
+    gradients(*waiting)
 
 
 def attention_body(
     at, hidden_ref, residual_ref, stat_ref, mask_ref, vec_ref, own_ref, other_ref,
     out_ref, direct_ref, taps_ref, back_ref, vec_grad_ref, in_nat, out_nat,
-    in_ref, weight_ref, q_ref, k_ref, v_ref, up_ref, mix_ref, dq_ref, dk_ref, dv_ref,
-    dk_acc, dv_acc, cot_ref, rows_ref, turn_ref, own_cot,
+    in_ref, weight_ref, q_ref, k_ref, v_ref, kt_ref, vt_ref, upt_ref, mixt_ref, dqt_ref,
+    dk_acc, dv_acc, cot_ref, rows_ref, terms_ref, own_cot,
 ):
     narrow = at[0]
     for index in range(3):
@@ -586,44 +657,60 @@
         valid = mask_ref[here, :]
         barred = jnp.where(valid > 0, 0.0, masked_score)
         barred = jnp.concatenate((barred, barred, barred, barred), axis=1)
-        k_ref[here, :] = jnp.where(spare == HEAD, barred, value).astype(bf16)
+        value = jnp.where(spare == HEAD, barred, value).astype(bf16)
+        k_ref[here, :] = value
+        kt_ref[:, here] = value.T
         value = jnp.dot(hidden, in_ref[:, 1024:1536], preferred_element_type=f32) + bias_v
-        v_ref[here, :] = jnp.where((spare == HEAD) | (spare == HEAD + 1), 1.0, value).astype(bf16)
-        up_ref[here, :] = lax.dot_general(
-            cot_ref[here, :], weight_ref[...], ON_LAST, preferred_element_type=f32
+        value = jnp.where((spare == HEAD) | (spare == HEAD + 1), 1.0, value).astype(bf16)
+        v_ref[here, :] = value
+        vt_ref[:, here] = value.T
+        upt_ref[:, here] = lax.dot_general(
+            weight_ref[...], cot_ref[here, :], ON_LAST, preferred_element_type=f32
         ).astype(bf16)
-    attention_both(q_ref, k_ref, v_ref, up_ref, mix_ref, dq_ref, dk_ref, dv_ref, dk_acc, dv_acc)
+    attention_both(q_ref, k_ref, v_ref, kt_ref, vt_ref, upt_ref, mixt_ref, dqt_ref, dk_acc, dv_acc)
+    dk_ref, dv_ref = k_ref, v_ref
     bias = vec_ref[10:11, :]
     for index in range(PIX // 128):
         here = slice(128 * index, 128 * index + 128)
-        value = jnp.dot(mix_ref[here, :], weight_ref[...], preferred_element_type=f32) + bias
+        value = jnp.dot(mixt_ref[:, here].T, weight_ref[...], preferred_element_type=f32) + bias
         valid = wide_mask(mask_ref, 128 * index, 128)
-        turn_ref[:, here] = (residual_ref[here, :] + value * valid).T
-    out_ref[...] = turn_ref[pl.ds(aligned(narrow * HALF, 16), HALF), :].astype(bf16)
+        quarter, side = divmod(index, 2)
+        terms_ref[quarter * C : quarter * C + C, 128 * side : 128 * side + 128] = (
+            residual_ref[here, :] + value * valid
+        ).T
+    for quarter in range(4):
+        out_ref[:, 256 * quarter : 256 * quarter + 256] = terms_ref[
+            pl.ds(aligned(quarter * C + narrow * HALF, 16), HALF), :
+        ].astype(bf16)
     heads_here = pl.ds(aligned(narrow * 256, 128), 256)
-    terms = lax.dot_general(mix_ref[...], own_cot[...], ON_FIRST, preferred_element_type=f32)
+    terms = jnp.dot(mixt_ref[...], own_cot[...], preferred_element_type=f32)
     for head in range(HEADS):
         out_nat[HEAD * head : HEAD * head + HEAD, 0:256] = terms[128 * head : 128 * head + HEAD]
-    sums = []
-    for index, source in enumerate((dq_ref, dk_ref, dv_ref)):
+    terms = jnp.dot(
+        dqt_ref[pl.ds(aligned(narrow * 256, 128), 256), :],
+        hidden_ref[...],
+        preferred_element_type=f32,
+    )
+    in_nat[:, 0:256] = join_heads(terms.T)
+    for index, source in ((1, dk_ref), (2, dv_ref)):
         terms = lax.dot_general(
             hidden_ref[...], source[:, heads_here], ON_FIRST, preferred_element_type=f32
         )
         in_nat[:, 256 * index : 256 * index + 256] = join_heads(terms)
-        acc = jnp.zeros((8, 512), f32)
-        if index != 1:
-            for part in range(PIX // 128):
-                acc = acc + fold(source[128 * part : 128 * part + 128, :].astype(f32))
-        sums.append(acc)
+    ones = jnp.ones((8, PIX), bf16)
+    sums = (
+        lax.dot_general(ones, dqt_ref[...], ON_LAST, preferred_element_type=f32),
+        jnp.dot(ones, dv_ref[...], preferred_element_type=f32),
+    )
     mean, inverse, tally = stat_ref[0:1, :], stat_ref[1:2, :], stat_ref[2:3, :]
     gain = vec_ref[6:7, :]
     acc_shift, acc_gain = zero, zero
     for index in range(PIX // 256):
         here = slice(256 * index, 256 * index + 256)
         value = None
-        for part, source in enumerate((dq_ref, dk_ref, dv_ref)):
+        for part, source in enumerate((dqt_ref[:, here].T, dk_ref[here, :], dv_ref[here, :])):
             term = lax.dot_general(
-                source[here, :], in_ref[:, 512 * part : 512 * part + 512], ON_LAST,
+                source, in_ref[:, 512 * part : 512 * part + 512], ON_LAST,
                 preferred_element_type=f32,
             )
             value = term if value is None else value + term
@@ -654,7 +741,7 @@
     vec_grad_ref[5:6, :] = total(bias_two)
     vec_grad_ref[6:7, :] = gain_grad
     vec_grad_ref[7:8, :] = shift_grad
-    for row, acc in ((8, sums[0]), (9, sums[2])):
+    for row, acc in ((8, sums[0]), (9, sums[1])):
         pair_one, pair_two = join_heads(acc[:, 0:256]), join_heads(acc[:, 256:512])
         turned = pltpu.roll(pair_two[:, 0:128], 64, 1)
         natural = jnp.concatenate(
@@ -665,7 +752,7 @@
             ),
             axis=1,
         )
-        vec_grad_ref[row : row + 1, :] = total(natural)
+        vec_grad_ref[row : row + 1, :] = natural[0:1]
     vec_grad_ref[10:11, :] = total(bias_out)
 
 
@@ -673,14 +760,31 @@
     return pl.ds(aligned(chip * 2 * grad + core * grad, 8), grad)
 
 
-def attention(at, hidden_ref, residual_ref, stat_ref, mask_ref, vec_ref, own_ref, other_ref, *refs):
-    shared = Gathered(at, refs[0:8])
-    out_ref, direct_ref, taps_ref, back_ref, vec_grad_ref, keep_ref, send_ref = refs[8:15]
-    in_nat, out_nat = refs[15:17]
-    place_attention(shared, in_nat, out_nat)
+def middle_of_block(
+    at, one_ref, stat_two_ref, turned_ref, mask_ref, vec_ref, embed_ref, own_ref, other_ref, *refs
+):
+    (
+        out_ref, direct_ref, back_taps_ref, vec_grad_ref, film_rows_ref, kernel_ref, soft_all_ref,
+        keep_ref, send_ref,
+    ) = refs[8:17]
+    (
+        taps_ref, residual_ref, hidden_ref, stat_ref, soft_ref, film_ref, held_ref, sems, back_ref,
+    ) = refs[17:26]
+    attention_refs = refs[26:]
+    in_nat, out_nat = attention_refs[0:2]
+    rows_ref, terms_ref = attention_refs[-3:-1]
+    units = Gathered(at, refs[0:8], held_ref, sems)
+    place_conv(units, kernel_ref)
+    place_film(units, film_ref)
+    place_embeddings(units, soft_all_ref)
+    film_to_third_norm(
+        one_ref, stat_two_ref, turned_ref, mask_ref, vec_ref, embed_ref, kernel_ref, film_ref,
+        taps_ref, residual_ref, hidden_ref, stat_ref, film_rows_ref, soft_ref, rows_ref,
+    )
+    place_attention(units, in_nat, out_nat)
     attention_body(
         at, hidden_ref, residual_ref, stat_ref, mask_ref, vec_ref, own_ref, other_ref,
-        out_ref, direct_ref, taps_ref, back_ref, vec_grad_ref, *refs[15:],
+        out_ref, direct_ref, back_taps_ref, back_ref, vec_grad_ref, *attention_refs,
     )
     for chip in range(8):
         for target, core in ((keep_ref, at[1]), (send_ref, 1 - at[1])):
@@ -688,11 +792,13 @@
             block = jnp.concatenate(
                 [in_nat[rows, 256 * index : 256 * index + 256] for index in range(3)], axis=0
             )
-            target[chip, 0:80, :] = pad_rows(block[:, 0:128], 80).astype(bf16)
-            target[chip, 80:128, :] = pad_rows(pair_rows(block[:, 128:256], 40), 48).astype(bf16)
+            target[chip, 336:416, :] = pad_rows(block[:, 0:128], 80).astype(bf16)
+            target[chip, 416:464, :] = pad_rows(pair_rows(block[:, 128:256], 40), 48).astype(bf16)
             block = out_nat[rows, 0:256]
-            target[chip, 128:160, :] = pad_rows(block[:, 0:128], 32).astype(bf16)
-            target[chip, 160:176, :] = pair_rows(block[:, 128:256], 16).astype(bf16)
+            target[chip, 464:496, :] = pad_rows(block[:, 0:128], 32).astype(bf16)
+            target[chip, 496:512, :] = pair_rows(block[:, 128:256], 16).astype(bf16)
+    kernel_terms(taps_ref, back_ref, terms_ref)
+    pack_units(terms_ref, at, keep_ref, send_ref)
 
 
 def attention_plain(
@@ -719,16 +825,23 @@
             target[chip, 224:336, :] = pair_rows(terms_ref[rows, 128:256], 112).astype(bf16)
 
 
-def conv_terms(at, taps_ref, own_ref, keep_ref, send_ref, terms_ref):
-    kernel_terms(taps_ref, own_ref, terms_ref)
-    pack_units(terms_ref, at, keep_ref, send_ref)
-
-
 def conv_terms_plain(at, taps_ref, own_ref, terms_ref):
     kernel_terms(taps_ref, own_ref, terms_ref)
 
 
-def second_back(
+def second_back(at, *refs):
+    taps_one_ref, back_taps_ref, vec_grad_ref, keep_ref, send_ref = refs[8:9] + refs[-8:-4]
+    grad_ref, rows_ref, back_ref, terms_ref = refs[-4:]
+    second_back_body(at, *refs[:8], back_taps_ref, back_ref, vec_grad_ref, grad_ref, rows_ref)
+    kernel_terms(taps_one_ref, back_ref, terms_ref)
+    pack_units(terms_ref, at, keep_ref, send_ref)
+
+
+def second_back_plain(at, *refs):
+    second_back_body(at, *refs)
+
+
+def second_back_body(
     at, taps_ref, kernel_ref, one_ref, stat_ref, film_rows_ref, mask_ref, vec_ref, vec_in_ref,
     back_taps_ref, back_ref, vec_grad_ref, grad_ref, rows_ref,
 ):
@@ -778,9 +891,10 @@
 
 
 def first_back(
-    at, taps_ref, kernel_ref, turned_ref, stat_ref, direct_ref, mask_ref, vec_ref, vec_in_ref,
-    out_ref, vec_grad_ref, grad_ref, turn_ref,
+    at, taps_ref, kernel_ref, turned_ref, stat_ref, direct_ref, mask_ref, vec_ref, vec_in_ref, *refs,
 ):
+    out_ref, vec_grad_ref, grad_ref, turn_ref = refs[-4:]
+
     def done(start, count, acc):
         grad_ref[pl.ds(start, count), :] = acc
 
@@ -809,9 +923,9 @@
         value = (grad_ref[here, :] * gain - first_mean - normed * second_mean) * inverse * valid
         turn_ref[:, here] = (value + direct_ref[here, :]).T
     out_ref[...] = turn_ref[pl.ds(aligned(at[0] * HALF, 16), HALF), :].astype(bf16)
-    vec_grad_ref[...] = vec_in_ref[...]
-    vec_grad_ref[0:1, :] = gain_grad
-    vec_grad_ref[1:2, :] = shift_grad
+    place = lax.broadcasted_iota(jnp.int32, (16, 1), 0)
+    rows = jnp.where(place == 0, gain_grad, jnp.where(place == 1, shift_grad, vec_in_ref[...]))
+    vec_grad_ref[...] = own_half(rows, at[0])
 
 
 def add_cores(at, keep_ref, back_ref, own_ref, across_ref):
@@ -843,6 +957,13 @@
     return jnp.concatenate((block, pltpu.roll(block, 64, 1)[0 : rows - top]), axis=0)
 
 
+def adam_into(gradient, given, outs, rate, where):
+    weight, moment, square = (ref[where] for ref in given)
+    results = adam_update(weight, gradient, moment, square, rate)
+    for out, value in zip(outs, (gradient,) + results):
+        out[where] = value
+
+
 def conv_adam(parts, weight_ref, moment_ref, square_ref, outs, rate):
     def summed(start, stop):
         return sum(part[start:stop, :].astype(f32) for part in parts[1:]) + parts[0][
@@ -851,12 +972,10 @@
 
     low = summed(0, 224)[0:ROWS]
     high = unpair_rows(summed(224, 336), ROWS)
-    for columns, gradient in ((slice(0, 128), low), (slice(128, 192), high[:, 0:64])):
-        results = adam_update(
-            weight_ref[:, columns], gradient, moment_ref[:, columns], square_ref[:, columns], rate
-        )
-        for out, value in zip(outs, (gradient,) + results):
-            out[:, columns] = value
+    gradient = jnp.concatenate((low, high[:, 0:64]), axis=1).T
+    results = adam_update(weight_ref[...], gradient, moment_ref[...], square_ref[...], rate)
+    for out, value in zip(outs, (gradient,) + results):
+        out[...] = value
     return summed
 
 
@@ -865,46 +984,89 @@
 
 
 def finish_second(at, *refs):
-    summed = conv_adam(refs[0:4], *refs[4:7], refs[7:11], step_rates()[1])
-    in_ref, out_ref = refs[11:]
-    low = summed(336, 416)[0:72]
-    high = unpair_rows(summed(416, 464)[0:40], 72)
+    given, results = refs[4:13], refs[13:]
+    summed = conv_adam(refs[0:4], *given[0:3], results[0:4], step_rates()[1])
+    gradient = jnp.concatenate(
+        (summed(336, 416)[0:72], unpair_rows(summed(416, 464)[0:40], 72)[:, 0:64]), axis=1
+    )
     for index in range(3):
-        part = slice(24 * index, 24 * index + 24)
-        in_ref[index, :, 0:128] = low[part]
-        in_ref[index, :, 128:192] = high[part, 0:64]
-    out_ref[:, 0:128] = summed(464, 496)[0:24]
-    out_ref[:, 128:192] = unpair_rows(summed(496, 512), 24)[:, 0:64]
-
-
-def gather_units(unit, cut, wide):
-    core_swap = [(i, i ^ 1) for i in range(wide)]
-    side_swap = [(i, i ^ 2) for i in range(wide)]
-    flip = [(0, 1), (1, 0)]
-    column = [unit] + [
+        adam_into(
+            gradient[24 * index : 24 * index + 24], given[3:6], results[4:8], step_rates()[3], index
+        )
+    gradient = jnp.concatenate(
+        (summed(464, 496)[0:24], unpair_rows(summed(496, 512), 24)[:, 0:64]), axis=1
+    )
+    adam_into(gradient, given[6:9], results[8:12], step_rates()[4], Ellipsis)
+
+
+def finish_small(at, own_ref, one_ref, two_ref, three_ref, soft_ref, *refs):
+    wide = (at[3] * 2 + at[2]) * 2 + at[1]
+    given, results, grad_ref = refs[0:6], refs[6:14], refs[14]
+    sums, films = None, []
+    for far, ref in enumerate((own_ref, one_ref, two_ref, three_ref)):
+        for near in range(4):
+            rows = ref[near]
+            sums = rows if sums is None else sums + rows
+            films.append(jnp.concatenate((rows[11:12], rows[12:13]), axis=1))
+    adam_into(sums[0:13, 0:HALF], given[0:3], results[0:4], step_rates()[5], Ellipsis)
+    grad_ref[...] = lax.dot_general(
+        soft_ref[...].astype(bf16), jnp.concatenate(films, axis=0).astype(bf16), ON_FIRST,
+        preferred_element_type=f32,
+    )
+    here = pl.ds(aligned(wide * 48, 8), 48)
+    for index in (0, 1):
+        gradient = grad_ref[here, 256 * index : 256 * index + HALF]
+        adam_into(
+            gradient, given[3:6], results[4:8], step_rates()[2], (slice(None), index, slice(None))
+        )
+
+
+def along_depth(unit, wide):
+    return [unit] + [
         lax.ppermute(unit, "wide", [(i, i ^ (4 * step)) for i in range(wide)])
         for step in (1, 2, 3)
     ]
-    one = jnp.stack([part[:cut] for part in column])
-    two = jnp.stack([part[cut:] for part in column])
-    side_one, side_two = (lax.ppermute(v, "wide", side_swap) for v in (one, two))
-    over_one, over_two = (lax.ppermute(v, "narrow", flip) for v in (one, two))
-    far_one = lax.ppermute(over_one, "wide", side_swap)
-    far_two = lax.ppermute(side_two, "narrow", flip)
-    ones = [one, side_one, over_one, far_one]
-    twos = [two, side_two, over_two, far_two]
-    ones = ones + [lax.ppermute(v, "wide", core_swap) for v in ones]
-    twos = twos + [lax.ppermute(v, "wide", core_swap) for v in twos]
-    return ones, twos
-
-
-def reduce_units(keep, send, scalars, wide):
-    rows = keep.shape[1]
+
+
+def gather_rest(depth, after, scalars, wide):
+    (whole,) = call(stack, (shaped((4, *depth[0].shape), bf16),), depth, scalars, far=after)
+    both = ("wide", "narrow")
+    diagonal = [(2 * i + x, 2 * (i ^ 2) + 1 - x) for i in range(wide) for x in (0, 1)]
+    return [
+        whole,
+        lax.ppermute(whole, "wide", [(i, i ^ 2) for i in range(wide)]),
+        lax.ppermute(whole, "narrow", [(0, 1), (1, 0)]),
+        lax.ppermute(whole, both, diagonal),
+    ]
+
+
+def both_cores(parts, wide):
+    return list(parts) + [
+        lax.ppermute(v, "wide", [(i, i ^ 1) for i in range(wide)]) for v in parts
+    ]
+
+
+def tie(values, after, scalars):
+    ins = [pltpu.with_memory_space_constraint(v, pltpu.HBM) for v in (*values, *after)]
+    return pl.pallas_call(
+        pass_on,
+        out_shape=tuple(shaped(v.shape, v.dtype) for v in values),
+        in_specs=[pl.BlockSpec(memory_space=pltpu.SMEM)]
+        + [pl.BlockSpec(memory_space=pltpu.HBM) for _ in ins],
+        out_specs=tuple(pl.BlockSpec(memory_space=pltpu.HBM) for _ in values),
+        input_output_aliases={index + 1: index for index in range(len(values))},
+    )(scalars, *ins)
+
+
+def add_core_units(keep, send, scalars, wide):
     back = lax.ppermute(send, "wide", [(i, i ^ 1) for i in range(wide)])
-    four = shaped((4, rows, 128), bf16)
-    one = shaped((rows, 128), bf16)
-    own, across = call(add_cores, (four, four), (keep, back), scalars)
+    four = shaped((4, keep.shape[1], 128), bf16)
+    return call(add_cores, (four, four), (keep, back), scalars)
+
+
+def add_far_units(own, across, scalars, wide):
     back = lax.ppermute(across, "wide", [(i, i ^ 2) for i in range(wide)])
+    one = shaped((own.shape[1], 128), bf16)
     parts = call(add_sides, (one,) * 4, (own, back), scalars)
     return [parts[0]] + [
         lax.ppermute(parts[step], "wide", [(i, i ^ (4 * step)) for i in range(wide)])
@@ -912,10 +1074,10 @@
     ]
 
 
-def sum_vectors(terms, wide):
-    for step in (1, 2, 4, 8):
-        terms = terms + lax.ppermute(terms, "wide", [(i, i ^ step) for i in range(wide)])
-    return terms
+def gather_vectors(rows, wide):
+    rows = jnp.stack((rows, lax.ppermute(rows, "wide", [(i, i ^ 1) for i in range(wide)])))
+    rows = jnp.concatenate((rows, lax.ppermute(rows, "wide", [(i, i ^ 2) for i in range(wide)])))
+    return along_depth(rows, wide)
 
 
 def per_device(
@@ -958,35 +1120,35 @@
     half_plane = shaped((HALF, PIX), bf16)
     rows_scratch = pltpu.VMEM((PIX + 16, C), f32)
 
-    vec_half = jnp.pad(vectors, ((0, 3), (0, 0)))
-    vec_other = lax.ppermute(vec_half, "narrow", flip)
-    vecs = jnp.where(
-        narrow_at == 0,
-        jnp.concatenate((vec_half, vec_other), axis=1),
-        jnp.concatenate((vec_other, vec_half), axis=1),
-    )
     mask = jnp.broadcast_to(valid_mask[0].astype(f32)[:, None], (PIX, 128))
     own_features = features[0]
     own_cotangent = cotangent[0]
-    other_features = lax.ppermute(own_features, "narrow", flip)
+    (exchange,) = call(
+        pack_exchange, (shaped((HALF + 16, PIX), bf16),), (own_features, vectors), scalars
+    )
+    other_features = lax.ppermute(exchange, "narrow", flip)
 
     if unit_path:
         (unit_first,) = call(
-            pack_first, (shaped((336, 128), bf16),), (conv_first,), scalars
-        )
-        first_ones, first_twos = gather_units(unit_first, 224, wide)
+            pack_first,
+            (shaped((FIRST_ROWS, 128), bf16),),
+            (jnp.transpose(conv_first),),
+            scalars,
+        )
+        depth_first = along_depth(unit_first, wide)
         (unit_second,) = call(
             pack_second,
-            (shaped((SHARED_AT + SECOND_ROWS, 128), bf16),),
+            (shaped((SECOND_ROWS, 128), bf16),),
             (
-                conv_second,
-                jnp.transpose(film_weight, (1, 0, 2)),
+                jnp.transpose(conv_second),
+                film_weight,
+                embedding,
                 jnp.transpose(attend_in, (1, 0, 2)),
                 attend_out,
             ),
             scalars,
         )
-        second_ones, second_twos = gather_units(unit_second, SHARED_AT, wide)
+        first_units = both_cores(gather_rest(depth_first, (unit_second,), scalars, wide), wide)
     else:
 
         def whole(array, axis):
@@ -997,22 +1159,37 @@
         film_full = whole(film_weight, 2).reshape(EMB, 2 * C)
         in_full = whole(attend_in, 2).reshape(C, 3 * C)
         out_full = whole(attend_out, 1)
-    other_cotangent = lax.ppermute(own_cotangent, "narrow", flip)
-
-    turned, taps_one, stat_one = call(
+
+    turned, taps_one, stat_one, vecs, cotangent_copy = call(
         first_norm,
-        (low_plane, taps, stats),
-        (own_features, other_features, mask, vecs),
+        (low_plane, taps, stats, vec_rows, half_plane),
+        (own_features, other_features, mask, vectors, own_cotangent),
         scalars,
         (rows_scratch, pltpu.VMEM((PIX, C), f32)),
-    )
+        far=(first_units[0],) if unit_path else (),
+        flops=4 * 10**9,
+    )
+    other_cotangent = lax.ppermute(cotangent_copy, "narrow", flip)
     if unit_path:
+        (unit_second,) = tie((unit_second,), (first_units[0],), scalars)
+        depth_second = along_depth(unit_second, wide)
+        second_parts = gather_rest(
+            depth_second, (*first_units[1:4], other_cotangent), scalars, wide
+        )
         out_one, kernel_one, stat_two = call(
             first_conv,
             (plane, kernel, stats),
-            (taps_one, mask, vecs, *first_ones, *first_twos),
+            (taps_one, mask, vecs),
             scalars,
-            flops=2 * 9 * C * C * PIX,
+            (
+                pltpu.VMEM((8, 4, FIRST_ROWS, 128), bf16),
+                pltpu.SemaphoreType.DMA((8,)),
+            ),
+            far=(*first_units, second_parts[0]),
+            flops=10**10,
+        )
+        second_units = both_cores(
+            [second_parts[0], *tie(second_parts[1:4], (stat_two,), scalars)], wide
         )
     else:
         kernel_one = first_full
@@ -1020,16 +1197,67 @@
             first_conv_plain, (plane, stats), (taps_one, mask, vecs, kernel_one), scalars
         )
     common = (out_one, stat_two, turned, mask, vecs, embedding)
-    scratch = (pltpu.VMEM((16, EMB), f32), rows_scratch)
+    attention_scratch = (
+        pltpu.VMEM((C, 3 * C), f32),
+        pltpu.VMEM((C, C), f32),
+        pltpu.VMEM((C, 1536), bf16),
+        pltpu.VMEM((512, C), bf16),
+        *([pltpu.VMEM((PIX, 512), bf16)] * 3),
+        *([pltpu.VMEM((512, PIX), bf16)] * 5),
+        pltpu.VMEM((PIX, 128), f32),
+        pltpu.VMEM((PIX, 128), f32),
+        pltpu.VMEM((PIX, C), bf16),
+        rows_scratch,
+        pltpu.VMEM((9 * C, 256), f32),
+        pltpu.VMEM((PIX, 256), bf16),
+    )
+    back_scratch = (pltpu.VMEM((PIX, C), f32), rows_scratch)
+    terms_scratch = (pltpu.VMEM((PADDED, 256), bf16), pltpu.VMEM((9 * C, 256), f32))
     if unit_path:
-        taps_two, residual, hidden, stat_three, film_rows, kernel_two = call(
-            second_conv,
-            (taps, plane, low_plane, stats, stats, kernel),
-            common + (*second_ones, *second_twos),
+        units = shaped((8, 512, 128), bf16)
+        (
+            output, direct, taps_back, vec_grad, film_rows, kernel_two, soft_all, keep, send,
+        ) = call(
+            middle_of_block,
+            (
+                half_plane, plane, taps, vec_rows, stats, kernel, shaped((16, EMB), f32),
+                units, units,
+            ),
+            common + (own_cotangent, other_cotangent),
             scalars,
-            scratch + (pltpu.VMEM((EMB, 2 * C), bf16),),
-            flops=2 * 9 * C * C * PIX,
-        )
+            (
+                pltpu.VMEM((PADDED, 3 * C), bf16),
+                pltpu.VMEM((PIX, C), f32),
+                pltpu.VMEM((PIX, C), bf16),
+                pltpu.VMEM((8, C), f32),
+                pltpu.VMEM((16, EMB), f32),
+                pltpu.VMEM((EMB, 2 * C), bf16),
+                pltpu.VMEM((8, 4, SECOND_ROWS, 128), bf16),
+                pltpu.SemaphoreType.DMA((8,)),
+                pltpu.VMEM((PADDED, 256), bf16),
+                *attention_scratch,
+            ),
+            far=second_units,
+            flops=4 * 10**10,
+        )
+        own_second, across_second = add_core_units(keep, send, scalars, wide)
+        units = shaped((8, 336, 128), bf16)
+        taps_back_one, vec_grad, keep, send = call(
+            second_back,
+            (taps, vec_rows, units, units),
+            (
+                taps_back, kernel_two, out_one, stat_two, film_rows, mask, vecs, vec_grad,
+                taps_one,
+            ),
+            scalars,
+            back_scratch + terms_scratch,
+            far=(across_second,),
+            flops=10**10,
+        )
+        own_first, across_first = add_core_units(keep, send, scalars, wide)
+        parts_second = add_far_units(own_second, across_second, scalars, wide)
+        parts_first = add_far_units(own_first, across_first, scalars, wide)
+        started = (across_first,)
     else:
         kernel_two = second_full
         taps_two, residual, hidden, stat_three, film_rows = call(
@@ -1037,126 +1265,107 @@
             (taps, plane, low_plane, stats, stats),
             common + (kernel_two, film_full),
             scalars,
-            scratch,
-        )
-    common = (hidden, residual, stat_three, mask, vecs, own_cotangent, other_cotangent)
-    padded = pltpu.VMEM((PIX, 512), bf16)
-    scratch = (
-        pltpu.VMEM((C, 3 * C), f32),
-        pltpu.VMEM((C, C), f32),
-        pltpu.VMEM((C, 1536), bf16),
-        pltpu.VMEM((512, C), bf16),
-        *([padded] * 8),
-        pltpu.VMEM((PIX, 128), f32),
-        pltpu.VMEM((PIX, 128), f32),
-        pltpu.VMEM((PIX, C), bf16),
-        rows_scratch,
-        pltpu.VMEM((C, PIX), f32),
-        pltpu.VMEM((PIX, 256), bf16),
-    )
-    flops = 2 * HEADS * PIX * PIX * 128 * 6
-    if unit_path:
-        units = shaped((8, 176, 128), bf16)
-        output, direct, taps_back, back_two, vec_grad, keep_att, send_att = call(
-            attention,
-            (half_plane, plane, taps, back_half, vec_rows, units, units),
-            common + tuple(second_twos),
-            scalars,
-            scratch,
-            flops=flops,
-        )
-        units = shaped((8, 336, 128), bf16)
-        keep, send = call(
-            conv_terms,
-            (units, units),
-            (taps_two, back_two),
-            scalars,
-            (pltpu.VMEM((9 * C, 256), f32),),
-            flops=2 * 9 * C * 256 * PIX,
-        )
-        parts_second = reduce_units(
-            jnp.concatenate((keep, keep_att), axis=1),
-            jnp.concatenate((send, send_att), axis=1),
-            scalars,
-            wide,
-        )
-    else:
+            (pltpu.VMEM((16, EMB), f32), rows_scratch),
+        )
         output, direct, taps_back, back_two, vec_grad, in_term, out_term = call(
             attention_plain,
             (
                 half_plane, plane, taps, back_half, vec_rows,
                 shaped((C, 768), f32), shaped((C, 256), f32),
             ),
-            common + (in_full, out_full),
+            (
+                hidden, residual, stat_three, mask, vecs, own_cotangent, other_cotangent,
+                in_full, out_full,
+            ),
             scalars,
-            scratch,
+            attention_scratch,
         )
         (second_term,) = call(
             conv_terms_plain, (shaped((9 * C, 256), f32),), (taps_two, back_two), scalars
         )
-    taps_back_one, back_one, vec_grad = call(
-        second_back,
-        (taps, back_half, vec_rows),
-        (taps_back, kernel_two, out_one, stat_two, film_rows, mask, vecs, vec_grad),
-        scalars,
-        (pltpu.VMEM((PIX, C), f32), rows_scratch),
-        flops=2 * 9 * C * C * PIX,
-    )
-    if unit_path:
-        units = shaped((8, 336, 128), bf16)
-        keep, send = call(
-            conv_terms,
-            (units, units),
-            (taps_one, back_one),
+        taps_back_one, back_one, vec_grad = call(
+            second_back_plain,
+            (taps, back_half, vec_rows),
+            (taps_back, kernel_two, out_one, stat_two, film_rows, mask, vecs, vec_grad),
             scalars,
-            (pltpu.VMEM((9 * C, 256), f32),),
-            flops=2 * 9 * C * 256 * PIX,
-        )
-        parts_first = reduce_units(keep, send, scalars, wide)
-    else:
+            back_scratch,
+        )
         (first_term,) = call(
             conv_terms_plain, (shaped((9 * C, 256), f32),), (taps_one, back_one), scalars
         )
-    soft = jax.nn.silu(embedding.astype(f32)).astype(bf16)
-    soft_all = lax.all_gather(soft, "wide", axis=0, tiled=True)
-    rows_here = film_weight.shape[0]
-    soft_here = lax.dynamic_slice_in_dim(soft_all, wide_at * rows_here, rows_here, axis=1)
-    film_term = lax.dynamic_slice_in_dim(vec_grad[11:13], narrow_at * HALF, HALF, axis=1)
-    film_all = lax.all_gather(film_term.astype(bf16)[None], "wide", axis=0, tiled=True)
-    film_gradient = jnp.einsum("se,stj->etj", soft_here, film_all, preferred_element_type=f32)
-
-    input_gradient, vec_grad = call(
+        started = ()
+    input_gradient, vec_half = call(
         first_back,
-        (half_plane, vec_rows),
+        (half_plane, shaped((16, 256), f32)),
         (taps_back_one, kernel_one, turned, stat_one, direct, mask, vecs, vec_grad),
         scalars,
         (pltpu.VMEM((PIX, C), f32), pltpu.VMEM((C, PIX), f32)),
-        flops=2 * 9 * C * C * PIX,
-    )
-    vec_half = lax.dynamic_slice_in_dim(vec_grad, narrow_at * HALF, HALF, axis=1)
+        far=started,
+        flops=10**10,
+    )
     if unit_path:
-        vec_sum = sum_vectors(vec_half, wide)[:13]
+        vec_shape, film_shape = shaped((13, HALF), f32), shaped(film_weight.shape, f32)
+        small = call(
+            finish_small,
+            (vec_shape,) * 4 + (film_shape,) * 4,
+            (
+                *gather_vectors(vec_half, wide),
+                soft_all,
+                vectors,
+                vectors_moment,
+                vectors_square,
+                film_weight,
+                film_weight_moment,
+                film_weight_square,
+            ),
+            scalars,
+            (pltpu.VMEM((EMB, 512), f32),),
+        )
+        vec_results, film_results = small[:4], small[4:]
     else:
-        vec_sum = lax.psum(vec_half, "wide")[:13]
+        vec_half = vec_half[:13, :HALF]
+        vec_sum = lax.psum(vec_half, "wide")
+        soft = jax.nn.silu(embedding.astype(f32)).astype(bf16)
+        soft_all = lax.all_gather(soft, "wide", axis=0, tiled=True)
+        rows_here = film_weight.shape[0]
+        soft_here = lax.dynamic_slice_in_dim(soft_all, wide_at * rows_here, rows_here, axis=1)
+        film_all = lax.all_gather(vec_half[11:13].astype(bf16)[None], "wide", axis=0, tiled=True)
+        film_gradient = jnp.einsum("se,stj->etj", soft_here, film_all, preferred_element_type=f32)
 
     rates = step_rates()
-    shard = shaped(conv_first.shape, f32)
+    shard = shaped((HALF, ROWS), f32)
+
+    def turned_shards(*shards):
+        return tuple(jnp.transpose(v) for v in shards)
+
     if unit_path:
+        in_shape, out_shape = shaped((3, 24, HALF), f32), shaped((24, HALF), f32)
+        in_given = tuple(
+            jnp.transpose(v, (1, 0, 2)) for v in (attend_in, attend_in_moment, attend_in_square)
+        )
         second_results = call(
             finish_second,
-            (shard,) * 4 + (shaped((3, 24, HALF), f32), shaped((24, HALF), f32)),
-            (*parts_second, conv_second, conv_second_moment, conv_second_square),
+            (shard,) * 4 + (in_shape,) * 4 + (out_shape,) * 4,
+            (
+                *parts_second,
+                *turned_shards(conv_second, conv_second_moment, conv_second_square),
+                *in_given,
+                attend_out,
+                attend_out_moment,
+                attend_out_square,
+            ),
             scalars,
         )
-        in_gradient = jnp.transpose(second_results[4], (1, 0, 2))
-        out_gradient = second_results[5]
-        second_results = second_results[:4]
+        in_results = tuple(jnp.transpose(v, (1, 0, 2)) for v in second_results[4:8])
+        out_results = second_results[8:12]
+        second_results = turned_shards(*second_results[:4])
         first_results = call(
             finish_first,
             (shard,) * 4,
-            (*parts_first, conv_first, conv_first_moment, conv_first_square),
+            (*parts_first, *turned_shards(conv_first, conv_first_moment, conv_first_square)),
             scalars,
         )
+        first_results = turned_shards(*first_results)
     else:
 
         def scatter(term):
@@ -1166,25 +1375,36 @@
         second_gradient = scatter(second_term[:, :HALF])
         in_gradient = scatter(in_term.reshape(C, 3, 256)[:, :, :HALF])
         out_gradient = scatter(out_term[:, :HALF])
-        first_results = (first_gradient,) + adam_update(
+
+        def finish(weight, gradient, moment, square, rate):
+            return (gradient,) + adam_update(weight, gradient, moment, square, rate)
+
+        first_results = finish(
             conv_first, first_gradient, conv_first_moment, conv_first_square, rates[0]
         )
-        second_results = (second_gradient,) + adam_update(
+        second_results = finish(
             conv_second, second_gradient, conv_second_moment, conv_second_square, rates[1]
         )
-
-    def finish(weight, gradient, moment, square, rate):
-        return (gradient,) + adam_update(weight, gradient, moment, square, rate)
+        film_results = finish(
+            film_weight, film_gradient, film_weight_moment, film_weight_square, rates[2]
+        )
+        in_results = finish(
+            attend_in, in_gradient, attend_in_moment, attend_in_square, rates[3]
+        )
+        out_results = finish(
+            attend_out, out_gradient, attend_out_moment, attend_out_square, rates[4]
+        )
+        vec_results = finish(vectors, vec_sum, vectors_moment, vectors_square, rates[5])
 
     return (
         output[None],
         input_gradient[None],
         *first_results,
         *second_results,
-        *finish(film_weight, film_gradient, film_weight_moment, film_weight_square, rates[2]),
-        *finish(attend_in, in_gradient, attend_in_moment, attend_in_square, rates[3]),
-        *finish(attend_out, out_gradient, attend_out_moment, attend_out_square, rates[4]),
-        *finish(vectors, vec_sum, vectors_moment, vectors_square, rates[5]),
+        *film_results,
+        *in_results,
+        *out_results,
+        *vec_results,
     )
 
 

time: 306 us -> 216 us (0.71)
  the two profiles are of different devices: /device:TPU:21 before, /device:TPU:0 now
where the time goes in v2:
time: 216 us; the launch traced here: 213 us
  Pallas kernels  96 us (44%)
  waiting for transfers between devices  48.8 us (23%)
  starting transfers between devices  42.7 us (20%)
  local copies, waits for them, and re-layouts  23.5 us (11%)
    pallas_call x17, Pallas kernels, call(): pl.pallas_call(body, out_shape=tuple(outs), in_specs=[pl.BlockSpec(memory...  94.7 us
    unnamed x134, local copies, waits for them, and re-layouts  23.3 us
    ppermute x2, waiting for transfers between devices, gather_rest(): lax.ppermute(whole, 'narrow', [(0, 1), (1, 0)])  19.4 us
    ppermute x9, starting transfers between devices, along_depth(): lax.ppermute(unit, 'wide', [(i, i ^ 4 * step) for i in range(wide)])  15.3 us
    ppermute x6, starting transfers between devices, add_far_units(): lax.ppermute(parts[step], 'wide', [(i, i ^ 4 * step) for i in range(wide)])  10.9 us
    ppermute x9, waiting for transfers between devices, along_depth(): lax.ppermute(unit, 'wide', [(i, i ^ 4 * step) for i in range(wide)])  7.58 us
    ppermute x1, waiting for transfers between devices, per_device(): other_cotangent = lax.ppermute(cotangent_copy, 'narrow', flip)  5.69 us
  transfers between devices with their start and end apart: 37, of which 17 were waited for; matrix products, arithmetic and copies ran while one was open for 0% of the time, Pallas kernels for 14%

profile of v2, /device:TPU:0, one launch (start us, length us, event | category | flops | bytes accessed | tf_op | source)
XLA Modules:
  0.0 212.5 jit_solution(1917491000780731929)
XLA Ops:
  3.1 3.0 %collective-permute-start = (bf16[208,1024]{1,0:T(8,128)(2,1)S(1)}, bf16[208,1024]{1,0:T(8,128)(2,1)S(1)}, u32[]{:S(2)}, u32[]{:S(2)}) collective-permute-start(bf16[208,1024]{1,0:T(8,128)(2,1)S(1)} %shard_map.413), channel_id=1, source_target_pairs={{0,1},{1,0},{2,3},{3,2},{4,5},{5,4},{6,7},{7,6},{8,9},{9,8},{10,11... | collective-permute-start | bytes 1277960 | tf_op jit(solution)/shard_map/ppermute | solution.py:1129
  7.8 3.7 %collective-permute-start.3 = (bf16[336,128]{1,0:T(8,128)(2,1)S(1)}, bf16[336,128]{1,0:T(8,128)(2,1)S(1)}, u32[]{:S(2)}, u32[]{:S(2)}) collective-permute-start(bf16[336,128]{1,0:T(8,128)(2,1)S(1)} %shard_map.414.refs_0_), channel_id=1, source_target_pairs={{0,24},{2,26},{4,28},{6,30},{8,16},{10,18},{12,20},{14,22},{16,8},... | collective-permute-start | bytes 258056 | tf_op jit(solution)/shard_map/ppermute | solution.py:1026
  20.4 3.1 %collective-permute-start.13 = (bf16[672,128]{1,0:T(8,128)(2,1)}, bf16[672,128]{1,0:T(8,128)(2,1)S(1)}, u32[]{:S(2)}, u32[]{:S(2)}) collective-permute-start(bf16[672,128]{1,0:T(8,128)(2,1)} %shard_map.418.refs_0_), channel_id=1, source_target_pairs={{0,24},{2,26},{4,28},{6,30},{8,16},{10,18},{12,20},{14,22},{16,8},... | collective-permute-start | bytes 516104 | tf_op jit(solution)/shard_map/ppermute | solution.py:1026
  26.3 3.5 %collective-permute-done.13.refs_3_ = bf16[672,128]{1,0:T(8,128)(2,1)S(1)} collective-permute-done((bf16[672,128]{1,0:T(8,128)(2,1)}, bf16[672,128]{1,0:T(8,128)(2,1)S(1)}, u32[]{:S(2)}, u32[]{:S(2)}) %collective-permute-start.13) | collective-permute-done | bytes 172064 | tf_op jit(solution)/shard_map/ppermute | solution.py:1026
  32.8 3.2 %shard_map.417 = (bf16[1024,384]{1,0:T(8,128)(2,1)S(1)}, bf16[1088,1152]{1,0:T(8,128)(2,1)S(1)}, f32[8,384]{1,0:T(8,128)S(1)}, f32[16,384]{1,0:T(8,128)S(1)}, bf16[192,1024]{1,0:T(8,128)(2,1)S(1)}) custom-call(s32[4]{0:T(128)S(1)} %copy-done.22, bf16[192,1024]{1,0:T(8,128)(2,1)S(1)} %bitcast.37, bf16[208,1024]{1,0:T(8,128)(2,1)S(1)} %collective-permute-done.other_ref, ...), custom_call_target="tpu_custom_call" | custom-call | flops 4000000000 | bytes 1024 | tf_op jit(solution)/shard_map/pallas_call | solution.py:56
  38.4 6.0 %collective-permute-done.5.refs_5_.refs_2_ = bf16[4,336,128]{2,1,0:T(8,128)(2,1)S(1)} collective-permute-done((bf16[4,336,128]{2,1,0:T(8,128)(2,1)}, bf16[4,336,128]{2,1,0:T(8,128)(2,1)S(1)}, u32[]{:S(2)}, u32[]{:S(2)}) %collective-permute-start.5) | collective-permute-done | bytes 344096 | tf_op jit(solution)/shard_map/ppermute | solution.py:1038
  44.9 5.7 %collective-permute-done.14.refs_7_.other_ref = bf16[192,1024]{1,0:T(8,128)(2,1)S(1)} collective-permute-done((bf16[192,1024]{1,0:T(8,128)(2,1)S(1)}, bf16[192,1024]{1,0:T(8,128)(2,1)S(1)}, u32[]{:S(2)}, u32[]{:S(2)}) %collective-permute-start.14) | collective-permute-done | bytes 393248 | tf_op jit(solution)/shard_map/ppermute | solution.py:1172
  56.4 8.7 %shard_map.420 = (f32[1024,384]{1,0:T(8,128)S(1)}, bf16[3456,384]{1,0:T(8,128)(2,1)S(1)}, f32[8,384]{1,0:T(8,128)S(1)}) custom-call(s32[4]{0:T(128)S(1)} %copy-done.23, bf16[1088,1152]{1,0:T(8,128)(2,1)S(1)} %get-tuple-element.88.taps_ref.refs_8_, f32[1024,128]{1,0:T(8,128)S(1)} %broadcast_in_dim.12.mask_ref.refs_5_, ...), custom_call_target="tpu_custom_call" | custom-call | flops 10000000000 | bytes 1024 | tf_op jit(solution)/shard_map/pallas_call | solution.py:56
  71.3 13.3 %collective-permute-done.16.refs_1_ = bf16[4,672,128]{2,1,0:T(8,128)(2,1)S(1)} collective-permute-done((bf16[4,672,128]{2,1,0:T(8,128)(2,1)S(1)}, bf16[4,672,128]{2,1,0:T(8,128)(2,1)S(1)}, u32[]{:S(2)}, u32[]{:S(2)}) %collective-permute-start.16) | collective-permute-done | bytes 688160 | tf_op jit(solution)/shard_map/ppermute | solution.py:1038
  94.5 51.7 %shard_map.422 = (bf16[192,1024]{1,0:T(8,128)(2,1)}, f32[1024,384]{1,0:T(8,128)S(1)}, bf16[1088,1152]{1,0:T(8,128)(2,1)}, f32[16,384]{1,0:T(8,128)S(1)}, f32[8,3...) custom-call(s32[4]{0:T(128)S(1)} %copy-done.24, ...), custom_call_target="tpu_custom_call" | custom-call | flops 40000000000 | bytes 1024 | tf_op jit(solution)/shard_map/pallas_call | solution.py:56
  146.4 2.5 %collective-permute-done.22.back_ref = bf16[8,512,128]{2,1,0:T(8,128)(2,1)S(1)} collective-permute-done((bf16[8,512,128]{2,1,0:T(8,128)(2,1)S(1)}, bf16[8,512,128]{2,1,0:T(8,128)(2,1)S(1)}, u32[]{:S(2)}, u32[]{:S(2)}) %collective-permute-start.22) | collective-permute-done | bytes 1048608 | tf_op jit(solution)/shard_map/ppermute | solution.py:1062
  154.0 11.0 %shard_map.424 = (bf16[1088,1152]{1,0:T(8,128)(2,1)S(1)}, f32[16,384]{1,0:T(8,128)S(1)}, bf16[8,336,128]{2,1,0:T(8,128)(2,1)S(1)}, bf16[8,336,128]{2,1,0:T(8,128)(2,1)S(1)}) custom-call(s32[4]{0:T(128)S(1)} %copy-done.24, bf16[1088,1152]{1,0:T(8,128)(2,1)S(1)} %copy-done.48, bf16[3456,384]{1,0:T(8,128)(2,1)S(1)} %copy-done.47, f32[1024,384]{1,0:T(8,128)S(1)} %copy-done.52, ...), custom_call_target="tpu_custom_call" | custom-call | flops 10000000000 | bytes 1024 | tf_op jit(solution)/shard_map/pallas_call | solution.py:56
  169.5 8.7 %shard_map.426 = (bf16[192,1024]{1,0:T(8,128)(2,1)}, f32[16,256]{1,0:T(8,128)S(1)}) custom-call(s32[4]{0:T(128)S(1)} %copy-done.24, bf16[1088,1152]{1,0:T(8,128)(2,1)S(1)} %get-tuple-element.105.taps_ref, bf16[3456,384]{1,0:T(8,128)(2,1)S(1)} %copy-done.50, bf16[1024,384]{1,0:T(8,128)(2,1)S(1)} %get-tuple-element.93.turned_ref, ...), custom_call_target="tpu_custom_call" | custom-call | flops 10000000000 | bytes 1024 | tf_op jit(solution)/shard_map/pallas_call | solution.py:56
  181.2 2.3 %collective-permute-start.30 = (bf16[512,128]{1,0:T(8,128)(2,1)S(1)}, bf16[512,128]{1,0:T(8,128)(2,1)S(1)}, u32[]{:S(2)}, u32[]{:S(2)}) collective-permute-start(bf16[512,128]{1,0:T(8,128)(2,1)S(1)} %get-tuple-element.126), channel_id=1, source_target_pairs={{0,16},{2,18},{4,20},{6,22},{8,24},{10,26},{12,28},{14,30},{16,0},... | collective-permute-start | bytes 393224 | tf_op jit(solution)/shard_map/ppermute | solution.py:1072
  185.3 2.1 %collective-permute-done.33 = f32[2,16,256]{2,1,0:T(8,128)S(1)} collective-permute-done((f32[2,16,256]{2,1,0:T(8,128)S(1)}, f32[2,16,256]{2,1,0:T(8,128)S(1)}, u32[]{:S(2)}, u32[]{:S(2)}) %collective-permute-start.33) | collective-permute-done | bytes 32800 | tf_op jit(solution)/shard_map/ppermute | solution.py:1079
  187.4 2.1 collective-permute-start.36
  190.3 2.3 %collective-permute-start.26 = (bf16[336,128]{1,0:T(8,128)(2,1)S(1)}, bf16[336,128]{1,0:T(8,128)(2,1)S(1)}, u32[]{:S(2)}, u32[]{:S(2)}) collective-permute-start(bf16[336,128]{1,0:T(8,128)(2,1)S(1)} %get-tuple-element.117), channel_id=1, source_target_pairs={{0,16},{2,18},{4,20},{6,22},{8,24},{10,26},{12,28},{14,30},{16,0},... | collective-permute-start | bytes 258056 | tf_op jit(solution)/shard_map/ppermute | solution.py:1072
  192.5 3.7 %collective-permute-done.30.refs_2_ = bf16[512,128]{1,0:T(8,128)(2,1)S(1)} collective-permute-done((bf16[512,128]{1,0:T(8,128)(2,1)S(1)}, bf16[512,128]{1,0:T(8,128)(2,1)S(1)}, u32[]{:S(2)}, u32[]{:S(2)}) %collective-permute-start.30) | collective-permute-done | bytes 131104 | tf_op jit(solution)/shard_map/ppermute | solution.py:1072
  196.2 4.1 %collective-permute-start.27 = (bf16[336,128]{1,0:T(8,128)(2,1)S(1)}, bf16[336,128]{1,0:T(8,128)(2,1)S(1)}, u32[]{:S(2)}, u32[]{:S(2)}) collective-permute-start(bf16[336,128]{1,0:T(8,128)(2,1)S(1)} %get-tuple-element.118), channel_id=1, source_target_pairs={{0,24},{2,26},{4,28},{6,30},{8,16},{10,18},{12,20},{14,22},{16,8},... | collective-permute-start | bytes 258056 | tf_op jit(solution)/shard_map/ppermute | solution.py:1072
  200.3 1.9 collective-permute-start.35
  202.2 2.4 %collective-permute-start.34 = (f32[4,16,256]{2,1,0:T(8,128)S(1)}, f32[4,16,256]{2,1,0:T(8,128)S(1)}, u32[]{:S(2)}, u32[]{:S(2)}) collective-permute-start(f32[4,16,256]{2,1,0:T(8,128)S(1)} %pad_maximum_fusion.own_ref), channel_id=1, source_target_pairs={{0,8},{2,10},{4,12},{6,14},{8,0},{10,2},{12,4},{14,6},{16,24},{18,... | collective-permute-start | bytes 196616 | tf_op jit(solution)/shard_map/ppermute | solution.py:1026
  204.7 1.8 shard_map.430
  206.5 2.1 %collective-permute-done.35.two_ref = f32[4,16,256]{2,1,0:T(8,128)S(1)} collective-permute-done((f32[4,16,256]{2,1,0:T(8,128)S(1)}, f32[4,16,256]{2,1,0:T(8,128)S(1)}, u32[]{:S(2)}, u32[]{:S(2)}) %collective-permute-start.35) | collective-permute-done | bytes 65568 | tf_op jit(solution)/shard_map/ppermute | solution.py:1026
  208.7 2.0 shard_map.431
  (208 shorter events, 60.1 us)
Async XLA Ops:
  3.1 27.3 %collective-permute-start = (bf16[208,1024]{1,0:T(8,128)(2,1)S(1)}, bf16[208,1024]{1,0:T(8,128)(2,1)S(1)}, u32[]{:S(2)}, u32[]{:S(2)}) collective-permute-start(bf16[208,1024]{1,0:T(8,128)(2,1)S(1)} %shard_map.413), channel_id=1, source_target_pairs={{0,1},{1,0},{2,3},{3,2},{4,5},{5,4},{6,7},{7,6},{8,9},{9,8},{10,11... | collective-permute-start | bytes 1277960 | tf_op jit(solution)/shard_map/ppermute | solution.py:1129
  7.8 10.1 %collective-permute-start.3 = (bf16[336,128]{1,0:T(8,128)(2,1)S(1)}, bf16[336,128]{1,0:T(8,128)(2,1)S(1)}, u32[]{:S(2)}, u32[]{:S(2)}) collective-permute-start(bf16[336,128]{1,0:T(8,128)(2,1)S(1)} %shard_map.414.refs_0_), channel_id=1, source_target_pairs={{0,24},{2,26},{4,28},{6,30},{8,16},{10,18},{12,20},{14,22},{16,8},... | collective-permute-start | bytes 258056 | tf_op jit(solution)/shard_map/ppermute | solution.py:1026
  23.5 13.8 %collective-permute-start.12 = (bf16[672,128]{1,0:T(8,128)(2,1)}, bf16[672,128]{1,0:T(8,128)(2,1)S(1)}, u32[]{:S(2)}, u32[]{:S(2)}) collective-permute-start(bf16[672,128]{1,0:T(8,128)(2,1)} %shard_map.418.refs_0_), channel_id=1, source_target_pairs={{0,16},{2,18},{4,20},{6,22},{8,24},{10,26},{12,28},{14,30},{16,0},... | collective-permute-start | bytes 516104 | tf_op jit(solution)/shard_map/ppermute | solution.py:1026
  23.5 14.3 %collective-permute-start.11 = (bf16[672,128]{1,0:T(8,128)(2,1)}, bf16[672,128]{1,0:T(8,128)(2,1)S(1)}, u32[]{:S(2)}, u32[]{:S(2)}) collective-permute-start(bf16[672,128]{1,0:T(8,128)(2,1)} %shard_map.418.refs_0_), channel_id=1, source_target_pairs={{0,8},{2,10},{4,12},{6,14},{8,0},{10,2},{12,4},{14,6},{16,24},{18,... | collective-permute-start | bytes 516104 | tf_op jit(solution)/shard_map/ppermute | solution.py:1026
  24.8 13.0 %collective-permute-start.6 = (bf16[4,336,128]{2,1,0:T(8,128)(2,1)}, bf16[4,336,128]{2,1,0:T(8,128)(2,1)S(1)}, u32[]{:S(2)}, u32[]{:S(2)}) collective-permute-start(bf16[4,336,128]{2,1,0:T(8,128)(2,1)} %copy-done.2), channel_id=1, source_target_pairs={{0,5},{1,4},{2,7},{3,6},{4,1},{5,0},{6,3},{7,2},{8,13},{9,12},{10,... | collective-permute-start | bytes 1032200 | tf_op jit(solution)/shard_map/ppermute | solution.py:1039
  29.8 14.6 %collective-permute-start.5 = (bf16[4,336,128]{2,1,0:T(8,128)(2,1)}, bf16[4,336,128]{2,1,0:T(8,128)(2,1)S(1)}, u32[]{:S(2)}, u32[]{:S(2)}) collective-permute-start(bf16[4,336,128]{2,1,0:T(8,128)(2,1)} %copy-done.2), channel_id=1, source_target_pairs={{0,1},{1,0},{2,3},{3,2},{4,5},{5,4},{6,7},{7,6},{8,9},{9,8},{10,11... | collective-permute-start | bytes 1032200 | tf_op jit(solution)/shard_map/ppermute | solution.py:1038
  30.4 14.0 %collective-permute-start.4 = (bf16[4,336,128]{2,1,0:T(8,128)(2,1)}, bf16[4,336,128]{2,1,0:T(8,128)(2,1)S(1)}, u32[]{:S(2)}, u32[]{:S(2)}) collective-permute-start(bf16[4,336,128]{2,1,0:T(8,128)(2,1)} %copy-done.2), channel_id=1, source_target_pairs={{0,4},{2,6},{4,0},{6,2},{8,12},{10,14},{12,8},{14,10},{16,20},{18,... | collective-permute-start | bytes 1032200 | tf_op jit(solution)/shard_map/ppermute | solution.py:1037
  37.3 13.3 %collective-permute-start.14 = (bf16[192,1024]{1,0:T(8,128)(2,1)S(1)}, bf16[192,1024]{1,0:T(8,128)(2,1)S(1)}, u32[]{:S(2)}, u32[]{:S(2)}) collective-permute-start(bf16[192,1024]{1,0:T(8,128)(2,1)S(1)} %get-tuple-element.90), channel_id=1, source_target_pairs={{0,1},{1,0},{2,3},{3,2},{4,5},{5,4},{6,7},{7,6},{8,9},{9,8},{10,11... | collective-permute-start | bytes 1179656 | tf_op jit(solution)/shard_map/ppermute | solution.py:1172
  37.8 14.2 %collective-permute-start.7 = (bf16[4,336,128]{2,1,0:T(8,128)(2,1)S(1)}, bf16[4,336,128]{2,1,0:T(8,128)(2,1)S(1)}, u32[]{:S(2)}, u32[]{:S(2)}) collective-permute-start(bf16[4,336,128]{2,1,0:T(8,128)(2,1)S(1)} %copy-done.3), channel_id=1, source_target_pairs={{0,2},{2,0},{4,6},{6,4},{8,10},{10,8},{12,14},{14,12},{16,18},{18,... | collective-permute-start | bytes 1032200 | tf_op jit(solution)/shard_map/ppermute | solution.py:1045
  37.9 14.5 %collective-permute-start.10 = (bf16[4,336,128]{2,1,0:T(8,128)(2,1)S(1)}, bf16[4,336,128]{2,1,0:T(8,128)(2,1)S(1)}, u32[]{:S(2)}, u32[]{:S(2)}) collective-permute-start(bf16[4,336,128]{2,1,0:T(8,128)(2,1)S(1)} %collective-permute-done.6.refs_6_.refs_3_), channel_id=1, source_target_pairs={{0,2},{2,0},{4,6},{6,4},{8,10},{10,8},{12,14},{14,12},{16,18},{18,... | collective-permute-start | bytes 1032200 | tf_op jit(solution)/shard_map/ppermute | solution.py:1045
  44.4 9.7 %collective-permute-start.9 = (bf16[4,336,128]{2,1,0:T(8,128)(2,1)S(1)}, bf16[4,336,128]{2,1,0:T(8,128)(2,1)S(1)}, u32[]{:S(2)}, u32[]{:S(2)}) collective-permute-start(bf16[4,336,128]{2,1,0:T(8,128)(2,1)S(1)} %collective-permute-done.5.refs_5_.refs_2_), channel_id=1, source_target_pairs={{0,2},{2,0},{4,6},{6,4},{8,10},{10,8},{12,14},{14,12},{16,18},{18,... | collective-permute-start | bytes 1032200 | tf_op jit(solution)/shard_map/ppermute | solution.py:1045
  44.4 11.2 %collective-permute-start.8 = (bf16[4,336,128]{2,1,0:T(8,128)(2,1)S(1)}, bf16[4,336,128]{2,1,0:T(8,128)(2,1)S(1)}, u32[]{:S(2)}, u32[]{:S(2)}) collective-permute-start(bf16[4,336,128]{2,1,0:T(8,128)(2,1)S(1)} %collective-permute-done.4.refs_4_.refs_1_), channel_id=1, source_target_pairs={{0,2},{2,0},{4,6},{6,4},{8,10},{10,8},{12,14},{14,12},{16,18},{18,... | collective-permute-start | bytes 1032200 | tf_op jit(solution)/shard_map/ppermute | solution.py:1045
  52.0 35.8 %collective-permute-start.18 = (bf16[4,672,128]{2,1,0:T(8,128)(2,1)S(1)}, bf16[4,672,128]{2,1,0:T(8,128)(2,1)}, u32[]{:S(2)}, u32[]{:S(2)}) collective-permute-start(bf16[4,672,128]{2,1,0:T(8,128)(2,1)S(1)} %shard_map.419.refs_8_.refs_0_), channel_id=1, source_target_pairs={{0,2},{2,0},{4,6},{6,4},{8,10},{10,8},{12,14},{14,12},{16,18},{18,... | collective-permute-start | bytes 2064392 | tf_op jit(solution)/shard_map/ppermute | solution.py:1045
  52.1 19.2 %collective-permute-start.17 = (bf16[4,672,128]{2,1,0:T(8,128)(2,1)S(1)}, bf16[4,672,128]{2,1,0:T(8,128)(2,1)S(1)}, u32[]{:S(2)}, u32[]{:S(2)}) collective-permute-start(bf16[4,672,128]{2,1,0:T(8,128)(2,1)S(1)} %shard_map.419.refs_8_.refs_0_), channel_id=1, source_target_pairs={{0,5},{1,4},{2,7},{3,6},{4,1},{5,0},{6,3},{7,2},{8,13},{9,12},{10,... | collective-permute-start | bytes 2064392 | tf_op jit(solution)/shard_map/ppermute | solution.py:1039
  52.4 32.3 %collective-permute-start.16 = (bf16[4,672,128]{2,1,0:T(8,128)(2,1)S(1)}, bf16[4,672,128]{2,1,0:T(8,128)(2,1)S(1)}, u32[]{:S(2)}, u32[]{:S(2)}) collective-permute-start(bf16[4,672,128]{2,1,0:T(8,128)(2,1)S(1)} %shard_map.419.refs_8_.refs_0_), channel_id=1, source_target_pairs={{0,1},{1,0},{2,3},{3,2},{4,5},{5,4},{6,7},{7,6},{8,9},{9,8},{10,11... | collective-permute-start | bytes 2064392 | tf_op jit(solution)/shard_map/ppermute | solution.py:1038
  54.1 31.4 %collective-permute-start.15 = (bf16[4,672,128]{2,1,0:T(8,128)(2,1)S(1)}, bf16[4,672,128]{2,1,0:T(8,128)(2,1)S(1)}, u32[]{:S(2)}, u32[]{:S(2)}) collective-permute-start(bf16[4,672,128]{2,1,0:T(8,128)(2,1)S(1)} %shard_map.419.refs_8_.refs_0_), channel_id=1, source_target_pairs={{0,4},{2,6},{4,0},{6,2},{8,12},{10,14},{12,8},{14,10},{16,20},{18,... | collective-permute-start | bytes 2064392 | tf_op jit(solution)/shard_map/ppermute | solution.py:1037
  165.1 15.0 %collective-permute-start.28 = (bf16[4,512,128]{2,1,0:T(8,128)(2,1)S(1)}, bf16[4,512,128]{2,1,0:T(8,128)(2,1)S(1)}, u32[]{:S(2)}, u32[]{:S(2)}) collective-permute-start(bf16[4,512,128]{2,1,0:T(8,128)(2,1)S(1)} %copy-done.42), channel_id=1, source_target_pairs={{0,4},{2,6},{4,0},{6,2},{8,12},{10,14},{12,8},{14,10},{16,20},{18,... | collective-permute-start | bytes 1572872 | tf_op jit(solution)/shard_map/ppermute | solution.py:1068
  167.9 21.7 %collective-permute-start.24 = (bf16[4,336,128]{2,1,0:T(8,128)(2,1)S(1)}, bf16[4,336,128]{2,1,0:T(8,128)(2,1)S(1)}, u32[]{:S(2)}, u32[]{:S(2)}) collective-permute-start(bf16[4,336,128]{2,1,0:T(8,128)(2,1)S(1)} %get-tuple-element.112.refs_0_), channel_id=1, source_target_pairs={{0,4},{2,6},{4,0},{6,2},{8,12},{10,14},{12,8},{14,10},{16,20},{18,... | collective-permute-start | bytes 1032200 | tf_op jit(solution)/shard_map/ppermute | solution.py:1068
  181.2 15.0 %collective-permute-start.30 = (bf16[512,128]{1,0:T(8,128)(2,1)S(1)}, bf16[512,128]{1,0:T(8,128)(2,1)S(1)}, u32[]{:S(2)}, u32[]{:S(2)}) collective-permute-start(bf16[512,128]{1,0:T(8,128)(2,1)S(1)} %get-tuple-element.126), channel_id=1, source_target_pairs={{0,16},{2,18},{4,20},{6,22},{8,24},{10,26},{12,28},{14,30},{16,0},... | collective-permute-start | bytes 393224 | tf_op jit(solution)/shard_map/ppermute | solution.py:1072
  183.6 16.7 %collective-permute-start.31 = (bf16[512,128]{1,0:T(8,128)(2,1)S(1)}, bf16[512,128]{1,0:T(8,128)(2,1)S(1)}, u32[]{:S(2)}, u32[]{:S(2)}) collective-permute-start(bf16[512,128]{1,0:T(8,128)(2,1)S(1)} %get-tuple-element.127), channel_id=1, source_target_pairs={{0,24},{2,26},{4,28},{6,30},{8,16},{10,18},{12,20},{14,22},{16,8},... | collective-permute-start | bytes 393224 | tf_op jit(solution)/shard_map/ppermute | solution.py:1072
  187.4 14.8 %collective-permute-start.36 = (f32[4,16,256]{2,1,0:T(8,128)S(1)}, f32[4,16,256]{2,1,0:T(8,128)S(1)}, u32[]{:S(2)}, u32[]{:S(2)}) collective-permute-start(f32[4,16,256]{2,1,0:T(8,128)S(1)} %pad_maximum_fusion.own_ref), channel_id=1, source_target_pairs={{0,24},{2,26},{4,28},{6,30},{8,16},{10,18},{12,20},{14,22},{16,8},... | collective-permute-start | bytes 196616 | tf_op jit(solution)/shard_map/ppermute | solution.py:1026
  190.2 20.5 %collective-permute-start.25 = (bf16[336,128]{1,0:T(8,128)(2,1)S(1)}, bf16[336,128]{1,0:T(8,128)(2,1)S(1)}, u32[]{:S(2)}, u32[]{:S(2)}) collective-permute-start(bf16[336,128]{1,0:T(8,128)(2,1)S(1)} %get-tuple-element.116), channel_id=1, source_target_pairs={{0,8},{2,10},{4,12},{6,14},{8,0},{10,2},{12,4},{14,6},{16,24},{18,... | collective-permute-start | bytes 258056 | tf_op jit(solution)/shard_map/ppermute | solution.py:1072
  190.3 20.4 %collective-permute-start.26 = (bf16[336,128]{1,0:T(8,128)(2,1)S(1)}, bf16[336,128]{1,0:T(8,128)(2,1)S(1)}, u32[]{:S(2)}, u32[]{:S(2)}) collective-permute-start(bf16[336,128]{1,0:T(8,128)(2,1)S(1)} %get-tuple-element.117), channel_id=1, source_target_pairs={{0,16},{2,18},{4,20},{6,22},{8,24},{10,26},{12,28},{14,30},{16,0},... | collective-permute-start | bytes 258056 | tf_op jit(solution)/shard_map/ppermute | solution.py:1072
  196.2 14.5 %collective-permute-start.27 = (bf16[336,128]{1,0:T(8,128)(2,1)S(1)}, bf16[336,128]{1,0:T(8,128)(2,1)S(1)}, u32[]{:S(2)}, u32[]{:S(2)}) collective-permute-start(bf16[336,128]{1,0:T(8,128)(2,1)S(1)} %get-tuple-element.118), channel_id=1, source_target_pairs={{0,24},{2,26},{4,28},{6,30},{8,16},{10,18},{12,20},{14,22},{16,8},... | collective-permute-start | bytes 258056 | tf_op jit(solution)/shard_map/ppermute | solution.py:1072
  (80 other events, 1084.8 us)

commit v3 on v2

--- a/solution.py
+++ b/solution.py
@@ -251,7 +251,8 @@
     return jnp.concatenate((one, two[0 : rows - top]), axis=0)
 
 
-def pack_exchange(at, features_ref, vec_ref, out_ref):
+def pack_exchange(at, features_ref, vec_ref, cot_ref, out_ref):
+    out_ref[HALF + 16 : 2 * HALF + 16, :] = cot_ref[...]
     out_ref[0:HALF, :] = features_ref[...]
     vec = jnp.concatenate((vec_ref[...], jnp.zeros((3, HALF), f32)), axis=0)
     coarse = vec.astype(bf16)
@@ -260,19 +261,15 @@
     out_ref[HALF : HALF + 16, 256 : 256 + HALF] = (vec - coarse.astype(f32)).astype(bf16)
 
 
-def pack_first(at, conv_ref, out_ref):
-    part, shared = tile_parts(conv_ref[...].T, at[0])
-    out_ref[0:224, :] = pad_rows(part, 224).astype(bf16)
-    out_ref[224:336, :] = pair_rows(shared, 112).astype(bf16)
-
-
 FIRST_ROWS = 336
 FILM_AT, FILM_SHARED, EMBED_AT, IN_AT, IN_SHARED, OUT_AT, OUT_SHARED, SECOND_ROWS = 336, 432, 480, 496, 576, 624, 656, 672
 
 
-def stack(at, *refs):
+def stack_all(at, *refs):
+    first_ref, second_ref = refs[4:6]
     for step in range(4):
-        refs[-1][step] = refs[step][...]
+        first_ref[step] = refs[step][0:FIRST_ROWS, :]
+        second_ref[step] = refs[step][FIRST_ROWS : FIRST_ROWS + SECOND_ROWS, :]
 
 
 def pass_on(at, *refs):
@@ -284,28 +281,41 @@
     out_ref[start : start + rows, :] = pad_rows(block, rows).astype(bf16)
 
 
-def pack_second(at, conv_ref, film_ref, embed_ref, in_ref, out_weight_ref, out_ref):
+def pack_weights(at, embed_ref, *refs):
+    unit_ref, first_ref, second_ref, film_ref, in_ref, out_ref, sems = refs[5:]
     narrow = at[0]
+    copies = [
+        pltpu.make_async_copy(source, target, sems.at[index])
+        for index, (source, target) in enumerate(
+            zip(refs[0:5], (first_ref, second_ref, film_ref, in_ref, out_ref))
+        )
+    ]
+    for copy in copies:
+        copy.start()
     embed = embed_ref[...].astype(f32)
     put_rows(
-        out_ref,
-        EMBED_AT,
+        unit_ref,
+        FIRST_ROWS + EMBED_AT,
         jnp.concatenate([embed[:, 128 * i : 128 * i + 128] for i in range(EMB // 128)], axis=0),
     )
-    part, shared = tile_parts(conv_ref[...].T, narrow)
-    put_rows(out_ref, 0, part)
-    put_rows(out_ref, 224, pair_rows(shared, 112))
-    part, shared = tile_parts(
-        jnp.concatenate((film_ref[:, 0, :], film_ref[:, 1, :]), axis=0), narrow
-    )
-    put_rows(out_ref, FILM_AT, part)
-    put_rows(out_ref, FILM_SHARED, pair_rows(shared, 48))
-    part, shared = tile_parts(jnp.concatenate((in_ref[0], in_ref[1], in_ref[2]), axis=0), narrow)
-    put_rows(out_ref, IN_AT, part)
-    put_rows(out_ref, IN_SHARED, pair_rows(shared, 40))
-    part, shared = tile_parts(out_weight_ref[...], narrow)
-    put_rows(out_ref, OUT_AT, part)
-    put_rows(out_ref, OUT_SHARED, pair_rows(shared, 16))
+    copies[0].wait()
+    part, shared = tile_parts(first_ref[...].T, narrow)
+    put_rows(unit_ref, 0, part)
+    put_rows(unit_ref, 224, pair_rows(shared, 112))
+    for copy in copies[1:]:
+        copy.wait()
+    for block, start, shared_start, top in (
+        (second_ref[...].T, 0, 224, 112),
+        (
+            jnp.concatenate((film_ref[:, 0, :], film_ref[:, 1, :]), axis=0),
+            FILM_AT, FILM_SHARED, 48,
+        ),
+        (jnp.concatenate((in_ref[0], in_ref[1], in_ref[2]), axis=0), IN_AT, IN_SHARED, 40),
+        (out_ref[...], OUT_AT, OUT_SHARED, 16),
+    ):
+        part, shared = tile_parts(block, narrow)
+        put_rows(unit_ref, FIRST_ROWS + start, part)
+        put_rows(unit_ref, FIRST_ROWS + shared_start, pair_rows(shared, top))
 
 
 class Gathered:
@@ -437,10 +447,9 @@
     return jnp.concatenate((jnp.where(lane(block.shape[0]) < HEAD, one, two), two), axis=1)
 
 
-def first_norm(at, own_ref, other_ref, mask_ref, vec_own_ref, cot_ref, *refs):
-    turned_ref, taps_ref, stat_ref, vec_ref, cot_out_ref, rows_ref, raw_ref = refs[-7:]
+def first_norm(at, own_ref, other_ref, mask_ref, vec_own_ref, *refs):
+    turned_ref, taps_ref, stat_ref, vec_ref, rows_ref, raw_ref = refs[-6:]
     narrow = at[0]
-    cot_out_ref[...] = cot_ref[...]
     own = vec_own_ref[...]
     other = (
         other_ref[HALF : HALF + 16, 0:HALF].astype(f32)
@@ -631,7 +640,7 @@
         weight_ref[128 * head : 128 * head + HEAD, :] = out_nat[HEAD * head : HEAD * head + HEAD, :].astype(bf16)
         weight_ref[128 * head + HEAD : 128 * head + 128, :] = blank
     own = own_ref[...].astype(f32)
-    other = other_ref[...].astype(f32)
+    other = other_ref[HALF + 16 : 2 * HALF + 16, :].astype(f32)
     low = jnp.where(narrow == 0, own, other)
     high = jnp.where(narrow == 0, other, own)
     zero = jnp.zeros((8, C), f32)
@@ -830,7 +839,8 @@
 
 
 def second_back(at, *refs):
-    taps_one_ref, back_taps_ref, vec_grad_ref, keep_ref, send_ref = refs[8:9] + refs[-8:-4]
+    taps_one_ref = refs[8]
+    back_taps_ref, vec_grad_ref, keep_ref, send_ref = refs[-8:-4]
     grad_ref, rows_ref, back_ref, terms_ref = refs[-4:]
     second_back_body(at, *refs[:8], back_taps_ref, back_ref, vec_grad_ref, grad_ref, rows_ref)
     kernel_terms(taps_one_ref, back_ref, terms_ref)
@@ -1028,15 +1038,13 @@
     ]
 
 
-def gather_rest(depth, after, scalars, wide):
-    (whole,) = call(stack, (shaped((4, *depth[0].shape), bf16),), depth, scalars, far=after)
-    both = ("wide", "narrow")
+def along_plane(stack, wide):
     diagonal = [(2 * i + x, 2 * (i ^ 2) + 1 - x) for i in range(wide) for x in (0, 1)]
     return [
-        whole,
-        lax.ppermute(whole, "wide", [(i, i ^ 2) for i in range(wide)]),
-        lax.ppermute(whole, "narrow", [(0, 1), (1, 0)]),
-        lax.ppermute(whole, both, diagonal),
+        stack,
+        lax.ppermute(stack, "wide", [(i, i ^ 2) for i in range(wide)]),
+        lax.ppermute(stack, "narrow", [(0, 1), (1, 0)]),
+        lax.ppermute(stack, ("wide", "narrow"), diagonal),
     ]
 
 
@@ -1124,31 +1132,36 @@
     own_features = features[0]
     own_cotangent = cotangent[0]
     (exchange,) = call(
-        pack_exchange, (shaped((HALF + 16, PIX), bf16),), (own_features, vectors), scalars
-    )
-    other_features = lax.ppermute(exchange, "narrow", flip)
+        pack_exchange,
+        (shaped((2 * HALF + 16, PIX), bf16),),
+        (own_features, vectors, own_cotangent),
+        scalars,
+    )
+    exchanged = lax.ppermute(exchange, "narrow", flip)
 
     if unit_path:
-        (unit_first,) = call(
-            pack_first,
-            (shaped((FIRST_ROWS, 128), bf16),),
-            (jnp.transpose(conv_first),),
+        weights = (
+            jnp.transpose(conv_first),
+            jnp.transpose(conv_second),
+            film_weight,
+            jnp.transpose(attend_in, (1, 0, 2)),
+            attend_out,
+        )
+        (unit,) = call(
+            pack_weights,
+            (shaped((FIRST_ROWS + SECOND_ROWS, 128), bf16),),
+            (embedding,),
             scalars,
-        )
-        depth_first = along_depth(unit_first, wide)
-        (unit_second,) = call(
-            pack_second,
-            (shaped((SECOND_ROWS, 128), bf16),),
-            (
-                jnp.transpose(conv_second),
-                film_weight,
-                embedding,
-                jnp.transpose(attend_in, (1, 0, 2)),
-                attend_out,
-            ),
+            tuple(pltpu.VMEM(v.shape, f32) for v in weights) + (pltpu.SemaphoreType.DMA((5,)),),
+            far=weights,
+        )
+        first_stack, second_stack = call(
+            stack_all,
+            tuple(shaped((4, rows, 128), bf16) for rows in (FIRST_ROWS, SECOND_ROWS)),
+            along_depth(unit, wide),
             scalars,
         )
-        first_units = both_cores(gather_rest(depth_first, (unit_second,), scalars, wide), wide)
+        first_units = both_cores(along_plane(first_stack, wide), wide)
     else:
 
         def whole(array, axis):
@@ -1160,22 +1173,16 @@
         in_full = whole(attend_in, 2).reshape(C, 3 * C)
         out_full = whole(attend_out, 1)
 
-    turned, taps_one, stat_one, vecs, cotangent_copy = call(
+    turned, taps_one, stat_one, vecs = call(
         first_norm,
-        (low_plane, taps, stats, vec_rows, half_plane),
-        (own_features, other_features, mask, vectors, own_cotangent),
+        (low_plane, taps, stats, vec_rows),
+        (own_features, exchanged, mask, vectors),
         scalars,
         (rows_scratch, pltpu.VMEM((PIX, C), f32)),
-        far=(first_units[0],) if unit_path else (),
-        flops=4 * 10**9,
-    )
-    other_cotangent = lax.ppermute(cotangent_copy, "narrow", flip)
+        far=(first_stack,) if unit_path else (),
+    )
     if unit_path:
-        (unit_second,) = tie((unit_second,), (first_units[0],), scalars)
-        depth_second = along_depth(unit_second, wide)
-        second_parts = gather_rest(
-            depth_second, (*first_units[1:4], other_cotangent), scalars, wide
-        )
+        second_parts = along_plane(second_stack, wide)
         out_one, kernel_one, stat_two = call(
             first_conv,
             (plane, kernel, stats),
@@ -1185,12 +1192,10 @@
                 pltpu.VMEM((8, 4, FIRST_ROWS, 128), bf16),
                 pltpu.SemaphoreType.DMA((8,)),
             ),
-            far=(*first_units, second_parts[0]),
-            flops=10**10,
-        )
-        second_units = both_cores(
-            [second_parts[0], *tie(second_parts[1:4], (stat_two,), scalars)], wide
-        )
+            far=(*first_units, second_stack),
+        )
+        arrived = [tie((part,), (stat_two,), scalars)[0] for part in second_parts[1:4]]
+        second_units = both_cores([second_parts[0], *arrived], wide)
     else:
         kernel_one = first_full
         out_one, stat_two = call(
@@ -1223,7 +1228,7 @@
                 half_plane, plane, taps, vec_rows, stats, kernel, shaped((16, EMB), f32),
                 units, units,
             ),
-            common + (own_cotangent, other_cotangent),
+            common + (own_cotangent, exchanged),
             scalars,
             (
                 pltpu.VMEM((PADDED, 3 * C), bf16),
@@ -1252,10 +1257,9 @@
             scalars,
             back_scratch + terms_scratch,
             far=(across_second,),
-            flops=10**10,
-        )
+        )
+        parts_second = add_far_units(own_second, across_second, scalars, wide)
         own_first, across_first = add_core_units(keep, send, scalars, wide)
-        parts_second = add_far_units(own_second, across_second, scalars, wide)
         parts_first = add_far_units(own_first, across_first, scalars, wide)
         started = (across_first,)
     else:
@@ -1274,7 +1278,7 @@
                 shaped((C, 768), f32), shaped((C, 256), f32),
             ),
             (
-                hidden, residual, stat_three, mask, vecs, own_cotangent, other_cotangent,
+                hidden, residual, stat_three, mask, vecs, own_cotangent, exchanged,
                 in_full, out_full,
             ),
             scalars,
@@ -1301,7 +1305,6 @@
         scalars,
         (pltpu.VMEM((PIX, C), f32), pltpu.VMEM((C, PIX), f32)),
         far=started,
-        flops=10**10,
     )
     if unit_path:
         vec_shape, film_shape = shaped((13, HALF), f32), shaped(film_weight.shape, f32)

time: 216 us -> 208 us (0.963)
  local copies, waits for them, and re-layouts: 23.5 us -> 17.4 us
  starting transfers between devices: 42.7 us -> 38 us
  waiting for transfers between devices: 48.8 us -> 51.3 us
    ppermute x9 -> x6, waiting for transfers between devices: 7.58 us -> 18.6 us  [along_depth(): lax.ppermute(unit, 'wide', [(i, i ^ 4 * step) for i in range(wide)])]
    ppermute x8 -> x7, waiting for transfers between devices: 27.5 us -> 20.8 us  [the longest x2 16.8 us: along_plane(): lax.ppermute(stack, ('wide', 'narrow'), diagonal)]
    unnamed x134 -> x104, local copies, waits for them, and re-layouts: 23.3 us -> 17.2 us
    ppermute x9 -> x6, starting transfers between devices: 15.3 us -> 11.8 us  [along_depth(): lax.ppermute(unit, 'wide', [(i, i ^ 4 * step) for i in range(wide)])]
    ppermute x8 -> x7, starting transfers between devices: 10.6 us -> 9.18 us  [the longest x2 3.36 us: along_plane(): lax.ppermute(stack, ('wide', 'narrow'), diagonal)]
    pallas_call x17 -> x15, Pallas kernels: 94.7 us -> 95.1 us  [call(): pl.pallas_call(body, out_shape=tuple(outs), in_specs=[pl.BlockSpec(memory...]
  transfers between devices with their start and end apart: 37 -> 33, of which waited for: 17 -> 12; matrix products, arithmetic and copies ran while one was open for 0% -> 0% of each run, Pallas kernels for 14% -> 15%
where the time goes in v3:
time: 208 us; the launch traced here: 206 us
  Pallas kernels  97.3 us (47%)
  waiting for transfers between devices  51.3 us (25%)
  starting transfers between devices  38 us (18%)
  local copies, waits for them, and re-layouts  17.4 us (8%)
    pallas_call x15, Pallas kernels, call(): pl.pallas_call(body, out_shape=tuple(outs), in_specs=[pl.BlockSpec(memory...  95.1 us
    ppermute x6, waiting for transfers between devices, along_depth(): lax.ppermute(unit, 'wide', [(i, i ^ 4 * step) for i in range(wide)])  18.6 us
    unnamed x104, local copies, waits for them, and re-layouts  17.2 us
    ppermute x2, waiting for transfers between devices, along_plane(): lax.ppermute(stack, ('wide', 'narrow'), diagonal)  16.8 us
    ppermute x6, starting transfers between devices, along_depth(): lax.ppermute(unit, 'wide', [(i, i ^ 4 * step) for i in range(wide)])  11.8 us
    ppermute x6, starting transfers between devices, add_far_units(): lax.ppermute(parts[step], 'wide', [(i, i ^ 4 * step) for i in range(wide)])  11.6 us
  transfers between devices with their start and end apart: 33, of which 12 were waited for; matrix products, arithmetic and copies ran while one was open for 0% of the time, Pallas kernels for 15%

profile of v3, /device:TPU:0, one launch (start us, length us, event | category | flops | bytes accessed | tf_op | source)
XLA Modules:
  0.0 205.6 jit_solution(733502918311660260)
XLA Ops:
  1.5 2.0 shard_map.414.refs_0_
  3.5 5.1 %collective-permute-start.3 = (bf16[1008,128]{1,0:T(8,128)(2,1)S(1)}, bf16[1008,128]{1,0:T(8,128)(2,1)S(1)}, u32[]{:S(2)}, u32[]{:S(2)}) collective-permute-start(bf16[1008,128]{1,0:T(8,128)(2,1)S(1)} %shard_map.414.refs_0_), channel_id=1, source_target_pairs={{0,24},{2,26},{4,28},{6,30},{8,16},{10,18},{12,20},{14,22},{16,8},... | collective-permute-start | bytes 774152 | tf_op jit(solution)/shard_map/ppermute | solution.py:1036
  15.8 14.8 %collective-permute-done.2.refs_2_ = bf16[1008,128]{1,0:T(8,128)(2,1)S(1)} collective-permute-done((bf16[1008,128]{1,0:T(8,128)(2,1)S(1)}, bf16[1008,128]{1,0:T(8,128)(2,1)S(1)}, u32[]{:S(2)}, u32[]{:S(2)}) %collective-permute-start.2) | collective-permute-done | bytes 258080 | tf_op jit(solution)/shard_map/ppermute | solution.py:1036
  32.0 2.4 %collective-permute-start.6 = (bf16[4,336,128]{2,1,0:T(8,128)(2,1)S(1)}, bf16[4,336,128]{2,1,0:T(8,128)(2,1)S(1)}, u32[]{:S(2)}, u32[]{:S(2)}) collective-permute-start(bf16[4,336,128]{2,1,0:T(8,128)(2,1)S(1)} %get-tuple-element.86.refs_0_), channel_id=1, source_target_pairs={{0,5},{1,4},{2,7},{3,6},{4,1},{5,0},{6,3},{7,2},{8,13},{9,12},{10,... | collective-permute-start | bytes 1032200 | tf_op jit(solution)/shard_map/ppermute | solution.py:1047
  35.5 8.4 %collective-permute-done.6.refs_3_ = bf16[4,336,128]{2,1,0:T(8,128)(2,1)S(1)} collective-permute-done((bf16[4,336,128]{2,1,0:T(8,128)(2,1)S(1)}, bf16[4,336,128]{2,1,0:T(8,128)(2,1)S(1)}, u32[]{:S(2)}, u32[]{:S(2)}) %collective-permute-start.6) | collective-permute-done | bytes 344096 | tf_op jit(solution)/shard_map/ppermute | solution.py:1047
  45.6 3.9 %collective-permute-done.5.refs_2_ = bf16[4,336,128]{2,1,0:T(8,128)(2,1)S(1)} collective-permute-done((bf16[4,336,128]{2,1,0:T(8,128)(2,1)S(1)}, bf16[4,336,128]{2,1,0:T(8,128)(2,1)S(1)}, u32[]{:S(2)}, u32[]{:S(2)}) %collective-permute-start.5) | collective-permute-done | bytes 344096 | tf_op jit(solution)/shard_map/ppermute | solution.py:1046
  52.7 3.2 %shard_map.416 = (bf16[1024,384]{1,0:T(8,128)(2,1)S(1)}, bf16[1088,1152]{1,0:T(8,128)(2,1)S(1)}, f32[8,384]{1,0:T(8,128)S(1)}, f32[16,384]{1,0:T(8,128)S(1)}) custom-call(s32[4]{0:T(128)S(1)} %pad_add_fusion.at, bf16[192,1024]{1,0:T(8,128)(2,1)S(1)} %bitcast.33, bf16[400,1024]{1,0:T(8,128)(2,1)S(1)} %collective-permute-done.other_ref, ...), custom_call_target="tpu_custom_call" | custom-call | bytes 1024 | tf_op jit(solution)/shard_map/pallas_call | solution.py:56
  57.6 8.6 %shard_map.417 = (f32[1024,384]{1,0:T(8,128)S(1)}, bf16[3456,384]{1,0:T(8,128)(2,1)S(1)}, f32[8,384]{1,0:T(8,128)S(1)}) custom-call(s32[4]{0:T(128)S(1)} %pad_add_fusion.at, bf16[1088,1152]{1,0:T(8,128)(2,1)S(1)} %get-tuple-element.87.taps_ref.refs_8_, f32[1024,128]{1,0:T(8,128)S(1)} %broadcast_in_dim.12.mask_ref.refs_5_, ...), custom_call_target="tpu_custom_call" | custom-call | bytes 1024 | tf_op jit(solution)/shard_map/pallas_call | solution.py:56
  71.7 8.4 %collective-permute-done.13.refs_0_ = bf16[4,672,128]{2,1,0:T(8,128)(2,1)} collective-permute-done((bf16[4,672,128]{2,1,0:T(8,128)(2,1)}, bf16[4,672,128]{2,1,0:T(8,128)(2,1)}, u32[]{:S(2)}, u32[]{:S(2)}) %collective-permute-start.13) | collective-permute-done | bytes 688160 | tf_op jit(solution)/shard_map/ppermute | solution.py:1047
  80.9 2.3 %collective-permute-done.17.refs_7_ = bf16[4,672,128]{2,1,0:T(8,128)(2,1)S(1)} collective-permute-done((bf16[4,672,128]{2,1,0:T(8,128)(2,1)}, bf16[4,672,128]{2,1,0:T(8,128)(2,1)S(1)}, u32[]{:S(2)}, u32[]{:S(2)}) %collective-permute-start.17) | collective-permute-done | bytes 688160 | tf_op jit(solution)/shard_map/ppermute | solution.py:1053
  87.7 51.3 %shard_map.421 = (bf16[192,1024]{1,0:T(8,128)(2,1)}, f32[1024,384]{1,0:T(8,128)S(1)}, bf16[1088,1152]{1,0:T(8,128)(2,1)}, f32[16,384]{1,0:T(8,128)S(1)}, f32[8,3...) custom-call(s32[4]{0:T(128)S(1)} %copy-done.29, ...), custom_call_target="tpu_custom_call" | custom-call | flops 40000000000 | bytes 1024 | tf_op jit(solution)/shard_map/pallas_call | solution.py:56
  139.3 2.5 %collective-permute-done.18.back_ref = bf16[8,512,128]{2,1,0:T(8,128)(2,1)S(1)} collective-permute-done((bf16[8,512,128]{2,1,0:T(8,128)(2,1)S(1)}, bf16[8,512,128]{2,1,0:T(8,128)(2,1)S(1)}, u32[]{:S(2)}, u32[]{:S(2)}) %collective-permute-start.18) | collective-permute-done | bytes 1048608 | tf_op jit(solution)/shard_map/ppermute | solution.py:1070
  146.9 10.9 %shard_map.423 = (bf16[1088,1152]{1,0:T(8,128)(2,1)S(1)}, f32[16,384]{1,0:T(8,128)S(1)}, bf16[8,336,128]{2,1,0:T(8,128)(2,1)S(1)}, bf16[8,336,128]{2,1,0:T(8,128)(2,1)S(1)}) custom-call(s32[4]{0:T(128)S(1)} %copy-done.29, bf16[1088,1152]{1,0:T(8,128)(2,1)S(1)} %copy-done.3, bf16[3456,384]{1,0:T(8,128)(2,1)S(1)} %copy-done.2, f32[1024,384]{1,0:T(8,128)S(1)} %copy-done.7, ...), custom_call_target="tpu_custom_call" | custom-call | bytes 1024 | tf_op jit(solution)/shard_map/pallas_call | solution.py:56
  162.5 8.7 %shard_map.425 = (bf16[192,1024]{1,0:T(8,128)(2,1)}, f32[16,256]{1,0:T(8,128)S(1)}) custom-call(s32[4]{0:T(128)S(1)} %copy-done.29, bf16[1088,1152]{1,0:T(8,128)(2,1)S(1)} %get-tuple-element.101.taps_ref, bf16[3456,384]{1,0:T(8,128)(2,1)S(1)} %copy-done.1, bf16[1024,384]{1,0:T(8,128)(2,1)S(1)} %copy-done.12, f32[8,384]{1,0:T(8,128)S(1)} %get-tuple-element.103.stat_ref, ...), custom_call_target="tpu_custom_call" | custom-call | bytes 1024 | tf_op jit(solution)/shard_map/pallas_call | solution.py:56
  173.9 2.7 %collective-permute-start.26 = (bf16[512,128]{1,0:T(8,128)(2,1)S(1)}, bf16[512,128]{1,0:T(8,128)(2,1)S(1)}, u32[]{:S(2)}, u32[]{:S(2)}) collective-permute-start(bf16[512,128]{1,0:T(8,128)(2,1)S(1)} %get-tuple-element.122), channel_id=1, source_target_pairs={{0,16},{2,18},{4,20},{6,22},{8,24},{10,26},{12,28},{14,30},{16,0},... | collective-permute-start | bytes 393224 | tf_op jit(solution)/shard_map/ppermute | solution.py:1080
  178.3 2.0 collective-permute-done.29
  180.3 2.1 %collective-permute-start.32 = (f32[4,16,256]{2,1,0:T(8,128)S(1)}, f32[4,16,256]{2,1,0:T(8,128)S(1)}, u32[]{:S(2)}, u32[]{:S(2)}) collective-permute-start(f32[4,16,256]{2,1,0:T(8,128)S(1)} %pad_maximum_fusion.own_ref), channel_id=1, source_target_pairs={{0,24},{2,26},{4,28},{6,30},{8,16},{10,18},{12,20},{14,22},{16,8},... | collective-permute-start | bytes 196616 | tf_op jit(solution)/shard_map/ppermute | solution.py:1036
  183.2 2.3 %collective-permute-start.22 = (bf16[336,128]{1,0:T(8,128)(2,1)S(1)}, bf16[336,128]{1,0:T(8,128)(2,1)S(1)}, u32[]{:S(2)}, u32[]{:S(2)}) collective-permute-start(bf16[336,128]{1,0:T(8,128)(2,1)S(1)} %get-tuple-element.113), channel_id=1, source_target_pairs={{0,16},{2,18},{4,20},{6,22},{8,24},{10,26},{12,28},{14,30},{16,0},... | collective-permute-start | bytes 258056 | tf_op jit(solution)/shard_map/ppermute | solution.py:1080
  185.4 3.3 %collective-permute-done.26.refs_2_ = bf16[512,128]{1,0:T(8,128)(2,1)S(1)} collective-permute-done((bf16[512,128]{1,0:T(8,128)(2,1)S(1)}, bf16[512,128]{1,0:T(8,128)(2,1)S(1)}, u32[]{:S(2)}, u32[]{:S(2)}) %collective-permute-start.26) | collective-permute-done | bytes 131104 | tf_op jit(solution)/shard_map/ppermute | solution.py:1080
  188.8 4.8 %collective-permute-start.23 = (bf16[336,128]{1,0:T(8,128)(2,1)S(1)}, bf16[336,128]{1,0:T(8,128)(2,1)S(1)}, u32[]{:S(2)}, u32[]{:S(2)}) collective-permute-start(bf16[336,128]{1,0:T(8,128)(2,1)S(1)} %get-tuple-element.114), channel_id=1, source_target_pairs={{0,24},{2,26},{4,28},{6,30},{8,16},{10,18},{12,20},{14,22},{16,8},... | collective-permute-start | bytes 258056 | tf_op jit(solution)/shard_map/ppermute | solution.py:1080
  193.5 1.9 collective-permute-start.31
  195.4 2.0 collective-permute-start.30
  199.3 2.3 %collective-permute-done.31.two_ref = f32[4,16,256]{2,1,0:T(8,128)S(1)} collective-permute-done((f32[4,16,256]{2,1,0:T(8,128)S(1)}, f32[4,16,256]{2,1,0:T(8,128)S(1)}, u32[]{:S(2)}, u32[]{:S(2)}) %collective-permute-start.31) | collective-permute-done | bytes 65568 | tf_op jit(solution)/shard_map/ppermute | solution.py:1036
  201.7 2.0 shard_map.430
  (169 shorter events, 45.9 us)
Async XLA Ops:
  3.5 12.3 %collective-permute-start.3 = (bf16[1008,128]{1,0:T(8,128)(2,1)S(1)}, bf16[1008,128]{1,0:T(8,128)(2,1)S(1)}, u32[]{:S(2)}, u32[]{:S(2)}) collective-permute-start(bf16[1008,128]{1,0:T(8,128)(2,1)S(1)} %shard_map.414.refs_0_), channel_id=1, source_target_pairs={{0,24},{2,26},{4,28},{6,30},{8,16},{10,18},{12,20},{14,22},{16,8},... | collective-permute-start | bytes 774152 | tf_op jit(solution)/shard_map/ppermute | solution.py:1036
  8.6 22.0 %collective-permute-start.2 = (bf16[1008,128]{1,0:T(8,128)(2,1)S(1)}, bf16[1008,128]{1,0:T(8,128)(2,1)S(1)}, u32[]{:S(2)}, u32[]{:S(2)}) collective-permute-start(bf16[1008,128]{1,0:T(8,128)(2,1)S(1)} %shard_map.414.refs_0_), channel_id=1, source_target_pairs={{0,16},{2,18},{4,20},{6,22},{8,24},{10,26},{12,28},{14,30},{16,0},... | collective-permute-start | bytes 774152 | tf_op jit(solution)/shard_map/ppermute | solution.py:1036
  8.6 22.0 %collective-permute-start.1 = (bf16[1008,128]{1,0:T(8,128)(2,1)S(1)}, bf16[1008,128]{1,0:T(8,128)(2,1)S(1)}, u32[]{:S(2)}, u32[]{:S(2)}) collective-permute-start(bf16[1008,128]{1,0:T(8,128)(2,1)S(1)} %shard_map.414.refs_0_), channel_id=1, source_target_pairs={{0,8},{2,10},{4,12},{6,14},{8,0},{10,2},{12,4},{14,6},{16,24},{18,... | collective-permute-start | bytes 774152 | tf_op jit(solution)/shard_map/ppermute | solution.py:1036
  12.6 39.4 %collective-permute-start = (bf16[400,1024]{1,0:T(8,128)(2,1)S(1)}, bf16[400,1024]{1,0:T(8,128)(2,1)S(1)}, u32[]{:S(2)}, u32[]{:S(2)}) collective-permute-start(bf16[400,1024]{1,0:T(8,128)(2,1)S(1)} %shard_map.413), channel_id=1, source_target_pairs={{0,1},{1,0},{2,3},{3,2},{4,5},{5,4},{6,7},{7,6},{8,9},{9,8},{10,11... | collective-permute-start | bytes 2457608 | tf_op jit(solution)/shard_map/ppermute | solution.py:1140
  32.0 11.9 %collective-permute-start.6 = (bf16[4,336,128]{2,1,0:T(8,128)(2,1)S(1)}, bf16[4,336,128]{2,1,0:T(8,128)(2,1)S(1)}, u32[]{:S(2)}, u32[]{:S(2)}) collective-permute-start(bf16[4,336,128]{2,1,0:T(8,128)(2,1)S(1)} %get-tuple-element.86.refs_0_), channel_id=1, source_target_pairs={{0,5},{1,4},{2,7},{3,6},{4,1},{5,0},{6,3},{7,2},{8,13},{9,12},{10,... | collective-permute-start | bytes 1032200 | tf_op jit(solution)/shard_map/ppermute | solution.py:1047
  34.5 9.5 %collective-permute-start.7 = (bf16[4,336,128]{2,1,0:T(8,128)(2,1)S(1)}, bf16[4,336,128]{2,1,0:T(8,128)(2,1)S(1)}, u32[]{:S(2)}, u32[]{:S(2)}) collective-permute-start(bf16[4,336,128]{2,1,0:T(8,128)(2,1)S(1)} %get-tuple-element.86.refs_0_), channel_id=1, source_target_pairs={{0,2},{2,0},{4,6},{6,4},{8,10},{10,8},{12,14},{14,12},{16,18},{18,... | collective-permute-start | bytes 1032200 | tf_op jit(solution)/shard_map/ppermute | solution.py:1053
  34.5 15.0 %collective-permute-start.5 = (bf16[4,336,128]{2,1,0:T(8,128)(2,1)S(1)}, bf16[4,336,128]{2,1,0:T(8,128)(2,1)S(1)}, u32[]{:S(2)}, u32[]{:S(2)}) collective-permute-start(bf16[4,336,128]{2,1,0:T(8,128)(2,1)S(1)} %get-tuple-element.86.refs_0_), channel_id=1, source_target_pairs={{0,1},{1,0},{2,3},{3,2},{4,5},{5,4},{6,7},{7,6},{8,9},{9,8},{10,11... | collective-permute-start | bytes 1032200 | tf_op jit(solution)/shard_map/ppermute | solution.py:1046
  35.0 16.0 %collective-permute-start.4 = (bf16[4,336,128]{2,1,0:T(8,128)(2,1)S(1)}, bf16[4,336,128]{2,1,0:T(8,128)(2,1)S(1)}, u32[]{:S(2)}, u32[]{:S(2)}) collective-permute-start(bf16[4,336,128]{2,1,0:T(8,128)(2,1)S(1)} %get-tuple-element.86.refs_0_), channel_id=1, source_target_pairs={{0,4},{2,6},{4,0},{6,2},{8,12},{10,14},{12,8},{14,10},{16,20},{18,... | collective-permute-start | bytes 1032200 | tf_op jit(solution)/shard_map/ppermute | solution.py:1045
  44.0 25.6 %collective-permute-start.11 = (bf16[4,672,128]{2,1,0:T(8,128)(2,1)}, bf16[4,672,128]{2,1,0:T(8,128)(2,1)}, u32[]{:S(2)}, u32[]{:S(2)}) collective-permute-start(bf16[4,672,128]{2,1,0:T(8,128)(2,1)} %get-tuple-element.89.refs_8_.refs_0_), channel_id=1, source_target_pairs={{0,4},{2,6},{4,0},{6,2},{8,12},{10,14},{12,8},{14,10},{16,20},{18,... | collective-permute-start | bytes 2064392 | tf_op jit(solution)/shard_map/ppermute | solution.py:1045
  49.5 21.3 %collective-permute-start.12 = (bf16[4,672,128]{2,1,0:T(8,128)(2,1)}, bf16[4,672,128]{2,1,0:T(8,128)(2,1)}, u32[]{:S(2)}, u32[]{:S(2)}) collective-permute-start(bf16[4,672,128]{2,1,0:T(8,128)(2,1)} %get-tuple-element.89.refs_8_.refs_0_), channel_id=1, source_target_pairs={{0,1},{1,0},{2,3},{3,2},{4,5},{5,4},{6,7},{7,6},{8,9},{9,8},{10,11... | collective-permute-start | bytes 2064392 | tf_op jit(solution)/shard_map/ppermute | solution.py:1046
  51.0 29.1 %collective-permute-start.13 = (bf16[4,672,128]{2,1,0:T(8,128)(2,1)}, bf16[4,672,128]{2,1,0:T(8,128)(2,1)}, u32[]{:S(2)}, u32[]{:S(2)}) collective-permute-start(bf16[4,672,128]{2,1,0:T(8,128)(2,1)} %get-tuple-element.89.refs_8_.refs_0_), channel_id=1, source_target_pairs={{0,5},{1,4},{2,7},{3,6},{4,1},{5,0},{6,3},{7,2},{8,13},{9,12},{10,... | collective-permute-start | bytes 2064392 | tf_op jit(solution)/shard_map/ppermute | solution.py:1047
  56.8 24.1 %collective-permute-start.14 = (bf16[4,672,128]{2,1,0:T(8,128)(2,1)}, bf16[4,672,128]{2,1,0:T(8,128)(2,1)}, u32[]{:S(2)}, u32[]{:S(2)}) collective-permute-start(bf16[4,672,128]{2,1,0:T(8,128)(2,1)} %get-tuple-element.89.refs_8_.refs_0_), channel_id=1, source_target_pairs={{0,2},{2,0},{4,6},{6,4},{8,10},{10,8},{12,14},{14,12},{16,18},{18,... | collective-permute-start | bytes 2064392 | tf_op jit(solution)/shard_map/ppermute | solution.py:1053
  70.4 10.5 %collective-permute-start.15 = (bf16[4,672,128]{2,1,0:T(8,128)(2,1)}, bf16[4,672,128]{2,1,0:T(8,128)(2,1)}, u32[]{:S(2)}, u32[]{:S(2)}) collective-permute-start(bf16[4,672,128]{2,1,0:T(8,128)(2,1)} %shard_map.418.refs_1_), channel_id=1, source_target_pairs={{0,2},{2,0},{4,6},{6,4},{8,10},{10,8},{12,14},{14,12},{16,18},{18,... | collective-permute-start | bytes 2064392 | tf_op jit(solution)/shard_map/ppermute | solution.py:1053
  71.5 9.4 %collective-permute-start.16 = (bf16[4,672,128]{2,1,0:T(8,128)(2,1)}, bf16[4,672,128]{2,1,0:T(8,128)(2,1)}, u32[]{:S(2)}, u32[]{:S(2)}) collective-permute-start(bf16[4,672,128]{2,1,0:T(8,128)(2,1)} %shard_map.419.refs_2_), channel_id=1, source_target_pairs={{0,2},{2,0},{4,6},{6,4},{8,10},{10,8},{12,14},{14,12},{16,18},{18,... | collective-permute-start | bytes 2064392 | tf_op jit(solution)/shard_map/ppermute | solution.py:1053
  158.1 15.1 %collective-permute-start.24 = (bf16[4,512,128]{2,1,0:T(8,128)(2,1)S(1)}, bf16[4,512,128]{2,1,0:T(8,128)(2,1)S(1)}, u32[]{:S(2)}, u32[]{:S(2)}) collective-permute-start(bf16[4,512,128]{2,1,0:T(8,128)(2,1)S(1)} %copy-done.16), channel_id=1, source_target_pairs={{0,4},{2,6},{4,0},{6,2},{8,12},{10,14},{12,8},{14,10},{16,20},{18,... | collective-permute-start | bytes 1572872 | tf_op jit(solution)/shard_map/ppermute | solution.py:1076
  160.8 21.7 %collective-permute-start.20 = (bf16[4,336,128]{2,1,0:T(8,128)(2,1)S(1)}, bf16[4,336,128]{2,1,0:T(8,128)(2,1)S(1)}, u32[]{:S(2)}, u32[]{:S(2)}) collective-permute-start(bf16[4,336,128]{2,1,0:T(8,128)(2,1)S(1)} %get-tuple-element.108.refs_0_), channel_id=1, source_target_pairs={{0,4},{2,6},{4,0},{6,2},{8,12},{10,14},{12,8},{14,10},{16,20},{18,... | collective-permute-start | bytes 1032200 | tf_op jit(solution)/shard_map/ppermute | solution.py:1076
  173.8 9.3 %collective-permute-start.25 = (bf16[512,128]{1,0:T(8,128)(2,1)S(1)}, bf16[512,128]{1,0:T(8,128)(2,1)S(1)}, u32[]{:S(2)}, u32[]{:S(2)}) collective-permute-start(bf16[512,128]{1,0:T(8,128)(2,1)S(1)} %get-tuple-element.121), channel_id=1, source_target_pairs={{0,8},{2,10},{4,12},{6,14},{8,0},{10,2},{12,4},{14,6},{16,24},{18,... | collective-permute-start | bytes 393224 | tf_op jit(solution)/shard_map/ppermute | solution.py:1080
  173.9 14.8 %collective-permute-start.26 = (bf16[512,128]{1,0:T(8,128)(2,1)S(1)}, bf16[512,128]{1,0:T(8,128)(2,1)S(1)}, u32[]{:S(2)}, u32[]{:S(2)}) collective-permute-start(bf16[512,128]{1,0:T(8,128)(2,1)S(1)} %get-tuple-element.122), channel_id=1, source_target_pairs={{0,16},{2,18},{4,20},{6,22},{8,24},{10,26},{12,28},{14,30},{16,0},... | collective-permute-start | bytes 393224 | tf_op jit(solution)/shard_map/ppermute | solution.py:1080
  176.6 17.0 %collective-permute-start.27 = (bf16[512,128]{1,0:T(8,128)(2,1)S(1)}, bf16[512,128]{1,0:T(8,128)(2,1)S(1)}, u32[]{:S(2)}, u32[]{:S(2)}) collective-permute-start(bf16[512,128]{1,0:T(8,128)(2,1)S(1)} %get-tuple-element.123), channel_id=1, source_target_pairs={{0,24},{2,26},{4,28},{6,30},{8,16},{10,18},{12,20},{14,22},{16,8},... | collective-permute-start | bytes 393224 | tf_op jit(solution)/shard_map/ppermute | solution.py:1080
  180.3 15.1 %collective-permute-start.32 = (f32[4,16,256]{2,1,0:T(8,128)S(1)}, f32[4,16,256]{2,1,0:T(8,128)S(1)}, u32[]{:S(2)}, u32[]{:S(2)}) collective-permute-start(f32[4,16,256]{2,1,0:T(8,128)S(1)} %pad_maximum_fusion.own_ref), channel_id=1, source_target_pairs={{0,24},{2,26},{4,28},{6,30},{8,16},{10,18},{12,20},{14,22},{16,8},... | collective-permute-start | bytes 196616 | tf_op jit(solution)/shard_map/ppermute | solution.py:1036
  183.1 20.6 %collective-permute-start.21 = (bf16[336,128]{1,0:T(8,128)(2,1)S(1)}, bf16[336,128]{1,0:T(8,128)(2,1)S(1)}, u32[]{:S(2)}, u32[]{:S(2)}) collective-permute-start(bf16[336,128]{1,0:T(8,128)(2,1)S(1)} %get-tuple-element.112), channel_id=1, source_target_pairs={{0,8},{2,10},{4,12},{6,14},{8,0},{10,2},{12,4},{14,6},{16,24},{18,... | collective-permute-start | bytes 258056 | tf_op jit(solution)/shard_map/ppermute | solution.py:1080
  183.2 20.5 %collective-permute-start.22 = (bf16[336,128]{1,0:T(8,128)(2,1)S(1)}, bf16[336,128]{1,0:T(8,128)(2,1)S(1)}, u32[]{:S(2)}, u32[]{:S(2)}) collective-permute-start(bf16[336,128]{1,0:T(8,128)(2,1)S(1)} %get-tuple-element.113), channel_id=1, source_target_pairs={{0,16},{2,18},{4,20},{6,22},{8,24},{10,26},{12,28},{14,30},{16,0},... | collective-permute-start | bytes 258056 | tf_op jit(solution)/shard_map/ppermute | solution.py:1080
  188.8 15.0 %collective-permute-start.23 = (bf16[336,128]{1,0:T(8,128)(2,1)S(1)}, bf16[336,128]{1,0:T(8,128)(2,1)S(1)}, u32[]{:S(2)}, u32[]{:S(2)}) collective-permute-start(bf16[336,128]{1,0:T(8,128)(2,1)S(1)} %get-tuple-element.114), channel_id=1, source_target_pairs={{0,24},{2,26},{4,28},{6,30},{8,16},{10,18},{12,20},{14,22},{16,8},... | collective-permute-start | bytes 258056 | tf_op jit(solution)/shard_map/ppermute | solution.py:1080
  193.5 8.1 %collective-permute-start.31 = (f32[4,16,256]{2,1,0:T(8,128)S(1)}, f32[4,16,256]{2,1,0:T(8,128)S(1)}, u32[]{:S(2)}, u32[]{:S(2)}) collective-permute-start(f32[4,16,256]{2,1,0:T(8,128)S(1)} %pad_maximum_fusion.own_ref), channel_id=1, source_target_pairs={{0,16},{2,18},{4,20},{6,22},{8,24},{10,26},{12,28},{14,30},{16,0},... | collective-permute-start | bytes 196616 | tf_op jit(solution)/shard_map/ppermute | solution.py:1036
  (61 other events, 990.4 us)

commit v4 on v3

--- a/solution.py
+++ b/solution.py
@@ -951,6 +951,20 @@
         target[...] = (own_ref[depth].astype(f32) + back_ref[depth].astype(f32)).astype(bf16)
 
 
+def add_cores_depth(at, keep_ref, back_ref, *targets):
+    for step, target in enumerate(targets):
+        for side in (0, 1):
+            chip = (at[3] ^ step) * 2 + side
+            target[side] = (keep_ref[chip].astype(f32) + back_ref[chip].astype(f32)).astype(bf16)
+
+
+def add_depths(at, *refs):
+    mine_ref, across_ref = refs[4:6]
+    for target, side in ((mine_ref, at[2]), (across_ref, 1 - at[2])):
+        terms = [ref[side].astype(f32) for ref in refs[0:4]]
+        target[...] = (terms[0] + terms[1] + terms[2] + terms[3]).astype(bf16)
+
+
 def adam_update(weight, gradient, moment, square, step_rate):
     moment_new = beta_one * moment + (1.0 - beta_one) * gradient
     square_new = beta_two * square + (1.0 - beta_two) * gradient * gradient
@@ -990,7 +1004,7 @@
 
 
 def finish_first(at, *refs):
-    conv_adam(refs[0:4], *refs[4:7], refs[7:11], step_rates()[0])
+    conv_adam(refs[0:2], *refs[2:5], refs[5:9], step_rates()[0])
 
 
 def finish_second(at, *refs):
@@ -1013,11 +1027,13 @@
     wide = (at[3] * 2 + at[2]) * 2 + at[1]
     given, results, grad_ref = refs[0:6], refs[6:14], refs[14]
     sums, films = None, []
-    for far, ref in enumerate((own_ref, one_ref, two_ref, three_ref)):
-        for near in range(4):
-            rows = ref[near]
-            sums = rows if sums is None else sums + rows
-            films.append(jnp.concatenate((rows[11:12], rows[12:13]), axis=1))
+    for ref in (own_ref, one_ref, two_ref, three_ref):
+        rows = ref[...]
+        sums = rows[0:16] if sums is None else sums + rows[0:16]
+        for start in range(16, 24, 2):
+            films.append(
+                jnp.concatenate((rows[start : start + 1], rows[start + 1 : start + 2]), axis=1)
+            )
     adam_into(sums[0:13, 0:HALF], given[0:3], results[0:4], step_rates()[5], Ellipsis)
     grad_ref[...] = lax.dot_general(
         soft_ref[...].astype(bf16), jnp.concatenate(films, axis=0).astype(bf16), ON_FIRST,
@@ -1082,10 +1098,25 @@
     ]
 
 
-def gather_vectors(rows, wide):
-    rows = jnp.stack((rows, lax.ppermute(rows, "wide", [(i, i ^ 1) for i in range(wide)])))
-    rows = jnp.concatenate((rows, lax.ppermute(rows, "wide", [(i, i ^ 2) for i in range(wide)])))
-    return along_depth(rows, wide)
+def apart_along_depth(parts, wide):
+    return [parts[0]] + [
+        lax.ppermute(parts[step], "wide", [(i, i ^ (4 * step)) for i in range(wide)])
+        for step in (1, 2, 3)
+    ]
+
+
+def pack_vectors(at, here_ref, core_ref, side_ref, out_ref):
+    samples = (here_ref[...], core_ref[...], side_ref[0], side_ref[1])
+    out_ref[0:16, :] = samples[0] + samples[1] + samples[2] + samples[3]
+    for index, rows in enumerate(samples):
+        out_ref[16 + 2 * index : 18 + 2 * index, :] = rows[11:13]
+
+
+def gather_vectors(rows, scalars, wide):
+    core = lax.ppermute(rows, "wide", [(i, i ^ 1) for i in range(wide)])
+    side = lax.ppermute(jnp.stack((rows, core)), "wide", [(i, i ^ 2) for i in range(wide)])
+    (packed,) = call(pack_vectors, (shaped((24, 256), f32),), (rows, core, side), scalars)
+    return along_depth(packed, wide)
 
 
 def per_device(
@@ -1259,9 +1290,19 @@
             far=(across_second,),
         )
         parts_second = add_far_units(own_second, across_second, scalars, wide)
-        own_first, across_first = add_core_units(keep, send, scalars, wide)
-        parts_first = add_far_units(own_first, across_first, scalars, wide)
-        started = (across_first,)
+        back = lax.ppermute(send, "wide", [(i, i ^ 1) for i in range(wide)])
+        sums_first = call(
+            add_cores_depth, (shaped((2, FIRST_ROWS, 128), bf16),) * 4, (keep, back), scalars
+        )
+        one = shaped((FIRST_ROWS, 128), bf16)
+        mine_first, across_first = call(
+            add_depths, (one, one), apart_along_depth(sums_first, wide), scalars
+        )
+        parts_first = (
+            mine_first,
+            lax.ppermute(across_first, "wide", [(i, i ^ 2) for i in range(wide)]),
+        )
+        started = (sums_first[1],)
     else:
         kernel_two = second_full
         taps_two, residual, hidden, stat_three, film_rows = call(
@@ -1312,7 +1353,7 @@
             finish_small,
             (vec_shape,) * 4 + (film_shape,) * 4,
             (
-                *gather_vectors(vec_half, wide),
+                *gather_vectors(vec_half, scalars, wide),
                 soft_all,
                 vectors,
                 vectors_moment,

time: 208 us -> 199 us (0.957)
  starting transfers between devices: 38 us -> 32.4 us
  waiting for transfers between devices: 51.3 us -> 47.2 us
    ppermute x6 -> x3, starting transfers between devices: 11.6 us -> 4.11 us  [add_far_units(): lax.ppermute(parts[step], 'wide', [(i, i ^ 4 * step) for i in range(wide)])]
    ppermute x2 -> x7, starting transfers between devices: 0.71 us -> 5.92 us  [the longest x3 3.55 us: apart_along_depth(): lax.ppermute(parts[step], 'wide', [(i, i ^ 4 * step) for i in range(wide)])]
    ppermute x6 -> x3, waiting for transfers between devices: 3.34 us -> 0.01 us  [add_far_units(): lax.ppermute(parts[step], 'wide', [(i, i ^ 4 * step) for i in range(wide)])]
    ppermute x2 -> x7, waiting for transfers between devices: 3.22 us -> 4.23 us  [the longest x1 3.41 us: gather_vectors(): lax.ppermute(jnp.stack((rows, core)), 'wide', [(i, i ^ 2) for i in range(...]
    pallas_call x15 -> x16, Pallas kernels: 95.1 us -> 95.7 us  [call(): pl.pallas_call(body, out_shape=tuple(outs), in_specs=[pl.BlockSpec(memory...]
  transfers between devices with their start and end apart: 33 -> 33, of which waited for: 12 -> 12; matrix products, arithmetic and copies ran while one was open for 0% -> 0% of each run, Pallas kernels for 15% -> 16%
where the time goes in v4:
time: 199 us; the launch traced here: 196 us
  Pallas kernels  97.8 us (49%)
  waiting for transfers between devices  47.2 us (24%)
  starting transfers between devices  32.4 us (16%)
  local copies, waits for them, and re-layouts  17.4 us (9%)
    pallas_call x16, Pallas kernels, call(): pl.pallas_call(body, out_shape=tuple(outs), in_specs=[pl.BlockSpec(memory...  95.7 us
    ppermute x6, waiting for transfers between devices, along_depth(): lax.ppermute(unit, 'wide', [(i, i ^ 4 * step) for i in range(wide)])  17.3 us
    unnamed x104, local copies, waits for them, and re-layouts  17.2 us
    ppermute x2, waiting for transfers between devices, along_plane(): lax.ppermute(stack, ('wide', 'narrow'), diagonal)  16.8 us
    ppermute x6, starting transfers between devices, along_depth(): lax.ppermute(unit, 'wide', [(i, i ^ 4 * step) for i in range(wide)])  10.2 us
    ppermute x3, starting transfers between devices, add_far_units(): lax.ppermute(parts[step], 'wide', [(i, i ^ 4 * step) for i in range(wide)])  4.11 us
  transfers between devices with their start and end apart: 33, of which 12 were waited for; matrix products, arithmetic and copies ran while one was open for 0% of the time, Pallas kernels for 16%

profile of v4, /device:TPU:0, one launch (start us, length us, event | category | flops | bytes accessed | tf_op | source)
XLA Modules:
  0.0 196.4 jit_solution(2346104040105530010)
XLA Ops:
  1.5 2.0 %shard_map.414.refs_0_ = bf16[1008,128]{1,0:T(8,128)(2,1)S(1)} custom-call(s32[4]{0:T(128)S(1)} %pad_add_fusion.at, bf16[1,768]{1,0:T(2,128)(2,1)S(1)} %copy-done.41, f32[192,216]{1,0:T(8,128)} %bitcast.36, f32[192,216]{1,0:T(8,128)} %bitcast.34, f32[48,2,192]{2,1,0:T(2,128)} %refs_3_.1, f32[3,24,192]{2,1,0:T(8,128)} %bitcast.40, f32[24,192]{1,0:T(8,128)} %refs_10_.1), custom_call_target="tpu_custom_call" | custom-call | bytes 1024 | tf_op jit(solution)/shard_map/pallas_call | solution.py:56
  3.5 5.1 %collective-permute-start.3 = (bf16[1008,128]{1,0:T(8,128)(2,1)S(1)}, bf16[1008,128]{1,0:T(8,128)(2,1)S(1)}, u32[]{:S(2)}, u32[]{:S(2)}) collective-permute-start(bf16[1008,128]{1,0:T(8,128)(2,1)S(1)} %shard_map.414.refs_0_), channel_id=1, source_target_pairs={{0,24},{2,26},{4,28},{6,30},{8,16},{10,18},{12,20},{14,22},{16,8},... | collective-permute-start | bytes 774152 | tf_op jit(solution)/shard_map/ppermute | solution.py:1052
  12.6 1.7 collective-permute-start
  15.8 14.8 %collective-permute-done.2.refs_2_ = bf16[1008,128]{1,0:T(8,128)(2,1)S(1)} collective-permute-done((bf16[1008,128]{1,0:T(8,128)(2,1)S(1)}, bf16[1008,128]{1,0:T(8,128)(2,1)S(1)}, u32[]{:S(2)}, u32[]{:S(2)}) %collective-permute-start.2) | collective-permute-done | bytes 258080 | tf_op jit(solution)/shard_map/ppermute | solution.py:1052
  32.0 2.4 %collective-permute-start.6 = (bf16[4,336,128]{2,1,0:T(8,128)(2,1)S(1)}, bf16[4,336,128]{2,1,0:T(8,128)(2,1)S(1)}, u32[]{:S(2)}, u32[]{:S(2)}) collective-permute-start(bf16[4,336,128]{2,1,0:T(8,128)(2,1)S(1)} %get-tuple-element.86.refs_0_), channel_id=1, source_target_pairs={{0,5},{1,4},{2,7},{3,6},{4,1},{5,0},{6,3},{7,2},{8,13},{9,12},{10,... | collective-permute-start | bytes 1032200 | tf_op jit(solution)/shard_map/ppermute | solution.py:1063
  35.5 8.4 %collective-permute-done.6.refs_3_ = bf16[4,336,128]{2,1,0:T(8,128)(2,1)S(1)} collective-permute-done((bf16[4,336,128]{2,1,0:T(8,128)(2,1)S(1)}, bf16[4,336,128]{2,1,0:T(8,128)(2,1)S(1)}, u32[]{:S(2)}, u32[]{:S(2)}) %collective-permute-start.6) | collective-permute-done | bytes 344096 | tf_op jit(solution)/shard_map/ppermute | solution.py:1063
  45.6 3.9 %collective-permute-done.5.refs_2_ = bf16[4,336,128]{2,1,0:T(8,128)(2,1)S(1)} collective-permute-done((bf16[4,336,128]{2,1,0:T(8,128)(2,1)S(1)}, bf16[4,336,128]{2,1,0:T(8,128)(2,1)S(1)}, u32[]{:S(2)}, u32[]{:S(2)}) %collective-permute-start.5) | collective-permute-done | bytes 344096 | tf_op jit(solution)/shard_map/ppermute | solution.py:1062
  52.7 3.2 %shard_map.416 = (bf16[1024,384]{1,0:T(8,128)(2,1)S(1)}, bf16[1088,1152]{1,0:T(8,128)(2,1)S(1)}, f32[8,384]{1,0:T(8,128)S(1)}, f32[16,384]{1,0:T(8,128)S(1)}) custom-call(s32[4]{0:T(128)S(1)} %pad_add_fusion.at, bf16[192,1024]{1,0:T(8,128)(2,1)S(1)} %bitcast.33, bf16[400,1024]{1,0:T(8,128)(2,1)S(1)} %collective-permute-done.other_ref, ...), custom_call_target="tpu_custom_call" | custom-call | bytes 1024 | tf_op jit(solution)/shard_map/pallas_call | solution.py:56
  57.6 8.6 %shard_map.417 = (f32[1024,384]{1,0:T(8,128)S(1)}, bf16[3456,384]{1,0:T(8,128)(2,1)S(1)}, f32[8,384]{1,0:T(8,128)S(1)}) custom-call(s32[4]{0:T(128)S(1)} %pad_add_fusion.at, bf16[1088,1152]{1,0:T(8,128)(2,1)S(1)} %get-tuple-element.87.taps_ref.refs_8_, f32[1024,128]{1,0:T(8,128)S(1)} %broadcast_in_dim.12.mask_ref.refs_5_, ...), custom_call_target="tpu_custom_call" | custom-call | bytes 1024 | tf_op jit(solution)/shard_map/pallas_call | solution.py:56
  71.7 8.4 %collective-permute-done.13.refs_0_ = bf16[4,672,128]{2,1,0:T(8,128)(2,1)} collective-permute-done((bf16[4,672,128]{2,1,0:T(8,128)(2,1)}, bf16[4,672,128]{2,1,0:T(8,128)(2,1)}, u32[]{:S(2)}, u32[]{:S(2)}) %collective-permute-start.13) | collective-permute-done | bytes 688160 | tf_op jit(solution)/shard_map/ppermute | solution.py:1063
  80.9 2.3 %collective-permute-done.17.refs_7_ = bf16[4,672,128]{2,1,0:T(8,128)(2,1)S(1)} collective-permute-done((bf16[4,672,128]{2,1,0:T(8,128)(2,1)}, bf16[4,672,128]{2,1,0:T(8,128)(2,1)S(1)}, u32[]{:S(2)}, u32[]{:S(2)}) %collective-permute-start.17) | collective-permute-done | bytes 688160 | tf_op jit(solution)/shard_map/ppermute | solution.py:1069
  87.7 51.3 %shard_map.421 = (bf16[192,1024]{1,0:T(8,128)(2,1)}, f32[1024,384]{1,0:T(8,128)S(1)}, bf16[1088,1152]{1,0:T(8,128)(2,1)}, f32[16,384]{1,0:T(8,128)S(1)}, f32[8,3...) custom-call(s32[4]{0:T(128)S(1)} %copy-done.28, ...), custom_call_target="tpu_custom_call" | custom-call | flops 40000000000 | bytes 1024 | tf_op jit(solution)/shard_map/pallas_call | solution.py:56
  139.3 2.5 %collective-permute-done.18.back_ref = bf16[8,512,128]{2,1,0:T(8,128)(2,1)S(1)} collective-permute-done((bf16[8,512,128]{2,1,0:T(8,128)(2,1)S(1)}, bf16[8,512,128]{2,1,0:T(8,128)(2,1)S(1)}, u32[]{:S(2)}, u32[]{:S(2)}) %collective-permute-start.18) | collective-permute-done | bytes 1048608 | tf_op jit(solution)/shard_map/ppermute | solution.py:1086
  143.4 1.7 copy-done
  145.2 1.7 copy-done.3
  146.9 10.9 %shard_map.423 = (bf16[1088,1152]{1,0:T(8,128)(2,1)S(1)}, f32[16,384]{1,0:T(8,128)S(1)}, bf16[8,336,128]{2,1,0:T(8,128)(2,1)S(1)}, bf16[8,336,128]{2,1,0:T(8,128)(2,1)S(1)}) custom-call(s32[4]{0:T(128)S(1)} %copy-done.28, bf16[1088,1152]{1,0:T(8,128)(2,1)S(1)} %copy-done.3, bf16[3456,384]{1,0:T(8,128)(2,1)S(1)} %copy-done, f32[1024,384]{1,0:T(8,128)S(1)} %copy-done.7, ...), custom_call_target="tpu_custom_call" | custom-call | bytes 1024 | tf_op jit(solution)/shard_map/pallas_call | solution.py:56
  164.4 8.7 %shard_map.425 = (bf16[192,1024]{1,0:T(8,128)(2,1)}, f32[16,256]{1,0:T(8,128)S(1)}) custom-call(s32[4]{0:T(128)S(1)} %copy-done.28, bf16[1088,1152]{1,0:T(8,128)(2,1)S(1)} %get-tuple-element.101.taps_ref, bf16[3456,384]{1,0:T(8,128)(2,1)S(1)} %copy-done.2, bf16[1024,384]{1,0:T(8,128)(2,1)S(1)} %copy-done.14, f32[8,384]{1,0:T(8,128)S(1)} %get-tuple-element.103.stat_ref, ...), custom_call_target="tpu_custom_call" | custom-call | bytes 1024 | tf_op jit(solution)/shard_map/pallas_call | solution.py:56
  175.1 1.6 collective-permute-start.26
  176.7 1.7 collective-permute-start.27
  181.2 3.4 %collective-permute-done.29.side_ref = f32[2,16,256]{2,1,0:T(8,128)S(1)} collective-permute-done((f32[2,16,256]{2,1,0:T(8,128)S(1)}, f32[2,16,256]{2,1,0:T(8,128)S(1)}, u32[]{:S(2)}, u32[]{:S(2)}) %collective-permute-start.29) | collective-permute-done | bytes 32800 | tf_op jit(solution)/shard_map/ppermute | solution.py:1117
  185.2 2.2 %collective-permute-start.32 = (f32[24,256]{1,0:T(8,128)S(1)}, f32[24,256]{1,0:T(8,128)S(1)}, u32[]{:S(2)}, u32[]{:S(2)}) collective-permute-start(f32[24,256]{1,0:T(8,128)S(1)} %shard_map.430.own_ref), channel_id=1, source_target_pairs={{0,24},{2,26},{4,28},{6,30},{8,16},{10,18},{12,20},{14,22},{16,8},... | collective-permute-start | bytes 73736 | tf_op jit(solution)/shard_map/ppermute | solution.py:1052
  189.7 1.8 shard_map.429
  192.5 2.0 %shard_map.431 = (f32[13,192]{1,0:T(8,128)}, f32[13,192]{1,0:T(8,128)}, f32[13,192]{1,0:T(8,128)}, f32[13,192]{1,0:T(8,128)}, f32[48,2,192]{2,1,0:T(2,128)}, /*i...) custom-call(s32[4]{0:T(128)S(1)} %copy-done.28, f32[24,256]{1,0:T(8,128)S(1)} %shard_map.430.own_ref, ...), custom_call_target="tpu_custom_call" | custom-call | bytes 1024 | tf_op jit(solution)/shard_map/pallas_call | solution.py:56
  194.6 1.6 shard_map.427
  (169 shorter events, 42.7 us)
Async XLA Ops:
  3.5 12.3 %collective-permute-start.3 = (bf16[1008,128]{1,0:T(8,128)(2,1)S(1)}, bf16[1008,128]{1,0:T(8,128)(2,1)S(1)}, u32[]{:S(2)}, u32[]{:S(2)}) collective-permute-start(bf16[1008,128]{1,0:T(8,128)(2,1)S(1)} %shard_map.414.refs_0_), channel_id=1, source_target_pairs={{0,24},{2,26},{4,28},{6,30},{8,16},{10,18},{12,20},{14,22},{16,8},... | collective-permute-start | bytes 774152 | tf_op jit(solution)/shard_map/ppermute | solution.py:1052
  8.6 22.0 %collective-permute-start.2 = (bf16[1008,128]{1,0:T(8,128)(2,1)S(1)}, bf16[1008,128]{1,0:T(8,128)(2,1)S(1)}, u32[]{:S(2)}, u32[]{:S(2)}) collective-permute-start(bf16[1008,128]{1,0:T(8,128)(2,1)S(1)} %shard_map.414.refs_0_), channel_id=1, source_target_pairs={{0,16},{2,18},{4,20},{6,22},{8,24},{10,26},{12,28},{14,30},{16,0},... | collective-permute-start | bytes 774152 | tf_op jit(solution)/shard_map/ppermute | solution.py:1052
  8.6 22.0 %collective-permute-start.1 = (bf16[1008,128]{1,0:T(8,128)(2,1)S(1)}, bf16[1008,128]{1,0:T(8,128)(2,1)S(1)}, u32[]{:S(2)}, u32[]{:S(2)}) collective-permute-start(bf16[1008,128]{1,0:T(8,128)(2,1)S(1)} %shard_map.414.refs_0_), channel_id=1, source_target_pairs={{0,8},{2,10},{4,12},{6,14},{8,0},{10,2},{12,4},{14,6},{16,24},{18,... | collective-permute-start | bytes 774152 | tf_op jit(solution)/shard_map/ppermute | solution.py:1052
  12.6 39.4 %collective-permute-start = (bf16[400,1024]{1,0:T(8,128)(2,1)S(1)}, bf16[400,1024]{1,0:T(8,128)(2,1)S(1)}, u32[]{:S(2)}, u32[]{:S(2)}) collective-permute-start(bf16[400,1024]{1,0:T(8,128)(2,1)S(1)} %shard_map.413), channel_id=1, source_target_pairs={{0,1},{1,0},{2,3},{3,2},{4,5},{5,4},{6,7},{7,6},{8,9},{9,8},{10,11... | collective-permute-start | bytes 2457608 | tf_op jit(solution)/shard_map/ppermute | solution.py:1171
  32.0 11.9 %collective-permute-start.6 = (bf16[4,336,128]{2,1,0:T(8,128)(2,1)S(1)}, bf16[4,336,128]{2,1,0:T(8,128)(2,1)S(1)}, u32[]{:S(2)}, u32[]{:S(2)}) collective-permute-start(bf16[4,336,128]{2,1,0:T(8,128)(2,1)S(1)} %get-tuple-element.86.refs_0_), channel_id=1, source_target_pairs={{0,5},{1,4},{2,7},{3,6},{4,1},{5,0},{6,3},{7,2},{8,13},{9,12},{10,... | collective-permute-start | bytes 1032200 | tf_op jit(solution)/shard_map/ppermute | solution.py:1063
  34.5 9.5 %collective-permute-start.7 = (bf16[4,336,128]{2,1,0:T(8,128)(2,1)S(1)}, bf16[4,336,128]{2,1,0:T(8,128)(2,1)S(1)}, u32[]{:S(2)}, u32[]{:S(2)}) collective-permute-start(bf16[4,336,128]{2,1,0:T(8,128)(2,1)S(1)} %get-tuple-element.86.refs_0_), channel_id=1, source_target_pairs={{0,2},{2,0},{4,6},{6,4},{8,10},{10,8},{12,14},{14,12},{16,18},{18,... | collective-permute-start | bytes 1032200 | tf_op jit(solution)/shard_map/ppermute | solution.py:1069
  34.5 15.0 %collective-permute-start.5 = (bf16[4,336,128]{2,1,0:T(8,128)(2,1)S(1)}, bf16[4,336,128]{2,1,0:T(8,128)(2,1)S(1)}, u32[]{:S(2)}, u32[]{:S(2)}) collective-permute-start(bf16[4,336,128]{2,1,0:T(8,128)(2,1)S(1)} %get-tuple-element.86.refs_0_), channel_id=1, source_target_pairs={{0,1},{1,0},{2,3},{3,2},{4,5},{5,4},{6,7},{7,6},{8,9},{9,8},{10,11... | collective-permute-start | bytes 1032200 | tf_op jit(solution)/shard_map/ppermute | solution.py:1062
  35.0 16.0 %collective-permute-start.4 = (bf16[4,336,128]{2,1,0:T(8,128)(2,1)S(1)}, bf16[4,336,128]{2,1,0:T(8,128)(2,1)S(1)}, u32[]{:S(2)}, u32[]{:S(2)}) collective-permute-start(bf16[4,336,128]{2,1,0:T(8,128)(2,1)S(1)} %get-tuple-element.86.refs_0_), channel_id=1, source_target_pairs={{0,4},{2,6},{4,0},{6,2},{8,12},{10,14},{12,8},{14,10},{16,20},{18,... | collective-permute-start | bytes 1032200 | tf_op jit(solution)/shard_map/ppermute | solution.py:1061
  44.0 8.0 %collective-permute-start.10 = (bf16[4,336,128]{2,1,0:T(8,128)(2,1)S(1)}, bf16[4,336,128]{2,1,0:T(8,128)(2,1)S(1)}, u32[]{:S(2)}, u32[]{:S(2)}) collective-permute-start(bf16[4,336,128]{2,1,0:T(8,128)(2,1)S(1)} %collective-permute-done.6.refs_3_), channel_id=1, source_target_pairs={{0,2},{2,0},{4,6},{6,4},{8,10},{10,8},{12,14},{14,12},{16,18},{18,... | collective-permute-start | bytes 1032200 | tf_op jit(solution)/shard_map/ppermute | solution.py:1069
  44.0 25.6 %collective-permute-start.11 = (bf16[4,672,128]{2,1,0:T(8,128)(2,1)}, bf16[4,672,128]{2,1,0:T(8,128)(2,1)}, u32[]{:S(2)}, u32[]{:S(2)}) collective-permute-start(bf16[4,672,128]{2,1,0:T(8,128)(2,1)} %get-tuple-element.89.refs_8_.refs_0_), channel_id=1, source_target_pairs={{0,4},{2,6},{4,0},{6,2},{8,12},{10,14},{12,8},{14,10},{16,20},{18,... | collective-permute-start | bytes 2064392 | tf_op jit(solution)/shard_map/ppermute | solution.py:1061
  49.5 21.3 %collective-permute-start.12 = (bf16[4,672,128]{2,1,0:T(8,128)(2,1)}, bf16[4,672,128]{2,1,0:T(8,128)(2,1)}, u32[]{:S(2)}, u32[]{:S(2)}) collective-permute-start(bf16[4,672,128]{2,1,0:T(8,128)(2,1)} %get-tuple-element.89.refs_8_.refs_0_), channel_id=1, source_target_pairs={{0,1},{1,0},{2,3},{3,2},{4,5},{5,4},{6,7},{7,6},{8,9},{9,8},{10,11... | collective-permute-start | bytes 2064392 | tf_op jit(solution)/shard_map/ppermute | solution.py:1062
  51.0 29.1 %collective-permute-start.13 = (bf16[4,672,128]{2,1,0:T(8,128)(2,1)}, bf16[4,672,128]{2,1,0:T(8,128)(2,1)}, u32[]{:S(2)}, u32[]{:S(2)}) collective-permute-start(bf16[4,672,128]{2,1,0:T(8,128)(2,1)} %get-tuple-element.89.refs_8_.refs_0_), channel_id=1, source_target_pairs={{0,5},{1,4},{2,7},{3,6},{4,1},{5,0},{6,3},{7,2},{8,13},{9,12},{10,... | collective-permute-start | bytes 2064392 | tf_op jit(solution)/shard_map/ppermute | solution.py:1063
  56.8 24.1 %collective-permute-start.14 = (bf16[4,672,128]{2,1,0:T(8,128)(2,1)}, bf16[4,672,128]{2,1,0:T(8,128)(2,1)}, u32[]{:S(2)}, u32[]{:S(2)}) collective-permute-start(bf16[4,672,128]{2,1,0:T(8,128)(2,1)} %get-tuple-element.89.refs_8_.refs_0_), channel_id=1, source_target_pairs={{0,2},{2,0},{4,6},{6,4},{8,10},{10,8},{12,14},{14,12},{16,18},{18,... | collective-permute-start | bytes 2064392 | tf_op jit(solution)/shard_map/ppermute | solution.py:1069
  70.4 10.5 %collective-permute-start.15 = (bf16[4,672,128]{2,1,0:T(8,128)(2,1)}, bf16[4,672,128]{2,1,0:T(8,128)(2,1)}, u32[]{:S(2)}, u32[]{:S(2)}) collective-permute-start(bf16[4,672,128]{2,1,0:T(8,128)(2,1)} %shard_map.418.refs_1_), channel_id=1, source_target_pairs={{0,2},{2,0},{4,6},{6,4},{8,10},{10,8},{12,14},{14,12},{16,18},{18,... | collective-permute-start | bytes 2064392 | tf_op jit(solution)/shard_map/ppermute | solution.py:1069
  71.5 9.4 %collective-permute-start.16 = (bf16[4,672,128]{2,1,0:T(8,128)(2,1)}, bf16[4,672,128]{2,1,0:T(8,128)(2,1)}, u32[]{:S(2)}, u32[]{:S(2)}) collective-permute-start(bf16[4,672,128]{2,1,0:T(8,128)(2,1)} %shard_map.419.refs_2_), channel_id=1, source_target_pairs={{0,2},{2,0},{4,6},{6,4},{8,10},{10,8},{12,14},{14,12},{16,18},{18,... | collective-permute-start | bytes 2064392 | tf_op jit(solution)/shard_map/ppermute | solution.py:1069
  158.1 15.3 %collective-permute-start.24 = (bf16[4,512,128]{2,1,0:T(8,128)(2,1)S(1)}, bf16[4,512,128]{2,1,0:T(8,128)(2,1)S(1)}, u32[]{:S(2)}, u32[]{:S(2)}) collective-permute-start(bf16[4,512,128]{2,1,0:T(8,128)(2,1)S(1)} %copy-done.16), channel_id=1, source_target_pairs={{0,4},{2,6},{4,0},{6,2},{8,12},{10,14},{12,8},{14,10},{16,20},{18,... | collective-permute-start | bytes 1572872 | tf_op jit(solution)/shard_map/ppermute | solution.py:1092
  160.8 14.3 %collective-permute-start.21 = (bf16[2,336,128]{2,1,0:T(8,128)(2,1)S(1)}, bf16[2,336,128]{2,1,0:T(8,128)(2,1)S(1)}, u32[]{:S(2)}, u32[]{:S(2)}) collective-permute-start(bf16[2,336,128]{2,1,0:T(8,128)(2,1)S(1)} %get-tuple-element.111), channel_id=1, source_target_pairs={{0,16},{2,18},{4,20},{6,22},{8,24},{10,26},{12,28},{14,30},{16,0},... | collective-permute-start | bytes 516104 | tf_op jit(solution)/shard_map/ppermute | solution.py:1103
  162.3 14.4 %collective-permute-start.22 = (bf16[2,336,128]{2,1,0:T(8,128)(2,1)S(1)}, bf16[2,336,128]{2,1,0:T(8,128)(2,1)S(1)}, u32[]{:S(2)}, u32[]{:S(2)}) collective-permute-start(bf16[2,336,128]{2,1,0:T(8,128)(2,1)S(1)} %get-tuple-element.112), channel_id=1, source_target_pairs={{0,24},{2,26},{4,28},{6,30},{8,16},{10,18},{12,20},{14,22},{16,8},... | collective-permute-start | bytes 516104 | tf_op jit(solution)/shard_map/ppermute | solution.py:1103
  163.0 15.4 %collective-permute-start.20 = (bf16[2,336,128]{2,1,0:T(8,128)(2,1)S(1)}, bf16[2,336,128]{2,1,0:T(8,128)(2,1)S(1)}, u32[]{:S(2)}, u32[]{:S(2)}) collective-permute-start(bf16[2,336,128]{2,1,0:T(8,128)(2,1)S(1)} %get-tuple-element.108.refs_0_), channel_id=1, source_target_pairs={{0,8},{2,10},{4,12},{6,14},{8,0},{10,2},{12,4},{14,6},{16,24},{18,... | collective-permute-start | bytes 516104 | tf_op jit(solution)/shard_map/ppermute | solution.py:1103
  173.2 7.5 %collective-permute-start.28 = (f32[16,256]{1,0:T(8,128)S(1)}, f32[16,256]{1,0:T(8,128)S(1)}, u32[]{:S(2)}, u32[]{:S(2)}) collective-permute-start(f32[16,256]{1,0:T(8,128)S(1)} %get-tuple-element.128.here_ref), channel_id=1, source_target_pairs={{0,2},{2,0},{4,6},{6,4},{8,10},{10,8},{12,14},{14,12},{16,18},{18,... | collective-permute-start | bytes 49160 | tf_op jit(solution)/shard_map/ppermute | solution.py:1116
  174.0 13.3 %collective-permute-start.25 = (bf16[512,128]{1,0:T(8,128)(2,1)S(1)}, bf16[512,128]{1,0:T(8,128)(2,1)S(1)}, u32[]{:S(2)}, u32[]{:S(2)}) collective-permute-start(bf16[512,128]{1,0:T(8,128)(2,1)S(1)} %get-tuple-element.121), channel_id=1, source_target_pairs={{0,8},{2,10},{4,12},{6,14},{8,0},{10,2},{12,4},{14,6},{16,24},{18,... | collective-permute-start | bytes 393224 | tf_op jit(solution)/shard_map/ppermute | solution.py:1096
  175.1 13.5 %collective-permute-start.26 = (bf16[512,128]{1,0:T(8,128)(2,1)S(1)}, bf16[512,128]{1,0:T(8,128)(2,1)S(1)}, u32[]{:S(2)}, u32[]{:S(2)}) collective-permute-start(bf16[512,128]{1,0:T(8,128)(2,1)S(1)} %get-tuple-element.122), channel_id=1, source_target_pairs={{0,16},{2,18},{4,20},{6,22},{8,24},{10,26},{12,28},{14,30},{16,0},... | collective-permute-start | bytes 393224 | tf_op jit(solution)/shard_map/ppermute | solution.py:1096
  176.7 12.9 %collective-permute-start.27 = (bf16[512,128]{1,0:T(8,128)(2,1)S(1)}, bf16[512,128]{1,0:T(8,128)(2,1)S(1)}, u32[]{:S(2)}, u32[]{:S(2)}) collective-permute-start(bf16[512,128]{1,0:T(8,128)(2,1)S(1)} %get-tuple-element.123), channel_id=1, source_target_pairs={{0,24},{2,26},{4,28},{6,30},{8,16},{10,18},{12,20},{14,22},{16,8},... | collective-permute-start | bytes 393224 | tf_op jit(solution)/shard_map/ppermute | solution.py:1096
  179.1 15.5 %collective-permute-start.23 = (bf16[336,128]{1,0:T(8,128)(2,1)S(1)}, bf16[336,128]{1,0:T(8,128)(2,1)S(1)}, u32[]{:S(2)}, u32[]{:S(2)}) collective-permute-start(bf16[336,128]{1,0:T(8,128)(2,1)S(1)} %get-tuple-element.114), channel_id=1, source_target_pairs={{0,4},{2,6},{4,0},{6,2},{8,12},{10,14},{12,8},{14,10},{16,20},{18,... | collective-permute-start | bytes 258056 | tf_op jit(solution)/shard_map/ppermute | solution.py:1303
  (61 other events, 812.9 us)

commit v5 on v4

--- a/solution.py
+++ b/solution.py
@@ -31,7 +31,7 @@
 bf16 = jnp.bfloat16
 ON_LAST = (((1,), (1,)), ((), ()))
 ON_FIRST = (((0,), (0,)), ((), ()))
-VMEM_BYTES = 45 * 1024 * 1024
+VMEM_BYTES = 46 * 1024 * 1024
 
 
 def step_rates():
@@ -640,7 +640,7 @@
         weight_ref[128 * head : 128 * head + HEAD, :] = out_nat[HEAD * head : HEAD * head + HEAD, :].astype(bf16)
         weight_ref[128 * head + HEAD : 128 * head + 128, :] = blank
     own = own_ref[...].astype(f32)
-    other = other_ref[HALF + 16 : 2 * HALF + 16, :].astype(f32)
+    other = other_ref[...].astype(f32)
     low = jnp.where(narrow == 0, own, other)
     high = jnp.where(narrow == 0, other, own)
     zero = jnp.zeros((8, C), f32)
@@ -770,22 +770,38 @@
 
 
 def middle_of_block(
-    at, one_ref, stat_two_ref, turned_ref, mask_ref, vec_ref, embed_ref, own_ref, other_ref, *refs
+    at, stat_two_ref, turned_ref, mask_ref, vec_ref, embed_ref, *refs
 ):
     (
         out_ref, direct_ref, back_taps_ref, vec_grad_ref, film_rows_ref, kernel_ref, soft_all_ref,
         keep_ref, send_ref,
-    ) = refs[8:17]
+    ) = refs[11:20]
     (
         taps_ref, residual_ref, hidden_ref, stat_ref, soft_ref, film_ref, held_ref, sems, back_ref,
-    ) = refs[17:26]
-    attention_refs = refs[26:]
+        one_ref, own_ref, other_ref, late_sems,
+    ) = refs[20:33]
+    attention_refs = refs[33:]
     in_nat, out_nat = attention_refs[0:2]
     rows_ref, terms_ref = attention_refs[-3:-1]
     units = Gathered(at, refs[0:8], held_ref, sems)
+    one_far, own_far, exchanged_far = refs[8:11]
+    late = [
+        pltpu.make_async_copy(source, target, late_sems.at[index])
+        for index, (source, target) in enumerate(
+            (
+                (one_far, one_ref),
+                (own_far, own_ref),
+                (exchanged_far.at[pl.ds(HALF + 16, HALF)], other_ref),
+            )
+        )
+    ]
+    for copy in late:
+        copy.start()
     place_conv(units, kernel_ref)
     place_film(units, film_ref)
     place_embeddings(units, soft_all_ref)
+    for copy in late:
+        copy.wait()
     film_to_third_norm(
         one_ref, stat_two_ref, turned_ref, mask_ref, vec_ref, embed_ref, kernel_ref, film_ref,
         taps_ref, residual_ref, hidden_ref, stat_ref, film_rows_ref, soft_ref, rows_ref,
@@ -819,8 +835,8 @@
     in_nat[...] = in_given[...].astype(f32)
     out_nat[...] = out_given[...].astype(f32)
     attention_body(
-        at, hidden_ref, residual_ref, stat_ref, mask_ref, vec_ref, own_ref, other_ref,
-        out_ref, direct_ref, taps_ref, back_ref, vec_grad_ref, *refs,
+        at, hidden_ref, residual_ref, stat_ref, mask_ref, vec_ref, own_ref,
+        other_ref.at[pl.ds(HALF + 16, HALF)], out_ref, direct_ref, taps_ref, back_ref, vec_grad_ref, *refs,
     )
     in_term_ref[...] = in_nat[:, 0:768]
     out_term_ref[...] = out_nat[:, 0:256]
@@ -839,10 +855,19 @@
 
 
 def second_back(at, *refs):
-    taps_one_ref = refs[8]
-    back_taps_ref, vec_grad_ref, keep_ref, send_ref = refs[-8:-4]
-    grad_ref, rows_ref, back_ref, terms_ref = refs[-4:]
-    second_back_body(at, *refs[:8], back_taps_ref, back_ref, vec_grad_ref, grad_ref, rows_ref)
+    back_taps_ref, vec_grad_ref, keep_ref, send_ref = refs[-11:-7]
+    grad_ref, rows_ref, back_ref, terms_ref, one_ref, taps_one_ref, sems = refs[-7:]
+    copies = [
+        pltpu.make_async_copy(source, target, sems.at[index])
+        for index, (source, target) in enumerate(zip(refs[7:9], (one_ref, taps_one_ref)))
+    ]
+    for copy in copies:
+        copy.start()
+    second_back_body(
+        at, *refs[:2], one_ref, *refs[2:7], back_taps_ref, back_ref, vec_grad_ref, grad_ref, rows_ref,
+        copies[0].wait,
+    )
+    copies[1].wait()
     kernel_terms(taps_one_ref, back_ref, terms_ref)
     pack_units(terms_ref, at, keep_ref, send_ref)
 
@@ -853,12 +878,14 @@
 
 def second_back_body(
     at, taps_ref, kernel_ref, one_ref, stat_ref, film_rows_ref, mask_ref, vec_ref, vec_in_ref,
-    back_taps_ref, back_ref, vec_grad_ref, grad_ref, rows_ref,
+    back_taps_ref, back_ref, vec_grad_ref, grad_ref, rows_ref, ready=None,
 ):
     def done(start, count, acc):
         grad_ref[pl.ds(start, count), :] = acc
 
     convolve_back(taps_ref, kernel_ref, done)
+    if ready is not None:
+        ready()
     mean, inverse, tally = stat_ref[0:1, :], stat_ref[1:2, :], stat_ref[2:3, :]
     gain, shift = vec_ref[3:4, :], vec_ref[4:5, :]
     scale, offset = film_rows_ref[0:1, :], film_rows_ref[1:2, :]
@@ -1259,7 +1286,7 @@
                 half_plane, plane, taps, vec_rows, stats, kernel, shaped((16, EMB), f32),
                 units, units,
             ),
-            common + (own_cotangent, exchanged),
+            common[1:],
             scalars,
             (
                 pltpu.VMEM((PADDED, 3 * C), bf16),
@@ -1271,9 +1298,13 @@
                 pltpu.VMEM((8, 4, SECOND_ROWS, 128), bf16),
                 pltpu.SemaphoreType.DMA((8,)),
                 pltpu.VMEM((PADDED, 256), bf16),
+                pltpu.VMEM((PIX, C), f32),
+                pltpu.VMEM((HALF, PIX), bf16),
+                pltpu.VMEM((HALF, PIX), bf16),
+                pltpu.SemaphoreType.DMA((3,)),
                 *attention_scratch,
             ),
-            far=second_units,
+            far=(*second_units, out_one, own_cotangent, exchanged),
             flops=4 * 10**10,
         )
         own_second, across_second = add_core_units(keep, send, scalars, wide)
@@ -1281,13 +1312,16 @@
         taps_back_one, vec_grad, keep, send = call(
             second_back,
             (taps, vec_rows, units, units),
-            (
-                taps_back, kernel_two, out_one, stat_two, film_rows, mask, vecs, vec_grad,
-                taps_one,
+            (taps_back, kernel_two, stat_two, film_rows, mask, vecs, vec_grad),
+            scalars,
+            back_scratch
+            + terms_scratch
+            + (
+                pltpu.VMEM((PIX, C), f32),
+                pltpu.VMEM((PADDED, 3 * C), bf16),
+                pltpu.SemaphoreType.DMA((2,)),
             ),
-            scalars,
-            back_scratch + terms_scratch,
-            far=(across_second,),
+            far=(out_one, taps_one, across_second),
         )
         parts_second = add_far_units(own_second, across_second, scalars, wide)
         back = lax.ppermute(send, "wide", [(i, i ^ 1) for i in range(wide)])

time: 199 us -> 195 us (0.980)
  local copies, waits for them, and re-layouts: 17.4 us -> 13 us
    unnamed x104, local copies, waits for them, and re-layouts: 17.2 us -> 12.8 us
where the time goes in v5:
time: 195 us; the launch traced here: 192 us
  Pallas kernels  98.7 us (51%)
  waiting for transfers between devices  46.5 us (24%)
  starting transfers between devices  32.5 us (17%)
  local copies, waits for them, and re-layouts  13 us (7%)
    pallas_call x16, Pallas kernels, call(): pl.pallas_call(body, out_shape=tuple(outs), in_specs=[pl.BlockSpec(memory...  96.7 us
    ppermute x6, waiting for transfers between devices, along_depth(): lax.ppermute(unit, 'wide', [(i, i ^ 4 * step) for i in range(wide)])  17.4 us
    ppermute x2, waiting for transfers between devices, along_plane(): lax.ppermute(stack, ('wide', 'narrow'), diagonal)  15.9 us
    unnamed x104, local copies, waits for them, and re-layouts  12.8 us
    ppermute x6, starting transfers between devices, along_depth(): lax.ppermute(unit, 'wide', [(i, i ^ 4 * step) for i in range(wide)])  10.2 us
    ppermute x3, starting transfers between devices, add_far_units(): lax.ppermute(parts[step], 'wide', [(i, i ^ 4 * step) for i in range(wide)])  3.98 us
    ppermute x2, waiting for transfers between devices, along_plane(): lax.ppermute(stack, 'narrow', [(0, 1), (1, 0)])  3.94 us
  transfers between devices with their start and end apart: 33, of which 12 were waited for; matrix products, arithmetic and copies ran while one was open for 0% of the time, Pallas kernels for 16%

profile of v5, /device:TPU:0, one launch (start us, length us, event | category | flops | bytes accessed | tf_op | source)
XLA Modules:
  0.0 192.2 jit_solution(17413690009229000974)
XLA Ops:
  1.5 2.0 %shard_map.414.refs_0_ = bf16[1008,128]{1,0:T(8,128)(2,1)S(1)} custom-call(s32[4]{0:T(128)S(1)} %pad_add_fusion.at, bf16[1,768]{1,0:T(2,128)(2,1)S(1)} %copy-done.38, f32[192,216]{1,0:T(8,128)} %bitcast.36, f32[192,216]{1,0:T(8,128)} %bitcast.34, f32[48,2,192]{2,1,0:T(2,128)} %refs_3_.1, f32[3,24,192]{2,1,0:T(8,128)} %bitcast.40, f32[24,192]{1,0:T(8,128)} %refs_10_.1), custom_call_target="tpu_custom_call" | custom-call | bytes 1024 | tf_op jit(solution)/shard_map/pallas_call | solution.py:56
  3.5 5.1 %collective-permute-start.3 = (bf16[1008,128]{1,0:T(8,128)(2,1)S(1)}, bf16[1008,128]{1,0:T(8,128)(2,1)S(1)}, u32[]{:S(2)}, u32[]{:S(2)}) collective-permute-start(bf16[1008,128]{1,0:T(8,128)(2,1)S(1)} %shard_map.414.refs_0_), channel_id=1, source_target_pairs={{0,24},{2,26},{4,28},{6,30},{8,16},{10,18},{12,20},{14,22},{16,8},... | collective-permute-start | bytes 774152 | tf_op jit(solution)/shard_map/ppermute | solution.py:1079
  12.6 1.7 collective-permute-start
  15.8 14.8 %collective-permute-done.2.refs_2_ = bf16[1008,128]{1,0:T(8,128)(2,1)S(1)} collective-permute-done((bf16[1008,128]{1,0:T(8,128)(2,1)S(1)}, bf16[1008,128]{1,0:T(8,128)(2,1)S(1)}, u32[]{:S(2)}, u32[]{:S(2)}) %collective-permute-start.2) | collective-permute-done | bytes 258080 | tf_op jit(solution)/shard_map/ppermute | solution.py:1079
  32.0 2.4 %collective-permute-start.6 = (bf16[4,336,128]{2,1,0:T(8,128)(2,1)S(1)}, bf16[4,336,128]{2,1,0:T(8,128)(2,1)S(1)}, u32[]{:S(2)}, u32[]{:S(2)}) collective-permute-start(bf16[4,336,128]{2,1,0:T(8,128)(2,1)S(1)} %get-tuple-element.86.refs_0_), channel_id=1, source_target_pairs={{0,5},{1,4},{2,7},{3,6},{4,1},{5,0},{6,3},{7,2},{8,13},{9,12},{10,... | collective-permute-start | bytes 1032200 | tf_op jit(solution)/shard_map/ppermute | solution.py:1090
  35.5 8.4 %collective-permute-done.6.refs_3_ = bf16[4,336,128]{2,1,0:T(8,128)(2,1)S(1)} collective-permute-done((bf16[4,336,128]{2,1,0:T(8,128)(2,1)S(1)}, bf16[4,336,128]{2,1,0:T(8,128)(2,1)S(1)}, u32[]{:S(2)}, u32[]{:S(2)}) %collective-permute-start.6) | collective-permute-done | bytes 344096 | tf_op jit(solution)/shard_map/ppermute | solution.py:1090
  44.0 1.6 collective-permute-start.11
  45.6 3.9 %collective-permute-done.5.refs_2_ = bf16[4,336,128]{2,1,0:T(8,128)(2,1)S(1)} collective-permute-done((bf16[4,336,128]{2,1,0:T(8,128)(2,1)S(1)}, bf16[4,336,128]{2,1,0:T(8,128)(2,1)S(1)}, u32[]{:S(2)}, u32[]{:S(2)}) %collective-permute-start.5) | collective-permute-done | bytes 344096 | tf_op jit(solution)/shard_map/ppermute | solution.py:1089
  52.7 3.2 %shard_map.416 = (bf16[1024,384]{1,0:T(8,128)(2,1)S(1)}, bf16[1088,1152]{1,0:T(8,128)(2,1)S(1)}, f32[8,384]{1,0:T(8,128)S(1)}, f32[16,384]{1,0:T(8,128)S(1)}) custom-call(s32[4]{0:T(128)S(1)} %pad_add_fusion.at, bf16[192,1024]{1,0:T(8,128)(2,1)S(1)} %bitcast.33, bf16[400,1024]{1,0:T(8,128)(2,1)S(1)} %collective-permute-done.other_ref.refs_10_, ...), custom_call_target="tpu_custom_call" | custom-call | bytes 1024 | tf_op jit(solution)/shard_map/pallas_call | solution.py:56
  57.7 8.6 %shard_map.417 = (f32[1024,384]{1,0:T(8,128)S(1)}, bf16[3456,384]{1,0:T(8,128)(2,1)S(1)}, f32[8,384]{1,0:T(8,128)S(1)}) custom-call(s32[4]{0:T(128)S(1)} %pad_add_fusion.at, bf16[1088,1152]{1,0:T(8,128)(2,1)S(1)} %get-tuple-element.87.taps_ref.refs_8_, f32[1024,128]{1,0:T(8,128)S(1)} %broadcast_in_dim.12.mask_ref.refs_4_, ...), custom_call_target="tpu_custom_call" | custom-call | bytes 1024 | tf_op jit(solution)/shard_map/pallas_call | solution.py:56
  72.7 7.4 %collective-permute-done.13.refs_0_ = bf16[4,672,128]{2,1,0:T(8,128)(2,1)} collective-permute-done((bf16[4,672,128]{2,1,0:T(8,128)(2,1)}, bf16[4,672,128]{2,1,0:T(8,128)(2,1)}, u32[]{:S(2)}, u32[]{:S(2)}) %collective-permute-start.13) | collective-permute-done | bytes 688160 | tf_op jit(solution)/shard_map/ppermute | solution.py:1090
  80.9 2.3 %collective-permute-done.17.refs_7_ = bf16[4,672,128]{2,1,0:T(8,128)(2,1)S(1)} collective-permute-done((bf16[4,672,128]{2,1,0:T(8,128)(2,1)}, bf16[4,672,128]{2,1,0:T(8,128)(2,1)S(1)}, u32[]{:S(2)}, u32[]{:S(2)}) %collective-permute-start.17) | collective-permute-done | bytes 688160 | tf_op jit(solution)/shard_map/ppermute | solution.py:1096
  84.1 51.2 %shard_map.421 = (bf16[192,1024]{1,0:T(8,128)(2,1)}, f32[1024,384]{1,0:T(8,128)S(1)}, bf16[1088,1152]{1,0:T(8,128)(2,1)S(1)}, f32[16,384]{1,0:T(8,128)S(1)}, f32...) custom-call(s32[4]{0:T(128)S(1)} %copy-done.25, ...), custom_call_target="tpu_custom_call" | custom-call | flops 40000000000 | bytes 1024 | tf_op jit(solution)/shard_map/pallas_call | solution.py:56
  135.5 2.5 %collective-permute-done.18.back_ref = bf16[8,512,128]{2,1,0:T(8,128)(2,1)S(1)} collective-permute-done((bf16[8,512,128]{2,1,0:T(8,128)(2,1)S(1)}, bf16[8,512,128]{2,1,0:T(8,128)(2,1)S(1)}, u32[]{:S(2)}, u32[]{:S(2)}) %collective-permute-start.18) | collective-permute-done | bytes 1048608 | tf_op jit(solution)/shard_map/ppermute | solution.py:1113
  139.7 1.7 copy-done.1
  141.4 12.2 %shard_map.423 = (bf16[1088,1152]{1,0:T(8,128)(2,1)S(1)}, f32[16,384]{1,0:T(8,128)S(1)}, bf16[8,336,128]{2,1,0:T(8,128)(2,1)S(1)}, bf16[8,336,128]{2,1,0:T(8,128)(2,1)S(1)}) custom-call(s32[4]{0:T(128)S(1)} %copy-done.25, bf16[1088,1152]{1,0:T(8,128)(2,1)S(1)} %get-tuple-element.94.refs_0_, bf16[3456,384]{1,0:T(8,128)(2,1)S(1)} %copy-done.1, ...), custom_call_target="tpu_custom_call" | custom-call | bytes 1024 | tf_op jit(solution)/shard_map/pallas_call | solution.py:56
  160.2 8.6 %shard_map.425 = (bf16[192,1024]{1,0:T(8,128)(2,1)}, f32[16,256]{1,0:T(8,128)S(1)}) custom-call(s32[4]{0:T(128)S(1)} %copy-done.25, bf16[1088,1152]{1,0:T(8,128)(2,1)S(1)} %get-tuple-element.101.taps_ref, bf16[3456,384]{1,0:T(8,128)(2,1)S(1)} %copy-done.3, bf16[1024,384]{1,0:T(8,128)(2,1)S(1)} %copy-done.12, f32[8,384]{1,0:T(8,128)S(1)} %get-tuple-element.103.stat_ref, ...), custom_call_target="tpu_custom_call" | custom-call | bytes 1024 | tf_op jit(solution)/shard_map/pallas_call | solution.py:56
  172.4 1.7 collective-permute-start.27
  174.8 1.6 collective-permute-start.23
  176.9 3.4 %collective-permute-done.29.side_ref = f32[2,16,256]{2,1,0:T(8,128)S(1)} collective-permute-done((f32[2,16,256]{2,1,0:T(8,128)S(1)}, f32[2,16,256]{2,1,0:T(8,128)S(1)}, u32[]{:S(2)}, u32[]{:S(2)}) %collective-permute-start.29) | collective-permute-done | bytes 32800 | tf_op jit(solution)/shard_map/ppermute | solution.py:1144
  180.8 2.2 %collective-permute-start.32 = (f32[24,256]{1,0:T(8,128)S(1)}, f32[24,256]{1,0:T(8,128)S(1)}, u32[]{:S(2)}, u32[]{:S(2)}) collective-permute-start(f32[24,256]{1,0:T(8,128)S(1)} %shard_map.430.own_ref), channel_id=1, source_target_pairs={{0,24},{2,26},{4,28},{6,30},{8,16},{10,18},{12,20},{14,22},{16,8},... | collective-permute-start | bytes 73736 | tf_op jit(solution)/shard_map/ppermute | solution.py:1079
  185.4 1.8 shard_map.429
  188.3 2.0 %shard_map.431 = (f32[13,192]{1,0:T(8,128)}, f32[13,192]{1,0:T(8,128)}, f32[13,192]{1,0:T(8,128)}, f32[13,192]{1,0:T(8,128)}, f32[48,2,192]{2,1,0:T(2,128)}, /*i...) custom-call(s32[4]{0:T(128)S(1)} %copy-done.25, f32[24,256]{1,0:T(8,128)S(1)} %shard_map.430.own_ref, ...), custom_call_target="tpu_custom_call" | custom-call | bytes 1024 | tf_op jit(solution)/shard_map/pallas_call | solution.py:56
  190.4 1.6 shard_map.427
  (169 shorter events, 38.5 us)
Async XLA Ops:
  3.5 12.3 %collective-permute-start.3 = (bf16[1008,128]{1,0:T(8,128)(2,1)S(1)}, bf16[1008,128]{1,0:T(8,128)(2,1)S(1)}, u32[]{:S(2)}, u32[]{:S(2)}) collective-permute-start(bf16[1008,128]{1,0:T(8,128)(2,1)S(1)} %shard_map.414.refs_0_), channel_id=1, source_target_pairs={{0,24},{2,26},{4,28},{6,30},{8,16},{10,18},{12,20},{14,22},{16,8},... | collective-permute-start | bytes 774152 | tf_op jit(solution)/shard_map/ppermute | solution.py:1079
  8.6 22.0 %collective-permute-start.2 = (bf16[1008,128]{1,0:T(8,128)(2,1)S(1)}, bf16[1008,128]{1,0:T(8,128)(2,1)S(1)}, u32[]{:S(2)}, u32[]{:S(2)}) collective-permute-start(bf16[1008,128]{1,0:T(8,128)(2,1)S(1)} %shard_map.414.refs_0_), channel_id=1, source_target_pairs={{0,16},{2,18},{4,20},{6,22},{8,24},{10,26},{12,28},{14,30},{16,0},... | collective-permute-start | bytes 774152 | tf_op jit(solution)/shard_map/ppermute | solution.py:1079
  8.6 22.0 %collective-permute-start.1 = (bf16[1008,128]{1,0:T(8,128)(2,1)S(1)}, bf16[1008,128]{1,0:T(8,128)(2,1)S(1)}, u32[]{:S(2)}, u32[]{:S(2)}) collective-permute-start(bf16[1008,128]{1,0:T(8,128)(2,1)S(1)} %shard_map.414.refs_0_), channel_id=1, source_target_pairs={{0,8},{2,10},{4,12},{6,14},{8,0},{10,2},{12,4},{14,6},{16,24},{18,... | collective-permute-start | bytes 774152 | tf_op jit(solution)/shard_map/ppermute | solution.py:1079
  12.6 39.4 %collective-permute-start = (bf16[400,1024]{1,0:T(8,128)(2,1)S(1)}, bf16[400,1024]{1,0:T(8,128)(2,1)S(1)}, u32[]{:S(2)}, u32[]{:S(2)}) collective-permute-start(bf16[400,1024]{1,0:T(8,128)(2,1)S(1)} %shard_map.413), channel_id=1, source_target_pairs={{0,1},{1,0},{2,3},{3,2},{4,5},{5,4},{6,7},{7,6},{8,9},{9,8},{10,11... | collective-permute-start | bytes 2457608 | tf_op jit(solution)/shard_map/ppermute | solution.py:1198
  32.0 11.9 %collective-permute-start.6 = (bf16[4,336,128]{2,1,0:T(8,128)(2,1)S(1)}, bf16[4,336,128]{2,1,0:T(8,128)(2,1)S(1)}, u32[]{:S(2)}, u32[]{:S(2)}) collective-permute-start(bf16[4,336,128]{2,1,0:T(8,128)(2,1)S(1)} %get-tuple-element.86.refs_0_), channel_id=1, source_target_pairs={{0,5},{1,4},{2,7},{3,6},{4,1},{5,0},{6,3},{7,2},{8,13},{9,12},{10,... | collective-permute-start | bytes 1032200 | tf_op jit(solution)/shard_map/ppermute | solution.py:1090
  34.5 9.5 %collective-permute-start.7 = (bf16[4,336,128]{2,1,0:T(8,128)(2,1)S(1)}, bf16[4,336,128]{2,1,0:T(8,128)(2,1)S(1)}, u32[]{:S(2)}, u32[]{:S(2)}) collective-permute-start(bf16[4,336,128]{2,1,0:T(8,128)(2,1)S(1)} %get-tuple-element.86.refs_0_), channel_id=1, source_target_pairs={{0,2},{2,0},{4,6},{6,4},{8,10},{10,8},{12,14},{14,12},{16,18},{18,... | collective-permute-start | bytes 1032200 | tf_op jit(solution)/shard_map/ppermute | solution.py:1096
  34.5 15.0 %collective-permute-start.5 = (bf16[4,336,128]{2,1,0:T(8,128)(2,1)S(1)}, bf16[4,336,128]{2,1,0:T(8,128)(2,1)S(1)}, u32[]{:S(2)}, u32[]{:S(2)}) collective-permute-start(bf16[4,336,128]{2,1,0:T(8,128)(2,1)S(1)} %get-tuple-element.86.refs_0_), channel_id=1, source_target_pairs={{0,1},{1,0},{2,3},{3,2},{4,5},{5,4},{6,7},{7,6},{8,9},{9,8},{10,11... | collective-permute-start | bytes 1032200 | tf_op jit(solution)/shard_map/ppermute | solution.py:1089
  35.0 16.0 %collective-permute-start.4 = (bf16[4,336,128]{2,1,0:T(8,128)(2,1)S(1)}, bf16[4,336,128]{2,1,0:T(8,128)(2,1)S(1)}, u32[]{:S(2)}, u32[]{:S(2)}) collective-permute-start(bf16[4,336,128]{2,1,0:T(8,128)(2,1)S(1)} %get-tuple-element.86.refs_0_), channel_id=1, source_target_pairs={{0,4},{2,6},{4,0},{6,2},{8,12},{10,14},{12,8},{14,10},{16,20},{18,... | collective-permute-start | bytes 1032200 | tf_op jit(solution)/shard_map/ppermute | solution.py:1088
  44.0 8.0 %collective-permute-start.10 = (bf16[4,336,128]{2,1,0:T(8,128)(2,1)S(1)}, bf16[4,336,128]{2,1,0:T(8,128)(2,1)S(1)}, u32[]{:S(2)}, u32[]{:S(2)}) collective-permute-start(bf16[4,336,128]{2,1,0:T(8,128)(2,1)S(1)} %collective-permute-done.6.refs_3_), channel_id=1, source_target_pairs={{0,2},{2,0},{4,6},{6,4},{8,10},{10,8},{12,14},{14,12},{16,18},{18,... | collective-permute-start | bytes 1032200 | tf_op jit(solution)/shard_map/ppermute | solution.py:1096
  44.0 25.6 %collective-permute-start.11 = (bf16[4,672,128]{2,1,0:T(8,128)(2,1)}, bf16[4,672,128]{2,1,0:T(8,128)(2,1)S(1)}, u32[]{:S(2)}, u32[]{:S(2)}) collective-permute-start(bf16[4,672,128]{2,1,0:T(8,128)(2,1)} %get-tuple-element.89.refs_8_.refs_0_), channel_id=1, source_target_pairs={{0,4},{2,6},{4,0},{6,2},{8,12},{10,14},{12,8},{14,10},{16,20},{18,... | collective-permute-start | bytes 2064392 | tf_op jit(solution)/shard_map/ppermute | solution.py:1088
  49.5 22.4 %collective-permute-start.12 = (bf16[4,672,128]{2,1,0:T(8,128)(2,1)}, bf16[4,672,128]{2,1,0:T(8,128)(2,1)}, u32[]{:S(2)}, u32[]{:S(2)}) collective-permute-start(bf16[4,672,128]{2,1,0:T(8,128)(2,1)} %get-tuple-element.89.refs_8_.refs_0_), channel_id=1, source_target_pairs={{0,1},{1,0},{2,3},{3,2},{4,5},{5,4},{6,7},{7,6},{8,9},{9,8},{10,11... | collective-permute-start | bytes 2064392 | tf_op jit(solution)/shard_map/ppermute | solution.py:1089
  51.0 29.1 %collective-permute-start.13 = (bf16[4,672,128]{2,1,0:T(8,128)(2,1)}, bf16[4,672,128]{2,1,0:T(8,128)(2,1)}, u32[]{:S(2)}, u32[]{:S(2)}) collective-permute-start(bf16[4,672,128]{2,1,0:T(8,128)(2,1)} %get-tuple-element.89.refs_8_.refs_0_), channel_id=1, source_target_pairs={{0,5},{1,4},{2,7},{3,6},{4,1},{5,0},{6,3},{7,2},{8,13},{9,12},{10,... | collective-permute-start | bytes 2064392 | tf_op jit(solution)/shard_map/ppermute | solution.py:1090
  56.7 24.1 %collective-permute-start.14 = (bf16[4,672,128]{2,1,0:T(8,128)(2,1)}, bf16[4,672,128]{2,1,0:T(8,128)(2,1)S(1)}, u32[]{:S(2)}, u32[]{:S(2)}) collective-permute-start(bf16[4,672,128]{2,1,0:T(8,128)(2,1)} %get-tuple-element.89.refs_8_.refs_0_), channel_id=1, source_target_pairs={{0,2},{2,0},{4,6},{6,4},{8,10},{10,8},{12,14},{14,12},{16,18},{18,... | collective-permute-start | bytes 2064392 | tf_op jit(solution)/shard_map/ppermute | solution.py:1096
  71.1 9.7 %collective-permute-start.15 = (bf16[4,672,128]{2,1,0:T(8,128)(2,1)}, bf16[4,672,128]{2,1,0:T(8,128)(2,1)S(1)}, u32[]{:S(2)}, u32[]{:S(2)}) collective-permute-start(bf16[4,672,128]{2,1,0:T(8,128)(2,1)} %shard_map.418.refs_1_), channel_id=1, source_target_pairs={{0,2},{2,0},{4,6},{6,4},{8,10},{10,8},{12,14},{14,12},{16,18},{18,... | collective-permute-start | bytes 2064392 | tf_op jit(solution)/shard_map/ppermute | solution.py:1096
  72.6 8.3 %collective-permute-start.16 = (bf16[4,672,128]{2,1,0:T(8,128)(2,1)}, bf16[4,672,128]{2,1,0:T(8,128)(2,1)}, u32[]{:S(2)}, u32[]{:S(2)}) collective-permute-start(bf16[4,672,128]{2,1,0:T(8,128)(2,1)} %shard_map.419.refs_2_), channel_id=1, source_target_pairs={{0,2},{2,0},{4,6},{6,4},{8,10},{10,8},{12,14},{14,12},{16,18},{18,... | collective-permute-start | bytes 2064392 | tf_op jit(solution)/shard_map/ppermute | solution.py:1096
  153.9 15.1 %collective-permute-start.24 = (bf16[4,512,128]{2,1,0:T(8,128)(2,1)S(1)}, bf16[4,512,128]{2,1,0:T(8,128)(2,1)S(1)}, u32[]{:S(2)}, u32[]{:S(2)}) collective-permute-start(bf16[4,512,128]{2,1,0:T(8,128)(2,1)S(1)} %copy-done.14), channel_id=1, source_target_pairs={{0,4},{2,6},{4,0},{6,2},{8,12},{10,14},{12,8},{14,10},{16,20},{18,... | collective-permute-start | bytes 1572872 | tf_op jit(solution)/shard_map/ppermute | solution.py:1119
  156.6 14.3 %collective-permute-start.21 = (bf16[2,336,128]{2,1,0:T(8,128)(2,1)S(1)}, bf16[2,336,128]{2,1,0:T(8,128)(2,1)S(1)}, u32[]{:S(2)}, u32[]{:S(2)}) collective-permute-start(bf16[2,336,128]{2,1,0:T(8,128)(2,1)S(1)} %get-tuple-element.111), channel_id=1, source_target_pairs={{0,16},{2,18},{4,20},{6,22},{8,24},{10,26},{12,28},{14,30},{16,0},... | collective-permute-start | bytes 516104 | tf_op jit(solution)/shard_map/ppermute | solution.py:1130
  158.1 14.3 %collective-permute-start.22 = (bf16[2,336,128]{2,1,0:T(8,128)(2,1)S(1)}, bf16[2,336,128]{2,1,0:T(8,128)(2,1)S(1)}, u32[]{:S(2)}, u32[]{:S(2)}) collective-permute-start(bf16[2,336,128]{2,1,0:T(8,128)(2,1)S(1)} %get-tuple-element.112), channel_id=1, source_target_pairs={{0,24},{2,26},{4,28},{6,30},{8,16},{10,18},{12,20},{14,22},{16,8},... | collective-permute-start | bytes 516104 | tf_op jit(solution)/shard_map/ppermute | solution.py:1130
  158.8 15.3 %collective-permute-start.20 = (bf16[2,336,128]{2,1,0:T(8,128)(2,1)S(1)}, bf16[2,336,128]{2,1,0:T(8,128)(2,1)S(1)}, u32[]{:S(2)}, u32[]{:S(2)}) collective-permute-start(bf16[2,336,128]{2,1,0:T(8,128)(2,1)S(1)} %get-tuple-element.108.refs_0_), channel_id=1, source_target_pairs={{0,8},{2,10},{4,12},{6,14},{8,0},{10,2},{12,4},{14,6},{16,24},{18,... | collective-permute-start | bytes 516104 | tf_op jit(solution)/shard_map/ppermute | solution.py:1130
  168.9 7.5 %collective-permute-start.28 = (f32[16,256]{1,0:T(8,128)S(1)}, f32[16,256]{1,0:T(8,128)S(1)}, u32[]{:S(2)}, u32[]{:S(2)}) collective-permute-start(f32[16,256]{1,0:T(8,128)S(1)} %get-tuple-element.128.here_ref), channel_id=1, source_target_pairs={{0,2},{2,0},{4,6},{6,4},{8,10},{10,8},{12,14},{14,12},{16,18},{18,... | collective-permute-start | bytes 49160 | tf_op jit(solution)/shard_map/ppermute | solution.py:1143
  169.7 13.3 %collective-permute-start.25 = (bf16[512,128]{1,0:T(8,128)(2,1)S(1)}, bf16[512,128]{1,0:T(8,128)(2,1)S(1)}, u32[]{:S(2)}, u32[]{:S(2)}) collective-permute-start(bf16[512,128]{1,0:T(8,128)(2,1)S(1)} %get-tuple-element.121), channel_id=1, source_target_pairs={{0,8},{2,10},{4,12},{6,14},{8,0},{10,2},{12,4},{14,6},{16,24},{18,... | collective-permute-start | bytes 393224 | tf_op jit(solution)/shard_map/ppermute | solution.py:1123
  170.9 13.5 %collective-permute-start.26 = (bf16[512,128]{1,0:T(8,128)(2,1)S(1)}, bf16[512,128]{1,0:T(8,128)(2,1)S(1)}, u32[]{:S(2)}, u32[]{:S(2)}) collective-permute-start(bf16[512,128]{1,0:T(8,128)(2,1)S(1)} %get-tuple-element.122), channel_id=1, source_target_pairs={{0,16},{2,18},{4,20},{6,22},{8,24},{10,26},{12,28},{14,30},{16,0},... | collective-permute-start | bytes 393224 | tf_op jit(solution)/shard_map/ppermute | solution.py:1123
  172.4 12.9 %collective-permute-start.27 = (bf16[512,128]{1,0:T(8,128)(2,1)S(1)}, bf16[512,128]{1,0:T(8,128)(2,1)S(1)}, u32[]{:S(2)}, u32[]{:S(2)}) collective-permute-start(bf16[512,128]{1,0:T(8,128)(2,1)S(1)} %get-tuple-element.123), channel_id=1, source_target_pairs={{0,24},{2,26},{4,28},{6,30},{8,16},{10,18},{12,20},{14,22},{16,8},... | collective-permute-start | bytes 393224 | tf_op jit(solution)/shard_map/ppermute | solution.py:1123
  174.8 15.6 %collective-permute-start.23 = (bf16[336,128]{1,0:T(8,128)(2,1)S(1)}, bf16[336,128]{1,0:T(8,128)(2,1)S(1)}, u32[]{:S(2)}, u32[]{:S(2)}) collective-permute-start(bf16[336,128]{1,0:T(8,128)(2,1)S(1)} %get-tuple-element.114), channel_id=1, source_target_pairs={{0,4},{2,6},{4,0},{6,2},{8,12},{10,14},{12,8},{14,10},{16,20},{18,... | collective-permute-start | bytes 258056 | tf_op jit(solution)/shard_map/ppermute | solution.py:1337
  (61 other events, 824.8 us)
